TPU v7x, 32 devices: a whole 2x2x4 slice. The times are simulated.
32 devices in a mesh: dp: 8 (over z, y), tensor: 4 (over x, core).
Axes of the slice: x: 2, y: 2, z: 4, core: 2. Of those that a mesh axis runs over, the one named last changes fastest.
Arguments:
- frames: bfloat16 [31744, 324], P(('dp', 'tensor')), may hold values from -6 to 6
- cotangent: bfloat16 [31744, 324], P(('dp', 'tensor')), may hold values from -6 to 6
- lengths: int32 [64], P('dp'), may hold values from 62 to 496, as said below
- rate_kind: int32 [64], P('dp'), may hold values from 0 to 2
- attn_w: float32 [4, 324, 324], P(None, None, 'tensor')
- attn_m: float32 [4, 324, 324], P(None, None, 'tensor')
- attn_v: float32 [4, 324, 324], P(None, None, 'tensor'), as said below
- ffin_w: float32 [2, 324, 1296], P(None, None, 'tensor')
- ffin_m: float32 [2, 324, 1296], P(None, None, 'tensor')
- ffin_v: float32 [2, 324, 1296], P(None, None, 'tensor'), as said below
- ffout_w: float32 [2, 1296, 324], P(None, 'tensor')
- ffout_m: float32 [2, 1296, 324], P(None, 'tensor')
- ffout_v: float32 [2, 1296, 324], P(None, 'tensor'), as said below
- convin_w: float32 [2, 324, 324], P(None, None, 'tensor')
- convin_m: float32 [2, 324, 324], P(None, None, 'tensor')
- convin_v: float32 [2, 324, 324], P(None, None, 'tensor'), as said below
- convout_w: float32 [324, 324], P('tensor')
- convout_m: float32 [324, 324], P('tensor')
- convout_v: float32 [324, 324], P('tensor'), as said below
- depth_w: float32 [31, 324], replicated
- depth_m: float32 [31, 324], replicated
- depth_v: float32 [31, 324], replicated, as said below
- norm_w: float32 [8, 324], replicated, as said below
- norm_m: float32 [8, 324], replicated
- norm_v: float32 [8, 324], replicated, as said below
- bn_w: float32 [2, 324], replicated, as said below
- bn_m: float32 [2, 324], replicated
- bn_v: float32 [2, 324], replicated, as said below
- table_w: float32 [3, 324], replicated, may hold values from -3 to 3
- table_m: float32 [3, 324], replicated
- table_v: float32 [3, 324], replicated, as said below
Outputs:
- out: bfloat16 [31744, 324], P(('dp', 'tensor'))
- in_grad: float32 [31744, 324], P(('dp', 'tensor'))
- attn_w_new: float32 [4, 324, 324], P(None, None, 'tensor')
- attn_m_new: float32 [4, 324, 324], P(None, None, 'tensor')
- attn_v_new: float32 [3, 324, 324], P(None, None, 'tensor')
- attn_out_v_new: float32 [324, 324], P(None, 'tensor')
- ffin_w_new: float32 [2, 324, 1296], P(None, None, 'tensor')
- ffin_m_new: float32 [2, 324, 1296], P(None, None, 'tensor')
- ffin_v_new: float32 [2, 324, 1296], P(None, None, 'tensor')
- ffout_w_new: float32 [2, 1296, 324], P(None, 'tensor')
- ffout_m_new: float32 [2, 1296, 324], P(None, 'tensor')
- ffout_v_new: float32 [2, 1296, 324], P(None, 'tensor')
- convin_w_new: float32 [2, 324, 324], P(None, None, 'tensor')
- convin_m_new: float32 [2, 324, 324], P(None, None, 'tensor')
- convin_v_new: float32 [2, 324, 324], P(None, None, 'tensor')
- convout_w_new: float32 [324, 324], P('tensor')
- convout_m_new: float32 [324, 324], P('tensor')
- convout_v_new: float32 [324, 324], P('tensor')
- depth_w_new: float32 [31, 324], replicated
- depth_m_new: float32 [31, 324], replicated
- depth_v_new: float32 [31, 324], replicated
- norm_w_new: float32 [8, 324], replicated
- norm_m_new: float32 [8, 324], replicated
- norm_v_new: float32 [8, 324], replicated
- bn_w_new: float32 [2, 324], replicated
- bn_m_new: float32 [2, 324], replicated
- bn_v_new: float32 [2, 324], replicated
- table_w_new: float32 [3, 324], replicated
- table_m_new: float32 [3, 324], replicated
- table_v_new: float32 [3, 324], replicated
- weight_norms: float32 [12], replicated
- update_norms: float32 [12], replicated
Inputs may be any that keep to these rules, and one draw needn't show every extreme that they name: `lengths`: valid frames of each utterance, counted from its start. `attn_v`: positive entries. `ffin_v`: positive entries. `ffout_v`: positive entries. `convin_v`: positive entries. `convout_v`: positive entries. `depth_v`: positive entries. `norm_v`: positive entries. `bn_v`: positive entries. `table_v`: positive entries. `norm_w`: gains (rows 0 to 3) are positive. `bn_w`: the gain (row 0) is positive.
All inputs are finite; a program needn't handle non-finite values.
Results may differ from a plain program's by a relative error of at most 0.03.
The roundings to bfloat16 on the way count: a program that leaves them out, or rounds other values in their place, can miss the bound.
Values may be sent and summed in bfloat16 or wider, within the bound.
No kernel may reach another device: no remote copies, remote signals or barrier semaphores. Data moves between devices by JAX's collectives and lax.ppermute only.
A program may use at most 192 MiB of HBM per device.

v0:
```python
import math

import jax
import jax.numpy as jnp
from jax import lax
from jax.sharding import PartitionSpec as P

D = 324
HEADS = 4
KERNEL = 31
RATES = 3
STEP = 10
SLOT = 496
HD = 81


PRECISE = lax.Precision.HIGHEST
EPS_NORM = 1e-05
BETA_ONE = 0.9
BETA_TWO = 0.999
ADAM_EPS = 1e-06
WEIGHT_DECAY = 0.01
RATE_MATRIX = 0.3
RATE_VECTOR = 0.5
MASK_FILL = -1e30


def product(left_side, right_side):
    return jnp.dot(left_side, right_side, preferred_element_type=jnp.float32)


def product_tn(left_side, right_side):
    return lax.dot_general(
        left_side, right_side, (((0,), (0,)), ((), ())), preferred_element_type=jnp.float32
    )


def product_nt(left_side, right_side):
    return lax.dot_general(
        left_side, right_side, (((1,), (1,)), ((), ())), preferred_element_type=jnp.float32
    )


def norm_forward(resid, gain_row, shift_row):
    center = resid - jnp.mean(resid, axis=-1, keepdims=True)
    spread = jnp.mean(center * center, axis=-1, keepdims=True)
    inv_scale = lax.rsqrt(spread + EPS_NORM)
    normal = center * inv_scale
    return (normal * gain_row + shift_row, normal, inv_scale)


def norm_backward(upstream, normal, inv_scale, gain_row):
    scaled = upstream * gain_row
    resid_grad = inv_scale * (
        scaled
        - jnp.mean(scaled, axis=-1, keepdims=True)
        - normal * jnp.mean(scaled * normal, axis=-1, keepdims=True)
    )
    return (resid_grad, jnp.sum(upstream * normal, axis=0), jnp.sum(upstream, axis=0))


def silu_slope(pre_act):
    sigmoid_of = jax.nn.sigmoid(pre_act)
    return sigmoid_of * (1.0 + pre_act * (1.0 - sigmoid_of))


def spread_rows(rows_low):
    return lax.all_gather(rows_low, "tensor", axis=0, tiled=True)


def spread_grads(grads_low):
    return lax.all_gather(grads_low, "tensor", axis=0, tiled=True)


def collect_rows(term_fn, row_total):
    return lax.psum_scatter(
        term_fn(jnp.int32(0), lax.axis_size("tensor") * row_total).astype(jnp.bfloat16),
        "tensor",
        scatter_dimension=0,
        tiled=True,
    ).astype(jnp.float32)


def collect_grads(term_fn, row_total):
    return lax.psum_scatter(
        term_fn(jnp.int32(0), lax.axis_size("tensor") * row_total).astype(jnp.bfloat16),
        "tensor",
        scatter_dimension=0,
        tiled=True,
    ).astype(jnp.float32)


def split_forward(inputs, weight_in, weight_out):
    gathered = spread_rows(inputs.astype(jnp.bfloat16))
    hidden_pre = product(gathered, weight_in)
    hidden_low = jax.nn.silu(hidden_pre).astype(jnp.bfloat16)

    def out_term(first_row, row_count):
        return product(hidden_low, weight_out)

    return (collect_rows(out_term, inputs.shape[0]), (gathered, hidden_pre, hidden_low))


def split_backward(upstream, saved, weight_in, weight_out):
    gathered, hidden_pre, hidden_low = saved
    grads_all = spread_grads(upstream.astype(jnp.bfloat16))
    pre_grad = (product_nt(grads_all, weight_out) * silu_slope(hidden_pre)).astype(jnp.bfloat16)
    out_weight_grad = product_tn(hidden_low, grads_all)
    in_weight_grad = product_tn(gathered, pre_grad)

    def back_term(first_row, row_count):
        return product_nt(pre_grad, weight_in)

    return (collect_grads(back_term, upstream.shape[0]), in_weight_grad, out_weight_grad)


def depth_forward(signal, kernel):
    half_width = KERNEL // 2
    padded = jnp.pad(signal, ((0, 0), (half_width, half_width), (0, 0)))
    total = jnp.zeros(signal.shape, jnp.float32)
    for offset in range(KERNEL):
        total = total + padded[:, offset : offset + SLOT, :] * kernel[offset]
    return total


def depth_backward(upstream, signal, kernel):
    half_width = KERNEL // 2
    grad_pad = jnp.pad(upstream, ((0, 0), (half_width, half_width), (0, 0)))
    signal_pad = jnp.pad(signal, ((0, 0), (half_width, half_width), (0, 0)))
    signal_grad = jnp.zeros(signal.shape, jnp.float32)
    tap_grads = []
    for offset in range(KERNEL):
        begin = 2 * half_width - offset
        signal_grad = signal_grad + grad_pad[:, begin : begin + SLOT, :] * kernel[offset]
        tap_grads.append(jnp.sum(signal_pad[:, offset : offset + SLOT, :] * upstream, axis=(0, 1)))
    return (signal_grad, jnp.stack(tap_grads))


def adam_step(first, second, grad_full):
    first_new = BETA_ONE * first + (1.0 - BETA_ONE) * grad_full
    second_new = BETA_TWO * second + (1.0 - BETA_TWO) * grad_full * grad_full
    direction = (
        first_new
        / (1.0 - BETA_ONE**STEP)
        / (jnp.sqrt(second_new / (1.0 - BETA_TWO**STEP)) + ADAM_EPS)
    )
    return (first_new, second_new, direction)


def lamb_parts(weight, first, second, grad_full):
    first_new, second_new, direction = adam_step(first, second, grad_full)
    direction = direction + WEIGHT_DECAY * weight
    axes_all = tuple(range(1, weight.ndim))
    return (
        first_new,
        second_new,
        direction,
        jnp.sum(weight * weight, axis=axes_all),
        jnp.sum(direction * direction, axis=axes_all),
    )


def body(
    frames,
    cotangent,
    lengths,
    rate_kind,
    attn_w,
    attn_m,
    attn_v,
    ffin_w,
    ffin_m,
    ffin_v,
    ffout_w,
    ffout_m,
    ffout_v,
    convin_w,
    convin_m,
    convin_v,
    convout_w,
    convout_m,
    convout_v,
    depth_w,
    depth_m,
    depth_v,
    norm_w,
    norm_m,
    norm_v,
    bn_w,
    bn_m,
    bn_v,
    table_w,
    table_m,
    table_v,
):
    tensor_rank = lax.axis_index("tensor")
    own_rows = frames.shape[0]
    own_utts = own_rows // SLOT
    group_utts = lengths.shape[0]
    slot_index = jnp.arange(SLOT, dtype=jnp.int32)
    group_mask = (slot_index[None, :] < lengths[:, None]).astype(jnp.float32)
    group_weight = group_mask.reshape(group_utts * SLOT, 1)
    own_lengths = lax.dynamic_slice_in_dim(lengths, tensor_rank * own_utts, own_utts, 0)
    own_kinds = lax.dynamic_slice_in_dim(rate_kind, tensor_rank * own_utts, own_utts, 0)
    own_valid = slot_index[None, :] < own_lengths[:, None]
    own_weight = own_valid.astype(jnp.float32).reshape(own_rows, 1)
    onehot = (own_kinds[:, None] == jnp.arange(RATES, dtype=jnp.int32)[None, :]).astype(jnp.float32)
    attn_low = attn_w.astype(jnp.bfloat16)
    convin_low = convin_w.astype(jnp.bfloat16)
    convout_low = convout_w.astype(jnp.bfloat16)
    attn_full = lax.all_gather(attn_low, "tensor", axis=2, tiled=True)
    ffin_use = ffin_w.astype(jnp.bfloat16)
    ffout_use = ffout_w.astype(jnp.bfloat16)
    ffn_forward, ffn_backward = (split_forward, split_backward)
    channels = convin_low.shape[2]
    chan_lo = tensor_rank * channels

    def widen(vector_in):
        blank = jnp.zeros(vector_in.shape[:-1] + (D,), jnp.float32)
        return lax.dynamic_update_slice_in_dim(blank, vector_in, chan_lo, vector_in.ndim - 1)

    def narrow(vector_in):
        return lax.dynamic_slice_in_dim(vector_in, chan_lo, channels, vector_in.ndim - 1)

    table_rows = jnp.dot(onehot, table_w, precision=PRECISE)
    base_rows = (
        frames.astype(jnp.float32).reshape(own_utts, SLOT, D) + table_rows[:, None, :]
    ).reshape(own_rows, D)
    base_low = base_rows.astype(jnp.bfloat16)
    projected = jnp.einsum(
        "rd,jde->jre", base_low, attn_full[:3], preferred_element_type=jnp.float32
    )
    head_split = projected.astype(jnp.bfloat16).reshape(3, own_utts, SLOT, HEADS, HD)
    queries, key_heads, value_heads = (head_split[0], head_split[1], head_split[2])
    score_scale = 1.0 / math.sqrt(HD)
    key_valid = own_valid[:, None, None, :]

    def masked_scores():
        raw_scores = (
            jnp.einsum("bqhe,bkhe->bhqk", queries, key_heads, preferred_element_type=jnp.float32)
            * score_scale
        )
        return jnp.where(key_valid, raw_scores, MASK_FILL)

    scores = masked_scores()
    score_top = jnp.max(scores, axis=-1, keepdims=True)
    exponent = jnp.exp(scores - score_top)
    exp_total = jnp.sum(exponent, axis=-1, keepdims=True)
    log_total = score_top + jnp.log(exp_total)
    prob_low = (exponent / exp_total).astype(jnp.bfloat16)
    mixed_low = (
        jnp.einsum("bhqk,bkhe->bqhe", prob_low, value_heads, preferred_element_type=jnp.float32)
        .reshape(own_rows, D)
        .astype(jnp.bfloat16)
    )
    attn_out = product(mixed_low, attn_full[3])
    first_out, first_normal, first_scale = norm_forward(base_rows + attn_out, norm_w[0], norm_w[4])
    update_one, saved_one = ffn_forward(first_out, ffin_use[0], ffout_use[0])
    second, second_normal, second_scale = norm_forward(first_out + update_one, norm_w[1], norm_w[5])
    second_low = second.astype(jnp.bfloat16)
    second_rows = spread_rows(second_low)
    depth_use = narrow(depth_w)
    bn_use = narrow(bn_w)
    value_pre = product(second_rows, convin_low[0])
    gate_pre = product(second_rows, convin_low[1])
    gate_sig = jax.nn.sigmoid(gate_pre)
    glu_out = value_pre * gate_sig * group_weight
    glu_cube = glu_out.reshape(group_utts, SLOT, channels)
    conv_out = depth_forward(glu_cube, depth_use).reshape(group_utts * SLOT, channels)
    count_local = jnp.sum(own_weight)
    sum_local = widen(jnp.sum(conv_out * group_weight, axis=0))
    total_sum, valid_count = lax.psum((sum_local, count_local), ("dp", "tensor"))
    bn_mean = narrow(total_sum) / valid_count
    center = conv_out - bn_mean
    bn_var = (
        narrow(lax.psum(widen(jnp.sum(center * center * group_weight, axis=0)), ("dp", "tensor")))
        / valid_count
    )
    bn_scale = lax.rsqrt(bn_var + EPS_NORM)
    bn_normal = center * bn_scale
    bn_out = bn_normal * bn_use[0] + bn_use[1]
    act_low = jax.nn.silu(bn_out).astype(jnp.bfloat16)

    def conv_term(first_row, row_count):
        return product(act_low, convout_low)

    conv_update = collect_rows(conv_term, own_rows)
    third_out, third_normal, third_scale = norm_forward(second + conv_update, norm_w[2], norm_w[6])
    update_two, saved_two = ffn_forward(third_out, ffin_use[1], ffout_use[1])
    fourth, fourth_normal, fourth_scale = norm_forward(third_out + update_two, norm_w[3], norm_w[7])
    grad_out = cotangent.astype(jnp.float32) * own_weight
    grad_four, gain_four, shift_four = norm_backward(
        grad_out, fourth_normal, fourth_scale, norm_w[3]
    )
    back_two, fin_two, fout_two = ffn_backward(grad_four, saved_two, ffin_use[1], ffout_use[1])
    grad_three, gain_three, shift_three = norm_backward(
        grad_four + back_two, third_normal, third_scale, norm_w[2]
    )
    grad_three_low = grad_three.astype(jnp.bfloat16)
    conv_grads = spread_grads(grad_three_low)
    act_grad = product_nt(conv_grads, convout_low)
    convout_grad = product_tn(act_low, conv_grads)
    bn_grad = act_grad * silu_slope(bn_out)
    sum_grad_all, sum_normal_all = lax.psum(
        (widen(jnp.sum(bn_grad, axis=0)), widen(jnp.sum(bn_grad * bn_normal, axis=0))),
        ("dp", "tensor"),
    )
    sum_grad = narrow(sum_grad_all)
    sum_normal = narrow(sum_normal_all)
    conv_grad = (
        group_weight
        * bn_scale
        * (
            bn_grad * bn_use[0]
            - bn_use[0] * sum_grad / valid_count
            - bn_normal * bn_use[0] * sum_normal / valid_count
        )
    )
    glu_grad, depth_grad = depth_backward(
        conv_grad.reshape(group_utts, SLOT, channels), glu_cube, depth_use
    )
    glu_grad = glu_grad.reshape(group_utts * SLOT, channels) * group_weight
    value_grad = (glu_grad * gate_sig).astype(jnp.bfloat16)
    gate_grad = (glu_grad * value_pre * gate_sig * (1.0 - gate_sig)).astype(jnp.bfloat16)
    convin_grad = jnp.stack(
        [product_tn(second_rows, value_grad), product_tn(second_rows, gate_grad)]
    )

    def glu_back_term(first_row, row_count):
        return product_nt(value_grad, convin_low[0]) + product_nt(gate_grad, convin_low[1])

    conv_back = collect_grads(glu_back_term, own_rows)
    grad_two, gain_two, shift_two = norm_backward(
        grad_three + conv_back, second_normal, second_scale, norm_w[1]
    )
    back_one, fin_one, fout_one = ffn_backward(grad_two, saved_one, ffin_use[0], ffout_use[0])
    grad_one, gain_one, shift_one = norm_backward(
        grad_two + back_one, first_normal, first_scale, norm_w[0]
    )
    attn_grad_low = grad_one.astype(jnp.bfloat16)
    out_proj_grad = product_tn(mixed_low, attn_grad_low)
    mixed_grad = (
        product_nt(attn_grad_low, attn_full[3])
        .astype(jnp.bfloat16)
        .reshape(own_utts, SLOT, HEADS, HD)
    )
    probs_again = jnp.exp(masked_scores() - log_total)
    probs_low = probs_again.astype(jnp.bfloat16)
    prob_grad = jnp.einsum(
        "bqhe,bkhe->bhqk", mixed_grad, value_heads, preferred_element_type=jnp.float32
    )
    score_grad = (
        probs_again * (prob_grad - jnp.sum(prob_grad * probs_again, axis=-1, keepdims=True))
    ).astype(jnp.bfloat16)
    query_grad = (
        jnp.einsum("bhqk,bkhe->bqhe", score_grad, key_heads, preferred_element_type=jnp.float32)
        * score_scale
    ).astype(jnp.bfloat16)
    key_grad = (
        jnp.einsum("bhqk,bqhe->bkhe", score_grad, queries, preferred_element_type=jnp.float32)
        * score_scale
    ).astype(jnp.bfloat16)
    value_grad_rows = jnp.einsum(
        "bhqk,bqhe->bkhe", probs_low, mixed_grad, preferred_element_type=jnp.float32
    ).astype(jnp.bfloat16)
    proj_grads = jnp.stack([query_grad, key_grad, value_grad_rows]).reshape(3, own_rows, D)
    qkv_weight_grad = jnp.einsum(
        "rd,jre->jde", base_low, proj_grads, preferred_element_type=jnp.float32
    )
    base_grad = grad_one + jnp.einsum(
        "jre,jde->rd", proj_grads, attn_full[:3], preferred_element_type=jnp.float32
    )
    attn_grad = jnp.concatenate([qkv_weight_grad, out_proj_grad[None]], axis=0)
    table_grad = jnp.dot(
        onehot.T, jnp.sum(base_grad.reshape(own_utts, SLOT, D), axis=1), precision=PRECISE
    )
    vector_part = jnp.concatenate(
        [
            jnp.stack(
                [
                    gain_one,
                    gain_two,
                    gain_three,
                    gain_four,
                    shift_one,
                    shift_two,
                    shift_three,
                    shift_four,
                ]
            ),
            table_grad,
            widen(depth_grad),
        ],
        axis=0,
    )
    attn_part = lax.psum_scatter(
        attn_grad.astype(jnp.bfloat16), "tensor", scatter_dimension=2, tiled=True
    ).astype(jnp.float32)
    fin_part = jnp.stack([fin_one, fin_two])
    fout_part = jnp.stack([fout_one, fout_two])
    attn_g, fin_g, fout_g, cin_g, cout_g, vector_dp = lax.psum(
        (attn_part, fin_part, fout_part, convin_grad, convout_grad, vector_part), "dp"
    )
    matrix_sets = [
        (attn_w, attn_m, attn_v, attn_g),
        (ffin_w, ffin_m, ffin_v, fin_g),
        (ffout_w, ffout_m, ffout_v, fout_g),
        (convin_w, convin_m, convin_v, cin_g),
        (convout_w[None], convout_m[None], convout_v[None], cout_g[None]),
    ]
    lamb_sets = [lamb_parts(*entry) for entry in matrix_sets]
    weight_sq = jnp.concatenate([entry[3] for entry in lamb_sets])
    update_sq = jnp.concatenate([entry[4] for entry in lamb_sets])
    norm_totals, vector_grad = (
        lax.psum(jnp.stack([weight_sq, update_sq]).astype(jnp.bfloat16), "tensor").astype(
            jnp.float32
        ),
        lax.psum(vector_dp.astype(jnp.bfloat16), "tensor").astype(jnp.float32),
    )
    shard_weight_norms = jnp.sqrt(norm_totals[0])
    shard_update_norms = jnp.sqrt(norm_totals[1])
    trust = shard_weight_norms / shard_update_norms
    bounds = [0, 4, 6, 8, 10, 11]
    new_states = []
    for place, entry in enumerate(matrix_sets):
        factor = trust[bounds[place] : bounds[place + 1]].reshape(-1, 1, 1)
        new_weight = entry[0] - RATE_MATRIX * factor * lamb_sets[place][2]
        new_states.append((new_weight, lamb_sets[place][0], lamb_sets[place][1]))
    depth_full = vector_grad[8 + RATES :]
    depth_first, depth_second, depth_dir, depth_wsq, depth_usq = lamb_parts(
        depth_w[None], depth_m[None], depth_v[None], depth_full[None]
    )
    depth_wnorm = jnp.sqrt(depth_wsq)
    depth_unorm = jnp.sqrt(depth_usq)
    depth_new = depth_w - RATE_MATRIX * (depth_wnorm[0] / depth_unorm[0]) * depth_dir[0]
    weight_norms = jnp.concatenate([shard_weight_norms, depth_wnorm])
    update_norms = jnp.concatenate([shard_update_norms, depth_unorm])
    norm_first, norm_second, norm_dir = adam_step(norm_m, norm_v, vector_grad[:8])
    table_first, table_second, table_dir = adam_step(table_m, table_v, vector_grad[8 : 8 + RATES])
    bn_first, bn_second, bn_dir = adam_step(bn_m, bn_v, jnp.stack([sum_normal_all, sum_grad_all]))
    return (
        fourth.astype(jnp.bfloat16),
        base_grad,
        new_states[0][0],
        new_states[0][1],
        new_states[0][2][:3],
        new_states[0][2][3],
        new_states[1][0],
        new_states[1][1],
        new_states[1][2],
        new_states[2][0],
        new_states[2][1],
        new_states[2][2],
        new_states[3][0],
        new_states[3][1],
        new_states[3][2],
        new_states[4][0][0],
        new_states[4][1][0],
        new_states[4][2][0],
        depth_new,
        depth_first[0],
        depth_second[0],
        norm_w - RATE_VECTOR * norm_dir,
        norm_first,
        norm_second,
        bn_w - RATE_VECTOR * bn_dir,
        bn_first,
        bn_second,
        table_w - RATE_VECTOR * table_dir,
        table_first,
        table_second,
        weight_norms,
        update_norms,
    )


def solution(mesh):
    placed = (
        P(("dp", "tensor"), None),
        P(("dp", "tensor"), None),
        P("dp"),
        P("dp"),
        P(None, None, "tensor"),
        P(None, None, "tensor"),
        P(None, None, "tensor"),
        P(None, None, "tensor"),
        P(None, None, "tensor"),
        P(None, None, "tensor"),
        P(None, "tensor", None),
        P(None, "tensor", None),
        P(None, "tensor", None),
        P(None, None, "tensor"),
        P(None, None, "tensor"),
        P(None, None, "tensor"),
        P("tensor", None),
        P("tensor", None),
        P("tensor", None),
        P(),
        P(),
        P(),
        P(),
        P(),
        P(),
        P(),
        P(),
        P(),
        P(),
        P(),
        P(),
    )
    return jax.shard_map(
        body,
        mesh=mesh,
        in_specs=placed,
        out_specs=(
            P(("dp", "tensor"), None),
            P(("dp", "tensor"), None),
            P(None, None, "tensor"),
            P(None, None, "tensor"),
            P(None, None, "tensor"),
            P(None, "tensor"),
            P(None, None, "tensor"),
            P(None, None, "tensor"),
            P(None, None, "tensor"),
            P(None, "tensor", None),
            P(None, "tensor", None),
            P(None, "tensor", None),
            P(None, None, "tensor"),
            P(None, None, "tensor"),
            P(None, None, "tensor"),
            P("tensor", None),
            P("tensor", None),
            P("tensor", None),
            P(),
            P(),
            P(),
            P(),
            P(),
            P(),
            P(),
            P(),
            P(),
            P(),
            P(),
            P(),
            P(),
            P(),
        ),
        check_vma=False,
    )
```

profile of v0, /device:TPU:0, one launch (start us, length us, event | category | flops | bytes accessed | tf_op | source)
XLA Modules:
  0.0 1115.1 jit_solution(11079958761843603074)
XLA Ops:
  13.1 11.3 %all_gather.21 = bf16[4,324,324]{1,0,2:T(4,128)(2,1)S(1)} all-gather(bf16[4,324,81]{1,0,2:T(4,128)(2,1)S(1)} %get-tuple-element.280), channel_id=1, replica_groups=mesh['dp'=8,'tensor'=4] {'tensor'}, dimensions={2}, use_global_device_ids=true | all-gather | bytes 1049760 | tf_op jit(solution)/shard_map/all_gather | solution.py:211
  55.4 24.6 %all-gather.13.cloned.1.call-done = bf16[4,992,324]{1,2,0:T(8,128)(2,1)} async-done(((bf16[1,992,324]{1,2,0:T(8,128)(2,1)}), bf16[4,992,324]{1,2,0:T(8,128)(2,1)}) %all-gather.13.cloned.1.call-update) | async-done | bytes 2571280 | tf_op jit(solution)/shard_map/all_gather | solution.py:68
  107.6 37.4 %reduce-scatter.19.cloned.1.call-done = bf16[992,324]{1,0:T(8,128)(2,1)} async-done(((bf16[3968,324]{1,0:T(8,128)(2,1)}), bf16[992,324]{1,0:T(8,128)(2,1)}) %reduce-scatter.19.cloned.1.call-update) | async-done | bytes 642832
  153.4 21.7 %all-gather.15.cloned.1.call-done = bf16[4,992,324]{1,2,0:T(8,128)(2,1)} async-done(((bf16[1,992,324]{1,2,0:T(8,128)(2,1)}), bf16[4,992,324]{1,2,0:T(8,128)(2,1)}) %all-gather.15.cloned.1.call-update) | async-done | bytes 2571280 | tf_op jit(solution)/shard_map/all_gather | solution.py:68
  192.7 32.0 %multiply_reduce_fusion.46 = (f32[81]{0:T(128)S(1)}, f32[8,496,81]{1,0,2:T(8,128)}) fusion(f32[8,496]{1,0:T(8,128)S(1)} %fusion.131, f32[81]{0:T(128)S(1)} %get-tuple-element.311, f32[81]{0:T(128)S(1)} %get-tuple-element.310, f32[81]{0:T(128)S(1)} %get-tuple-element.282, f32[81]{0:T(128)S(1)} %get-tuple-element.283, f32[81]{0:T(128)S(1)} %get-tuple-element.284, ...), kind=kLoop, calls=%fused_computation.237 | loop fusion | flops 20248624 | bytes 2597504 | tf_op jit(solution)/shard_map/reduce_sum | solution.py:271
  228.0 39.6 %all-reduce.4 = (f32[324]{0:T(512)S(1)}, f32[]{:T(128)}) all-reduce(f32[324]{0:T(512)S(1)} %dynamic_update_slice.15, f32[]{:T(128)} %convert_reduce_fusion), channel_id=1, replica_groups=mesh['dp'=8,'tensor'=4] {'dp','tensor'}, use_global_device_ids=true, to_apply=%region_8.9 | all-reduce | flops 325 | bytes 2600 | tf_op jit(solution)/shard_map/psum | solution.py:272
  271.1 41.4 %psum.93 = f32[324]{0:T(512)S(1)} all-reduce(f32[324]{0:T(512)S(1)} %dynamic_update_slice.16), channel_id=1, replica_groups=mesh['dp'=8,'tensor'=4] {'dp','tensor'}, use_global_device_ids=true, to_apply=%region_12.13 | all-reduce | flops 324 | bytes 2592 | tf_op jit(solution)/shard_map/psum | solution.py:276
  323.0 37.2 %reduce-scatter.21.cloned.1.call-done = bf16[992,324]{1,0:T(8,128)(2,1)} async-done(((bf16[3968,324]{1,0:T(8,128)(2,1)}), bf16[992,324]{1,0:T(8,128)(2,1)}) %reduce-scatter.21.cloned.1.call-update) | async-done | bytes 642832
  365.5 26.0 %all-gather.17.cloned.1.call-done = bf16[4,992,324]{1,2,0:T(8,128)(2,1)} async-done(((bf16[1,992,324]{1,2,0:T(8,128)(2,1)}), bf16[4,992,324]{1,2,0:T(8,128)(2,1)}) %all-gather.17.cloned.1.call-update) | async-done | bytes 2571280 | tf_op jit(solution)/shard_map/all_gather | solution.py:68
  419.6 36.7 %reduce-scatter.23.cloned.1.call-done = bf16[992,324]{1,0:T(8,128)(2,1)} async-done(((bf16[3968,324]{1,0:T(8,128)(2,1)}), bf16[992,324]{1,0:T(8,128)(2,1)}) %reduce-scatter.23.cloned.1.call-update) | async-done | bytes 642832
  463.7 26.0 %all-gather.19.cloned.1.call-done = bf16[4,992,324]{1,2,0:T(8,128)(2,1)} async-done(((bf16[1,992,324]{1,2,0:T(8,128)(2,1)}), bf16[4,992,324]{1,2,0:T(8,128)(2,1)}) %all-gather.19.cloned.1.call-update) | async-done | bytes 2571280 | tf_op jit(solution)/shard_map/all_gather | solution.py:72
  517.1 37.3 %reduce-scatter.25.cloned.1.call-done = bf16[992,324]{1,0:T(8,128)(2,1)} async-done(((bf16[3968,324]{1,0:T(8,128)(2,1)}), bf16[992,324]{1,0:T(8,128)(2,1)}) %reduce-scatter.25.cloned.1.call-update) | async-done | bytes 642832
  563.7 26.0 %all-gather.21.cloned.1.call-done = bf16[4,992,324]{1,2,0:T(8,128)(2,1)} async-done(((bf16[1,992,324]{1,2,0:T(8,128)(2,1)}), bf16[4,992,324]{1,2,0:T(8,128)(2,1)}) %all-gather.21.cloned.1.call-update) | async-done | bytes 2571280 | tf_op jit(solution)/shard_map/all_gather | solution.py:72
  606.6 39.5 %all-reduce.3 = (f32[324]{0:T(512)S(1)}, f32[324]{0:T(512)S(1)}) all-reduce(f32[324]{0:T(512)S(1)} %dynamic_update_slice.18, f32[324]{0:T(512)S(1)} %dynamic_update_slice.17), channel_id=1, replica_groups=mesh['dp'=8,'tensor'=4] {'dp','tensor'}, use_global_device_ids=true, to_apply=%region_27.28 | all-reduce | flops 648 | bytes 5184 | tf_op jit(solution)/shard_map/psum | solution.py:304
  656.3 31.3 %fusion.76 = f32[8,496,81]{1,0,2:T(8,128)} fusion(f32[8,496,81]{1,0,2:T(8,128)} %reshape.371, f32[81]{0:T(128)S(1)} %copy-done.176, f32[81]{0:T(128)S(1)} %copy-done.174, f32[81]{0:T(128)S(1)} %get-tuple-element.282, f32[81]{0:T(128)S(1)} %get-tuple-element.283, f32[81]{0:T(128)S(1)} %get-tuple-element.284, f32[81]{0:T(128)S(1)} %get-tuple-element.285, ...), kind=kLoop, calls=%fused_computation.199 | loop fusion | flops 19605888 | bytes 2581308 | tf_op jit(solution)/shard_map/add | solution.py:134
  701.4 37.7 %reduce-scatter.27.cloned.1.call-done = bf16[992,324]{1,0:T(8,128)(2,1)} async-done(((bf16[3968,324]{1,0:T(8,128)(2,1)}), bf16[992,324]{1,0:T(8,128)(2,1)}) %reduce-scatter.27.cloned.1.call-update) | async-done | bytes 642832
  747.9 26.1 %all-gather.23.cloned.1.call-done = bf16[4,992,324]{1,2,0:T(8,128)(2,1)} async-done(((bf16[1,992,324]{1,2,0:T(8,128)(2,1)}), bf16[4,992,324]{1,2,0:T(8,128)(2,1)}) %all-gather.23.cloned.1.call-update) | async-done | bytes 2571280 | tf_op jit(solution)/shard_map/all_gather | solution.py:72
  817.2 21.4 %reduce-scatter.29.cloned.1.call-done = bf16[992,324]{1,0:T(8,128)(2,1)} async-done(((bf16[3968,324]{1,0:T(8,128)(2,1)}), bf16[992,324]{1,0:T(8,128)(2,1)}) %reduce-scatter.29.cloned.1.call-update) | async-done | bytes 642832
  883.6 30.6 %all-reduce.10.cloned.1.call-done = bf16[4,324,324]{1,0,2:T(4,128)(2,1)} async-done(((bf16[4,324,324]{1,0,2:T(4,128)(2,1)}), bf16[4,324,324]{1,0,2:T(4,128)(2,1)}) %all-reduce.10.cloned.1.call-update) | async-done | bytes 839824
  925.3 7.8 multiply_reduce_fusion.33
  933.2 10.9 multiply_reduce_fusion.15
  952.8 39.1 %psum.102 = bf16[42,324]{1,0:T(8,128)(2,1)} all-reduce(f32[42,324]{1,0:T(8,128)S(1)} %concatenate.25), channel_id=1, replica_groups=mesh['dp'=8,'tensor'=4] {'dp'}, use_global_device_ids=true, to_apply=%region_93.94 | all-reduce | flops 13608 | bytes 81648 | tf_op jit(solution)/shard_map/psum | solution.py:401
  991.9 54.8 %all-reduce.12.cloned.1.call-done = (f32[4,324,81]{1,0,2:T(4,128)}, f32[2,324,324]{2,1,0:T(8,128)}, f32[2,324,324]{2,1,0:T(8,128)}, f32[2,324,81]{1,2,0:T(8,128)}, f32[81,324]{1,0:T(8,128)}) async-done(((f32[4,324,81]{1,0,2:T(4,128)}, f32[2,324,324]{2,1,0:T(8,128)}, f32[2,324,324]{2,1,0:T(8,128)}, f32[2,324,81]{1,2,0:T(8,128)}, f32[81,324]{1,0:T(8,128)}), (f32[4,324,81]{1,0,2:T(4,128)}, ...) | async-done | bytes 2414464 | tf_op jit(solution)/shard_map/psum | solution.py:401
  1069.7 12.8 %all-reduce.6 = (bf16[2,11]{1,0:T(2,128)(2,1)S(1)}, bf16[42,324]{1,0:T(8,128)(2,1)}) all-reduce(bf16[2,11]{1,0:T(2,128)(2,1)} %pad_maximum_fusion.5, bf16[42,324]{1,0:T(8,128)(2,1)S(1)} %copy-done.90), channel_id=1, replica_groups=mesh['dp'=8,'tensor'=4] {'tensor'}, use_global_device_ids=true, to_apply=%region_51.52 | all-reduce | flops 13630 | bytes 54520 | tf_op jit(solution)/shard_map/psum | solution.py:415
  (635 shorter events, 386.7 us)
Async XLA Ops:
  7.2 72.8 %all-gather.13.cloned.1.call-start = ((), (), s32[]{:S(2)}) async-start(), calls=%async_computation.6 | async-start | bytes 3358720 | tf_op jit(solution)/shard_map/all_gather | solution.py:68
  11.0 136.0 %copy-start.103 = (f32[324]{0:T(512)}, f32[324]{0:T(512)S(1)}, u32[]{:S(2)}) copy-start(f32[324]{0:T(512)S(1)} %get-tuple-element.215) | copy-start | bytes 3892
  51.8 94.7 %copy-start.6 = (f32[992,324]{0,1:T(8,128)}, f32[992,324]{0,1:T(8,128)S(1)}, u32[]{:S(2)}) copy-start(f32[992,324]{0,1:T(8,128)S(1)} %get-tuple-element.324) | copy-start | bytes 3856900
  53.1 92.0 %reduce-scatter.19.cloned.1.call-start = ((), (), s32[]{:S(2)}) async-start(), calls=%async_computation.12 | async-start | bytes 3809280
  107.6 67.5 %all-gather.15.cloned.1.call-start = ((), (), s32[]{:S(2)}) async-start(), calls=%async_computation.7 | async-start | bytes 3358720 | tf_op jit(solution)/shard_map/all_gather | solution.py:68
  149.0 211.2 %reduce-scatter.21.cloned.1.call-start = ((), (), s32[]{:S(2)}) async-start(), calls=%async_computation.13 | async-start | bytes 3809280
  153.4 159.7 %copy-start.177 = (f32[81]{0:T(128)}, f32[81]{0:T(128)S(1)}, u32[]{:S(2)}) copy-start(f32[81]{0:T(128)S(1)} %get-tuple-element.314) | copy-start | bytes 976
  153.4 159.7 %copy-start.188 = (f32[81]{0:T(128)}, f32[81]{0:T(128)S(1)}, u32[]{:S(2)}) copy-start(f32[81]{0:T(128)S(1)} %get-tuple-element.315) | copy-start | bytes 976
  270.8 45.2 %copy-start.67 = (f32[81,324]{1,0:T(8,128)S(1)}, f32[81,324]{1,0:T(8,128)}, u32[]{:S(2)}) copy-start(f32[81,324]{1,0:T(8,128)} %param.47) | copy-start | bytes 314932
  313.1 288.5 %copy-start.179 = (f32[81]{0:T(128)}, f32[81]{0:T(128)S(1)}, u32[]{:S(2)}) copy-start(f32[81]{0:T(128)S(1)} %add_rsqrt_fusion.4) | copy-start | bytes 976
  322.9 68.6 %all-gather.17.cloned.1.call-start = ((), (), s32[]{:S(2)}) async-start(), calls=%async_computation.8 | async-start | bytes 3358720 | tf_op jit(solution)/shard_map/all_gather | solution.py:68
  365.5 90.8 %reduce-scatter.23.cloned.1.call-start = ((), (), s32[]{:S(2)}) async-start(), calls=%async_computation.14 | async-start | bytes 3809280
  418.8 70.9 %all-gather.19.cloned.1.call-start = ((), (), s32[]{:S(2)}) async-start(), calls=%async_computation.9 | async-start | bytes 3358720 | tf_op jit(solution)/shard_map/all_gather | solution.py:72
  463.6 90.7 %reduce-scatter.25.cloned.1.call-start = ((), (), s32[]{:S(2)}) async-start(), calls=%async_computation.15 | async-start | bytes 3809280
  516.9 72.9 %all-gather.21.cloned.1.call-start = ((), (), s32[]{:S(2)}) async-start(), calls=%async_computation.10 | async-start | bytes 3358720 | tf_op jit(solution)/shard_map/all_gather | solution.py:72
  563.7 175.4 %reduce-scatter.27.cloned.1.call-start = ((), (), s32[]{:S(2)}) async-start(), calls=%async_computation.16 | async-start | bytes 3809280
  700.9 73.1 %all-gather.23.cloned.1.call-start = ((), (), s32[]{:S(2)}) async-start(), calls=%async_computation.11 | async-start | bytes 3358720 | tf_op jit(solution)/shard_map/all_gather | solution.py:72
  747.9 90.8 %reduce-scatter.29.cloned.1.call-start = ((), (), s32[]{:S(2)}) async-start(), calls=%async_computation.17 | async-start | bytes 3809280
  801.2 113.0 %all-reduce.10.cloned.1.call-start = ((), (), s32[]{:S(2)}) async-start(), calls=%async_computation.18 | async-start | bytes 1990656
  878.4 168.3 %all-reduce.12.cloned.1.call-start = ((), (), s32[]{:S(2)}) async-start(), calls=%async_computation.19 | async-start | bytes 5836800 | tf_op jit(solution)/shard_map/psum | solution.py:401
  951.0 98.2 %copy-start.86 = (f32[2,324,81]{1,0,2:T(2,128)S(1)}, f32[2,324,81]{1,0,2:T(2,128)}, u32[]{:S(2)}) copy-start(f32[2,324,81]{1,0,2:T(2,128)} %param.45) | copy-start | bytes 629860
  951.5 97.7 %copy-start.87 = (f32[2,324,81]{1,0,2:T(2,128)S(1)}, f32[2,324,81]{1,0,2:T(2,128)}, u32[]{:S(2)}) copy-start(f32[2,324,81]{1,0,2:T(2,128)} %param.46) | copy-start | bytes 629860
  991.9 59.9 %copy-start.41 = (f32[4,324,81]{1,0,2:T(4,128)S(1)}, f32[4,324,81]{1,0,2:T(4,128)}, u32[]{:S(2)}) copy-start(f32[4,324,81]{1,0,2:T(4,128)} %param.35) | copy-start | bytes 1259716
  991.9 59.9 %copy-start.82 = (f32[4,324,81]{1,0,2:T(4,128)S(1)}, f32[4,324,81]{1,0,2:T(4,128)}, u32[]{:S(2)}) copy-start(f32[4,324,81]{1,0,2:T(4,128)} %param.36) | copy-start | bytes 1259716
  (185 other events, 1909.2 us)
Sparse Core Ops, SparseCore 0:
  53.2 26.8 all-gather.12
  107.7 37.3 reduce-scatter.18
  149.1 25.9 all-gather.14
  323.0 37.1 reduce-scatter.20
  365.6 25.9 all-gather.16
  419.0 37.3 reduce-scatter.22
  463.8 25.9 all-gather.18
  517.0 37.3 reduce-scatter.24
  563.8 25.9 all-gather.20
  701.0 38.0 reduce-scatter.26
  748.0 25.9 all-gather.22
  801.3 37.3 reduce-scatter.28
  878.5 35.6 all-reduce.9
  920.0 126.6 all-reduce.11
where the time goes:
time: 1130 us; the launch traced here: 1120 us
  waiting for transfers between devices  444 us (39%)
  local copies, waits for them, and re-layouts  208 us (18%)
  blocking collectives  184 us (16%)
  other arithmetic  163 us (14%)
  matrix products  95.2 us (8%)
  between operations  19.3 us (2%)
    unnamed x21, waiting for transfers between devices  239 us
    unnamed x426, local copies, waits for them, and re-layouts  112 us
    all_gather x3, waiting for transfers between devices, spread_grads(): return lax.all_gather(grads_low, 'tensor', axis=0, tiled=True)  78.1 us
    all_gather x3, waiting for transfers between devices, spread_rows(): return lax.all_gather(rows_low, 'tensor', axis=0, tiled=True)  72.3 us
    psum x1, waiting for transfers between devices, body(): lax.psum((attn_part, fin_part, fout_part, convin_grad, convout_grad, vect...  54.8 us
    psum x1, blocking collectives, body(): lax.psum(widen(jnp.sum(center * center * group_weight, axis=0)), ('dp', '...  41.4 us
    psum x1, blocking collectives, body(): lax.psum((sum_local, count_local), ('dp', 'tensor'))  39.6 us
    psum x1, blocking collectives, body(): lax.psum((widen(jnp.sum(bn_grad, axis=0)), widen(jnp.sum(bn_grad * bn_nor...  39.5 us
  transfers between devices with their start and end apart: 14, of which 14 were waited for; matrix products, arithmetic and copies ran while one was open for 5% of the time, Pallas kernels for 0%

commit v1 on v0

v1 whole, which is shorter than its diff:
```python
import functools
import math

import jax
import jax.numpy as jnp
import numpy as np
from jax import lax
from jax.experimental import pallas as pl
from jax.experimental.pallas import tpu as pltpu
from jax.sharding import PartitionSpec as P

D = 324
HEADS = 4
KERNEL = 31
HALF = KERNEL // 2
RATES = 3
STEP = 10
SLOT = 496
HD = 81
PAD = 96
WIDE = HEADS * PAD

EPS_NORM = 1e-05
BETA_ONE = 0.9
BETA_TWO = 0.999
ADAM_EPS = 1e-06
WEIGHT_DECAY = 0.01
RATE_MATRIX = 0.3
RATE_VECTOR = 0.5
MASK_FILL = -1e30
SCALE = 1.0 / math.sqrt(HD)
PRECISE = lax.Precision.HIGHEST

F32 = jnp.float32
BF16 = jnp.bfloat16
VMEM_LIMIT = 56 * 1024 * 1024
LEAD = 16
SPAN = 544


def dot_nn(left, right):
    return lax.dot_general(left, right, (((1,), (0,)), ((), ())), preferred_element_type=F32)


def dot_nt(left, right):
    return lax.dot_general(left, right, (((1,), (1,)), ((), ())), preferred_element_type=F32)


def dot_tn(left, right):
    return lax.dot_general(left, right, (((0,), (0,)), ((), ())), preferred_element_type=F32)


def sigmoid(value):
    return 0.5 * jnp.tanh(0.5 * value) + 0.5


def ln_forward(resid):
    center = resid - jnp.mean(resid, axis=-1, keepdims=True)
    inv = lax.rsqrt(jnp.mean(center * center, axis=-1, keepdims=True) + EPS_NORM)
    return center * inv, inv


def ln_backward(upstream, normal, inv, gain):
    scaled = upstream * gain
    grad = inv * (
        scaled
        - jnp.mean(scaled, axis=-1, keepdims=True)
        - normal * jnp.mean(scaled * normal, axis=-1, keepdims=True)
    )
    gain_sum = jnp.sum(upstream * normal, axis=0, keepdims=True)
    shift_sum = jnp.sum(upstream, axis=0, keepdims=True)
    return grad, gain_sum, shift_sum


def put_sums(ref, first, gain_sum, shift_sum):
    @pl.when(first)
    def _():
        ref[...] = jnp.zeros_like(ref)

    ref[0:1, :] += gain_sum
    ref[1:2, :] += shift_sum


def attn_fwd_kernel(
    rank_ref, len_ref, kind_ref, frames, table, weights, pick, norm,
    qkv_out, mixed_out, lse_out, n1_out, s1_out, wout_out,
):
    utt = pl.program_id(0)
    rank = rank_ref[0]

    @pl.when(utt == 0)
    def _():
        turned = jnp.concatenate([weights[t ^ rank, 3] for t in range(HEADS)], axis=0)
        spaced = dot_nt(pick[...], turned).astype(BF16)
        wout_out[...] = dot_nn(spaced, pick[...]).astype(BF16)

    base = frames[...].astype(F32) + table[pl.ds(kind_ref[utt], 1), :]
    base_low = base.astype(BF16)
    valid = lax.broadcasted_iota(jnp.int32, (SLOT, 1), 0) < len_ref[utt]
    for head in range(HEADS):
        w_head = weights[head ^ rank, 0:3].reshape(3 * PAD, D)
        qkv = dot_nt(w_head, base_low).astype(BF16)
        qkv_out[head] = qkv
        queries, keys, values = qkv[:PAD], qkv[PAD : 2 * PAD], qkv[2 * PAD :]
        scores = jnp.where(valid, dot_tn(keys, queries) * SCALE, MASK_FILL)
        top = jnp.max(scores, axis=0, keepdims=True)
        expo = jnp.exp(scores - top)
        total = jnp.sum(expo, axis=0, keepdims=True)
        probs = (expo * (1.0 / total)).astype(BF16)
        lse_out[head] = top + jnp.log(total)
        mixed_out[head * PAD : (head + 1) * PAD, :] = dot_nn(values, probs).astype(BF16)
    attn_out = dot_tn(mixed_out[...], wout_out[...])
    normal, inv = ln_forward(base + attn_out)
    n1_out[...] = normal
    s1_out[...] = inv


def ffn_fwd_kernel(
    last_layer, n_in, norm_in, norm_out, w_in, w_out, *rest,
):
    if last_layer:
        cot, weight, hid_out, slope_out, out_ref, grad_ref, sums_ref, acc, z_low = rest
    else:
        hid_out, slope_out, n_ref, s_ref, acc, z_low = rest
    step = pl.program_id(0)

    @pl.when(step == 0)
    def _():
        z = n_in[...] * norm_in[0:1, :] + norm_in[1:2, :]
        acc[...] = z
        z_low[...] = z.astype(BF16)

    pre = dot_nn(z_low[...], w_in[0])
    sig = sigmoid(pre)
    hidden = pre * sig
    hid_low = hidden.astype(BF16)
    hid_out[0] = hid_low
    slope_out[0] = (sig + hidden * (1.0 - sig)).astype(BF16)
    acc[...] += dot_nn(hid_low, w_out[0])

    @pl.when(step == pl.num_programs(0) - 1)
    def _():
        normal, inv = ln_forward(acc[...])
        if last_layer:
            gain = norm_out[0:1, :]
            out_ref[...] = (normal * gain + norm_out[1:2, :]).astype(BF16)
            upstream = cot[...].astype(F32) * weight[...]
            grad, gain_sum, shift_sum = ln_backward(upstream, normal, inv, gain)
            grad_ref[...] = grad
            sums_ref[...] = jnp.zeros_like(sums_ref)
            sums_ref[0:1, :] = gain_sum
            sums_ref[1:2, :] = shift_sum
        else:
            n_ref[...] = normal
            s_ref[...] = inv


def ffn_bwd_kernel(
    up, n_in, s_in, norm_in, w_in, w_out, hid, slope,
    win_out, wout_out, grad_ref, sums_ref, acc, up_low, up_turn, z_turn,
):
    step = pl.program_id(0)

    @pl.when(step == 0)
    def _():
        upstream = up[...]
        acc[...] = upstream
        low = upstream.astype(BF16)
        up_low[...] = low
        up_turn[...] = low.T
        z = n_in[...] * norm_in[0:1, :] + norm_in[1:2, :]
        z_turn[...] = z.astype(BF16).T

    pre_grad = (dot_nt(up_low[...], w_out[0]) * slope[0].astype(F32)).astype(BF16)
    wout_out[0] = dot_nn(up_turn[...], hid[0]).astype(BF16)
    win_out[0] = dot_nn(z_turn[...], pre_grad).astype(BF16)
    acc[...] += dot_nt(pre_grad, w_in[0])

    @pl.when(step == pl.num_programs(0) - 1)
    def _():
        grad, gain_sum, shift_sum = ln_backward(acc[...], n_in[...], s_in[...], norm_in[0:1, :])
        grad_ref[...] = grad
        sums_ref[...] = jnp.zeros_like(sums_ref)
        sums_ref[0:1, :] = gain_sum
        sums_ref[1:2, :] = shift_sum


def shifted(scratch):
    for shift in range(1, 8):
        scratch[shift, 0 : SPAN - 8, :] = scratch[0, pl.ds(shift, SPAN - 8), :]


def load_padded(scratch, signal):
    scratch[0, 0:LEAD, :] = jnp.zeros((LEAD, WIDE), F32)
    scratch[0, pl.ds(LEAD + SLOT, SPAN - LEAD - SLOT), :] = jnp.zeros((SPAN - LEAD - SLOT, WIDE), F32)
    scratch[0, pl.ds(LEAD, SLOT), :] = signal
    shifted(scratch)


ROWS_AT_ONCE = SLOT // 2
LANES = 128


def depth_loop(body_fn):
    for half in range(SLOT // ROWS_AT_ONCE):
        for tile in range(WIDE // LANES):
            body_fn(half * ROWS_AT_ONCE, slice(tile * LANES, (tile + 1) * LANES))


def conv_fwd_kernel(
    rank_ref, len_ref, n_in, norm_in, weights, taps,
    value_out, sig_out, conv_out, stat_out, padded,
):
    utt = pl.program_id(0)
    rank = rank_ref[0]
    z_low = (n_in[...] * norm_in[0:1, :] + norm_in[1:2, :]).astype(BF16)
    w_value = jnp.concatenate([weights[t ^ rank, 0] for t in range(HEADS)], axis=0)
    w_gate = jnp.concatenate([weights[t ^ rank, 1] for t in range(HEADS)], axis=0)
    value = dot_nt(z_low, w_value)
    sig = sigmoid(dot_nt(z_low, w_gate))
    value_out[...] = value
    sig_out[...] = sig
    count = len_ref[utt]
    valid = (lax.broadcasted_iota(jnp.int32, (SLOT, 1), 0) < count).astype(F32)
    load_padded(padded, value * sig * valid)

    def block(row, lanes):
        total = jnp.zeros((ROWS_AT_ONCE, LANES), F32)
        for tap in range(KERNEL):
            place = tap + 1
            rows = pl.ds(row + place // 8 * 8, ROWS_AT_ONCE)
            total = total + padded[place % 8, rows, lanes] * taps[tap : tap + 1, lanes]
        conv_out[pl.ds(row, ROWS_AT_ONCE), lanes] = total

    depth_loop(block)
    conv = conv_out[...]
    number = count.astype(F32)
    mean = jnp.sum(conv * valid, axis=0, keepdims=True) / number
    center = (conv - mean) * valid
    stat_out[...] = jnp.zeros_like(stat_out)
    stat_out[0:1, :] = mean
    stat_out[1:2, :] = jnp.sum(center * center, axis=0, keepdims=True)
    stat_out[2:3, :] = jnp.zeros_like(mean) + number


def mid_fwd_kernel(conv, stats, bn, n_in, norm_in, weights, act_out, n_ref, s_ref):
    normal = (conv[...] - stats[0:1, :]) * stats[1:2, :]
    out = normal * bn[0:1, :] + bn[1:2, :]
    act = (out * sigmoid(out)).astype(BF16)
    act_out[...] = act
    second = n_in[...] * norm_in[0:1, :] + norm_in[1:2, :]
    normal, inv = ln_forward(second + dot_nn(act, weights[...]))
    n_ref[...] = normal
    s_ref[...] = inv


def mid_bwd_kernel(rank_ref, conv, stats, bn, act, grad, weights, b_out, wgrad_out, sums_ref, acc):
    utt = pl.program_id(0)
    grad_low = grad[...].astype(BF16)
    normal = (conv[...] - stats[0:1, :]) * stats[1:2, :]
    out = normal * bn[0:1, :] + bn[1:2, :]
    sig = sigmoid(out)
    b_grad = dot_nt(grad_low, weights[...]) * (sig * (1.0 + out * (1.0 - sig)))
    b_out[...] = b_grad
    put_sums(
        sums_ref,
        utt == 0,
        jnp.sum(b_grad * normal, axis=0, keepdims=True),
        jnp.sum(b_grad, axis=0, keepdims=True),
    )
    part = dot_tn(act[...], grad_low)

    @pl.when(utt == 0)
    def _():
        acc[...] = part

    @pl.when(utt > 0)
    def _():
        acc[...] += part

    @pl.when(utt == pl.num_programs(0) - 1)
    def _():
        rank = rank_ref[0]
        for t in range(HEADS):
            wgrad_out[t ^ rank] = acc[t * PAD : (t + 1) * PAD, :].astype(BF16)


def conv_bwd_kernel(
    rank_ref, len_ref, b_in, conv, value_in, sig_in, stats, bn, bsums, taps, weights,
    n_in, s_in, norm_in, up, grad_ref, wgrad_out, tap_out, sums_ref, glu_pad, cg_pad, cg_ref,
    gg_ref, acc,
):
    utt = pl.program_id(0)
    rank = rank_ref[0]
    valid = (lax.broadcasted_iota(jnp.int32, (SLOT, 1), 0) < len_ref[utt]).astype(F32)
    value, sig = value_in[...], sig_in[...]
    load_padded(glu_pad, value * sig * valid)
    gain, inv = bn[0:1, :], stats[1:2, :]
    normal = (conv[...] - stats[0:1, :]) * inv
    conv_grad = (valid * inv) * (
        b_in[...] * gain - gain * bsums[1:2, :] - normal * (gain * bsums[0:1, :])
    )
    cg_ref[...] = conv_grad
    load_padded(cg_pad, conv_grad)

    @pl.when(utt == 0)
    def _():
        tap_out[...] = jnp.zeros_like(tap_out)

    def block(row, lanes):
        own = cg_ref[pl.ds(row, ROWS_AT_ONCE), lanes]
        for tap in range(KERNEL):
            place = tap + 1
            rows = pl.ds(row + place // 8 * 8, ROWS_AT_ONCE)
            part = glu_pad[place % 8, rows, lanes] * own
            tap_out[tap, :, lanes] += jnp.sum(part.reshape(ROWS_AT_ONCE // 8, 8, LANES), axis=0)

    depth_loop(block)

    def back_block(row, lanes):
        total = jnp.zeros((ROWS_AT_ONCE, LANES), F32)
        for tap in range(KERNEL):
            place = KERNEL - tap
            rows = pl.ds(row + place // 8 * 8, ROWS_AT_ONCE)
            total = total + cg_pad[place % 8, rows, lanes] * taps[tap : tap + 1, lanes]
        gg_ref[pl.ds(row, ROWS_AT_ONCE), lanes] = total

    depth_loop(back_block)
    glu_grad = gg_ref[...] * valid
    value_grad = (glu_grad * sig).astype(BF16)
    gate_grad = (glu_grad * value * sig * (1.0 - sig)).astype(BF16)
    w_value = jnp.concatenate([weights[t ^ rank, 0] for t in range(HEADS)], axis=0)
    w_gate = jnp.concatenate([weights[t ^ rank, 1] for t in range(HEADS)], axis=0)
    z_low = (n_in[...] * norm_in[0:1, :] + norm_in[1:2, :]).astype(BF16)
    value_part = dot_tn(value_grad, z_low)
    gate_part = dot_tn(gate_grad, z_low)

    @pl.when(utt == 0)
    def _():
        acc[0] = value_part
        acc[1] = gate_part

    @pl.when(utt > 0)
    def _():
        acc[0] += value_part
        acc[1] += gate_part

    @pl.when(utt == pl.num_programs(0) - 1)
    def _():
        for t in range(HEADS):
            wgrad_out[t ^ rank, 0] = acc[0, t * PAD : (t + 1) * PAD, :].astype(BF16)
            wgrad_out[t ^ rank, 1] = acc[1, t * PAD : (t + 1) * PAD, :].astype(BF16)

    upstream = up[...] + dot_nn(value_grad, w_value) + dot_nn(gate_grad, w_gate)
    grad, gain_sum, shift_sum = ln_backward(upstream, n_in[...], s_in[...], norm_in[0:1, :])
    grad_ref[...] = grad
    put_sums(sums_ref, utt == 0, gain_sum, shift_sum)


def attn_bwd_kernel(
    rank_ref, len_ref, kind_ref, frames, table, weights, wout, pick, qkv_in, mixed, lse, grad,
    grad_out, wgrad_out, table_out, acc, acc_out,
):
    utt = pl.program_id(0)
    rank = rank_ref[0]
    kind = kind_ref[utt]

    @pl.when(utt == 0)
    def _():
        acc[...] = jnp.zeros_like(acc)
        acc_out[...] = jnp.zeros_like(acc_out)
        table_out[...] = jnp.zeros_like(table_out)

    base_low = (frames[...].astype(F32) + table[pl.ds(kind, 1), :]).astype(BF16)
    valid = lax.broadcasted_iota(jnp.int32, (SLOT, 1), 0) < len_ref[utt]
    upstream = grad[...]
    up_low = upstream.astype(BF16)
    acc_out[...] += dot_nn(mixed[...], up_low)
    mixed_grad = dot_nt(wout[...], up_low).astype(BF16)
    total = upstream
    for head in range(HEADS):
        queries = qkv_in[head, 0:PAD, :]
        keys = qkv_in[head, PAD : 2 * PAD, :]
        values = qkv_in[head, 2 * PAD :, :]
        up_head = mixed_grad[head * PAD : (head + 1) * PAD, :]
        scores = jnp.where(valid, dot_tn(keys, queries) * SCALE, MASK_FILL)
        probs = jnp.exp(scores - lse[head])
        prob_grad = dot_tn(values, up_head)
        delta = jnp.sum(prob_grad * probs, axis=0, keepdims=True)
        score_grad = (probs * (prob_grad - delta)).astype(BF16)
        query_grad = (dot_nn(keys, score_grad) * SCALE).astype(BF16)
        key_grad = (dot_nt(queries, score_grad) * SCALE).astype(BF16)
        value_grad = dot_nt(up_head, probs.astype(BF16)).astype(BF16)
        grads = jnp.concatenate([query_grad, key_grad, value_grad], axis=0)
        acc[head] += dot_nn(grads, base_low)
        total = total + dot_tn(grads, weights[head ^ rank, 0:3].reshape(3 * PAD, D))
    grad_out[...] = total
    column = jnp.sum(total, axis=0, keepdims=True)
    place = lax.broadcasted_iota(jnp.int32, table_out.shape, 0)
    table_out[...] += jnp.where(place == kind, column, 0.0)

    @pl.when(utt == pl.num_programs(0) - 1)
    def _():
        turned = dot_nt(pick[...], acc_out[...].astype(BF16)).astype(BF16)
        turned = dot_nn(turned, pick[...]).astype(BF16)
        for t in range(HEADS):
            wgrad_out[t ^ rank, 0:3] = acc[t].astype(BF16).reshape(3, PAD, D)
            wgrad_out[t ^ rank, 3] = turned[t * PAD : (t + 1) * PAD, :]


def adam_step(first, second, grad_full):
    first_new = BETA_ONE * first + (1.0 - BETA_ONE) * grad_full
    second_new = BETA_TWO * second + (1.0 - BETA_TWO) * grad_full * grad_full
    direction = (first_new * (1.0 / (1.0 - BETA_ONE**STEP))) / (
        jnp.sqrt(second_new * (1.0 / (1.0 - BETA_TWO**STEP))) + ADAM_EPS
    )
    return (first_new, second_new, direction)


def lamb_kernel(turn, weight, first, second, grad, m_out, v_out, u_out, sums_out):
    full = grad[0].astype(F32)
    if turn:
        full = full.T
    rows, columns = weight.shape[1:]
    full = full[:rows, :columns]
    own = weight[0]
    first_new, second_new, direction = adam_step(first[0], second[0], full)
    direction = direction + WEIGHT_DECAY * own
    m_out[0] = first_new
    v_out[0] = second_new
    u_out[0] = direction
    place = lax.broadcasted_iota(jnp.int32, (8, 128), 0)
    sums_out[0] = jnp.where(place == 0, jnp.sum(own * own), jnp.sum(direction * direction))


def whole(shape):
    return pl.BlockSpec(shape, lambda *_: (0,) * len(shape))


def lead(shape, rest):
    return pl.BlockSpec(shape, lambda i, *_: (i,) + (0,) * rest)


SMEM = pl.BlockSpec(memory_space=pltpu.SMEM)


def call(kernel, grid, in_specs, out_specs, out_shape, scratch=(), cost=None):
    return pl.pallas_call(
        kernel,
        grid=(grid,),
        in_specs=in_specs,
        out_specs=out_specs,
        out_shape=[jax.ShapeDtypeStruct(*entry) for entry in out_shape],
        scratch_shapes=list(scratch),
        cost_estimate=None
        if cost is None
        else pl.CostEstimate(flops=cost, bytes_accessed=10_000_000, transcendentals=0),
        compiler_params=pltpu.CompilerParams(vmem_limit_bytes=VMEM_LIMIT),
    )


def swap(value, axis, bit):
    size = lax.axis_size(axis)
    return lax.ppermute(value, axis, [(i, i ^ bit) for i in range(size)])


def bits_of(axis):
    size = lax.axis_size(axis)
    assert size & (size - 1) == 0
    return [1 << i for i in range(size.bit_length() - 1)]


def gather_tensor(shard):
    parts = {0: shard}
    for bit in reversed(bits_of("tensor")):
        for place in list(parts):
            parts[place ^ bit] = swap(parts[place], "tensor", bit)
    return jnp.stack([parts[i] for i in range(len(parts))])


def reduce_tensor(blocks):
    parts = blocks
    for bit in bits_of("tensor"):
        pairs = parts.reshape((parts.shape[0] // 2, 2) + parts.shape[1:])
        got = swap(pairs[:, 1], "tensor", bit)
        parts = (pairs[:, 0].astype(F32) + got.astype(F32)).astype(BF16)
    return parts[0]


def sum_dp(value):
    for bit in bits_of("dp"):
        value = (value.astype(F32) + swap(value, "dp", bit).astype(F32)).astype(value.dtype)
    return value


def sum_all(value):
    for axis in ("tensor", "dp"):
        for bit in bits_of(axis):
            value = value + swap(value, axis, bit)
    return value


def merge_stats(one, two):
    mean_one, dev_one, count_one = one[0:1], one[1:2], one[2:3]
    mean_two, dev_two, count_two = two[0:1], two[1:2], two[2:3]
    count = count_one + count_two
    mean = (mean_one * count_one + mean_two * count_two) / count
    gap = mean_one - mean_two
    dev = dev_one + dev_two + gap * gap * (count_one * count_two / count)
    return jnp.concatenate([mean, dev, count], axis=0)


def pick_matrix():
    pick = np.zeros((WIDE, D), np.float32)
    for column in range(D):
        pick[column // HD * PAD + column % HD, column] = 1.0
    return pick


def turn_pad(shard):
    turned = jnp.swapaxes(shard, -1, -2)
    widths = [(0, 0)] * (turned.ndim - 2) + [(0, PAD - HD), (0, 0)]
    return jnp.pad(turned, widths)


def body(
    frames, cotangent, lengths, rate_kind, attn_w, attn_m, attn_v, ffin_w, ffin_m, ffin_v,
    ffout_w, ffout_m, ffout_v, convin_w, convin_m, convin_v, convout_w, convout_m, convout_v,
    depth_w, depth_m, depth_v, norm_w, norm_m, norm_v, bn_w, bn_m, bn_v, table_w, table_m, table_v,
):
    rank = lax.axis_index("tensor")
    rank_one = rank.reshape(1).astype(jnp.int32)
    rows = frames.shape[0]
    utts = rows // SLOT
    own_len = lax.dynamic_slice_in_dim(lengths, rank * utts, utts, 0)
    own_kind = lax.dynamic_slice_in_dim(rate_kind, rank * utts, utts, 0)
    slot_index = jnp.arange(SLOT, dtype=jnp.int32)
    weight_col = (slot_index[None, :] < own_len[:, None]).astype(F32).reshape(rows, 1)
    pick = jnp.asarray(pick_matrix(), BF16)
    pick_wide = jnp.asarray(pick_matrix(), F32)

    attn_all = gather_tensor(turn_pad(attn_w.astype(BF16)))
    ffin_low, ffout_low = ffin_w.astype(BF16), ffout_w.astype(BF16)
    ffin_all = [gather_tensor(ffin_low[i]) for i in range(2)]
    ffout_all = [gather_tensor(ffout_low[i]) for i in range(2)]
    convin_all = gather_tensor(turn_pad(convin_w.astype(BF16)))
    convout_low = jnp.pad(convout_w.astype(BF16), ((0, PAD - HD), (0, 0)))
    convout_xor = gather_tensor(convout_low)
    convout_all = jnp.concatenate(
        [lax.dynamic_index_in_dim(convout_xor, t ^ rank, 0, False) for t in range(HEADS)], axis=0
    )
    channel_rows = jnp.concatenate([depth_w, bn_w], axis=0)
    channel_rows = lax.dot_general(
        channel_rows, pick_wide, (((1,), (1,)), ((), ())), precision=PRECISE
    )
    taps, bn = channel_rows[:KERNEL], channel_rows[KERNEL:]
    norms = [jnp.stack([norm_w[i], norm_w[i + 4]]) for i in range(4)]

    rowspec = lead((SLOT, D), 1)
    chanspec = lead((SLOT, WIDE), 1)
    onespec = lead((SLOT, 1), 1)
    normspec = whole((2, D))
    attn_block = (HEADS, 4, PAD, D)
    qkv, mixed, lse, n1, s1, wout = call(
        attn_fwd_kernel,
        utts,
        [SMEM, SMEM, SMEM, rowspec, whole((RATES, D)), whole(attn_block), whole((WIDE, D)), normspec],
        [
            pl.BlockSpec((None, HEADS, 3 * PAD, SLOT), lambda i: (i, 0, 0, 0)),
            pl.BlockSpec((None, WIDE, SLOT), lambda i: (i, 0, 0)),
            pl.BlockSpec((None, HEADS, 1, SLOT), lambda i: (i, 0, 0, 0)),
            rowspec,
            onespec,
            whole((WIDE, D)),
        ],
        [
            ((utts, HEADS, 3 * PAD, SLOT), BF16),
            ((utts, WIDE, SLOT), BF16),
            ((utts, HEADS, 1, SLOT), F32),
            ((rows, D), F32),
            ((rows, 1), F32),
            ((WIDE, D), BF16),
        ],
        cost=8_000_000_000,
    )(rank_one, own_len, own_kind, frames, table_w, attn_all, pick, norms[0])

    hid = ffin_w.shape[2]
    groups = ffin_all[0].shape[0]
    wspec = lead((1, hid, D), 2)
    winspec = lead((1, D, hid), 2)
    hidspec = lead((1, rows, hid), 2)
    ffn_scratch = [pltpu.VMEM((rows, D), F32), pltpu.VMEM((rows, D), BF16)]
    hid_one, slope_one, n2, s2 = call(
        functools.partial(ffn_fwd_kernel, False),
        groups,
        [whole((rows, D)), normspec, normspec, winspec, wspec],
        [hidspec, hidspec, whole((rows, D)), whole((rows, 1))],
        [
            ((groups, rows, hid), BF16),
            ((groups, rows, hid), BF16),
            ((rows, D), F32),
            ((rows, 1), F32),
        ],
        ffn_scratch,
        cost=4_000_000_000,
    )(n1, norms[0], norms[1], ffin_all[0], ffout_all[0])

    convin_block = (HEADS, 2, PAD, D)
    value_pre, gate_sig, conv, stats = call(
        conv_fwd_kernel,
        utts,
        [SMEM, SMEM, rowspec, normspec, whole(convin_block), whole((KERNEL, WIDE))],
        [chanspec, chanspec, chanspec, pl.BlockSpec((None, 8, WIDE), lambda i: (i, 0, 0))],
        [((rows, WIDE), F32)] * 3 + [((utts, 8, WIDE), F32)],
        [pltpu.VMEM((8, SPAN, WIDE), F32)],
        cost=4_000_000_000,
    )(rank_one, own_len, n2, norms[1], convin_all, taps)

    stat = stats[0, :3]
    for i in range(1, utts):
        stat = merge_stats(stat, stats[i, :3])
    for axis in ("tensor", "dp"):
        for bit in bits_of(axis):
            stat = merge_stats(stat, swap(stat, axis, bit))
    valid_count = stat[2:3]
    bn_stats = jnp.concatenate(
        [stat[0:1], lax.rsqrt(stat[1:2] / valid_count + EPS_NORM)], axis=0
    )

    chan_two = whole((2, WIDE))
    act, n3, s3 = call(
        mid_fwd_kernel,
        utts,
        [chanspec, chan_two, chan_two, rowspec, normspec, whole((WIDE, D))],
        [chanspec, rowspec, onespec],
        [((rows, WIDE), BF16), ((rows, D), F32), ((rows, 1), F32)],
        cost=1_000_000_000,
    )(conv, bn_stats, bn, n2, norms[1], convout_all)

    hid_two, slope_two, out, grad_four, sums_four = call(
        functools.partial(ffn_fwd_kernel, True),
        groups,
        [whole((rows, D)), normspec, normspec, winspec, wspec, whole((rows, D)), whole((rows, 1))],
        [hidspec, hidspec, whole((rows, D)), whole((rows, D)), whole((8, D))],
        [
            ((groups, rows, hid), BF16),
            ((groups, rows, hid), BF16),
            ((rows, D), BF16),
            ((rows, D), F32),
            ((8, D), F32),
        ],
        ffn_scratch,
        cost=4_000_000_000,
    )(n3, norms[2], norms[3], ffin_all[1], ffout_all[1], cotangent, weight_col)

    def ffn_backward(up, normal, inv, norm_pair, w_in, w_out, hidden, slope):
        return call(
            ffn_bwd_kernel,
            groups,
            [whole((rows, D)), whole((rows, D)), whole((rows, 1)), normspec, winspec, wspec]
            + [hidspec, hidspec],
            [winspec, wspec, whole((rows, D)), whole((8, D))],
            [
                ((groups, D, hid), BF16),
                ((groups, D, hid), BF16),
                ((rows, D), F32),
                ((8, D), F32),
            ],
            [
                pltpu.VMEM((rows, D), F32),
                pltpu.VMEM((rows, D), BF16),
                pltpu.VMEM((D, rows), BF16),
                pltpu.VMEM((D, rows), BF16),
            ],
            cost=8_000_000_000,
        )(up, normal, inv, norm_pair, w_in, w_out, hidden, slope)

    fin_two, fout_two, grad_three, sums_three = ffn_backward(
        grad_four, n3, s3, norms[2], ffin_all[1], ffout_all[1], hid_two, slope_two
    )

    b_grad, cout_grad, bsums = call(
        mid_bwd_kernel,
        utts,
        [SMEM, chanspec, chan_two, chan_two, chanspec, rowspec, whole((WIDE, D))],
        [chanspec, whole((HEADS, PAD, D)), whole((8, WIDE))],
        [((rows, WIDE), F32), ((HEADS, PAD, D), BF16), ((8, WIDE), F32)],
        [pltpu.VMEM((WIDE, D), F32)],
        cost=2_000_000_000,
    )(rank_one, conv, bn_stats, bn, act, grad_three, convout_all)

    bsum_all = sum_all(bsums[:2])
    bsum_mean = bsum_all / valid_count

    grad_two, cin_grad, tap_sums, sums_two = call(
        conv_bwd_kernel,
        utts,
        [SMEM, SMEM] + [chanspec] * 4 + [chan_two] * 3
        + [whole((KERNEL, WIDE)), whole(convin_block), rowspec, onespec, normspec, rowspec],
        [rowspec, whole(convin_block), whole((KERNEL, 8, WIDE)), whole((8, D))],
        [
            ((rows, D), F32),
            (convin_block, BF16),
            ((KERNEL, 8, WIDE), F32),
            ((8, D), F32),
        ],
        [
            pltpu.VMEM((8, SPAN, WIDE), F32),
            pltpu.VMEM((8, SPAN, WIDE), F32),
            pltpu.VMEM((SLOT, WIDE), F32),
            pltpu.VMEM((SLOT, WIDE), F32),
            pltpu.VMEM((2, WIDE, D), F32),
        ],
        cost=8_000_000_000,
    )(
        rank_one, own_len, b_grad, conv, value_pre, gate_sig, bn_stats, bn, bsum_mean, taps,
        convin_all, n2, s2, norms[1], grad_three,
    )

    fin_one, fout_one, grad_one, sums_one = ffn_backward(
        grad_two, n1, s1, norms[0], ffin_all[0], ffout_all[0], hid_one, slope_one
    )

    in_grad, attn_grad, table_sums = call(
        attn_bwd_kernel,
        utts,
        [SMEM, SMEM, SMEM, rowspec, whole((RATES, D)), whole(attn_block), whole((WIDE, D))]
        + [
            whole((WIDE, D)),
            pl.BlockSpec((None, HEADS, 3 * PAD, SLOT), lambda i: (i, 0, 0, 0)),
            pl.BlockSpec((None, WIDE, SLOT), lambda i: (i, 0, 0)),
            pl.BlockSpec((None, HEADS, 1, SLOT), lambda i: (i, 0, 0, 0)),
            rowspec,
        ],
        [rowspec, whole(attn_block), whole((8, D))],
        [((rows, D), F32), (attn_block, BF16), ((8, D), F32)],
        [pltpu.VMEM((HEADS, 3 * PAD, D), F32), pltpu.VMEM((WIDE, D), F32)],
        cost=16_000_000_000,
    )(
        rank_one, own_len, own_kind, frames, table_w, attn_all, wout, pick, qkv, mixed, lse,
        grad_one,
    )

    fin_two_g, fout_two_g, cout_g = (
        sum_dp(reduce_tensor(g)) for g in (fin_two, fout_two, cout_grad)
    )
    fin_one_g, fout_one_g, cin_g = (
        sum_dp(reduce_tensor(g)) for g in (fin_one, fout_one, cin_grad)
    )
    attn_g = sum_dp(reduce_tensor(attn_grad))

    tap_grad = lax.dot_general(
        jnp.sum(tap_sums, axis=1), pick_wide, (((1,), (0,)), ((), ())), precision=PRECISE
    )
    vectors = sum_all(
        jnp.concatenate(
            [sums_one[:2], sums_two[:2], sums_three[:2], sums_four[:2], table_sums[:RATES], tap_grad],
            axis=0,
        )
    )
    bn_grads = lax.dot_general(bsum_all, pick_wide, (((1,), (0,)), ((), ())), precision=PRECISE)

    def lamb(turn, weight, first, second, grads):
        count, height, width = weight.shape
        spec = lead((1, height, width), 2)
        return call(
            functools.partial(lamb_kernel, turn),
            count,
            [spec, spec, spec, lead((1,) + grads.shape[1:], 2)],
            [spec, spec, spec, lead((1, 8, 128), 2)],
            [(weight.shape, F32)] * 3 + [((count, 8, 128), F32)],
            cost=1_000_000,
        )(weight, first, second, grads)

    sets = [
        (attn_w, lamb(True, attn_w, attn_m, attn_v, attn_g)),
        (ffin_w, lamb(False, ffin_w, ffin_m, ffin_v, jnp.stack([fin_one_g, fin_two_g]))),
        (ffout_w, lamb(True, ffout_w, ffout_m, ffout_v, jnp.stack([fout_one_g, fout_two_g]))),
        (convin_w, lamb(True, convin_w, convin_m, convin_v, cin_g)),
        (
            convout_w[None],
            lamb(False, convout_w[None], convout_m[None], convout_v[None], cout_g[None]),
        ),
    ]
    squares = jnp.concatenate([entry[1][3][:, :2, 0] for entry in sets], axis=0)
    for bit in bits_of("tensor"):
        squares = squares + swap(squares, "tensor", bit)
    shard_norms = jnp.sqrt(squares)
    trust = shard_norms[:, 0] / shard_norms[:, 1]
    new_weights = []
    begin = 0
    for weight, entry in sets:
        factor = trust[begin : begin + weight.shape[0]].reshape(-1, 1, 1)
        begin += weight.shape[0]
        new_weights.append(weight - RATE_MATRIX * factor * entry[2])

    depth_first, depth_second, depth_dir = adam_step(depth_m, depth_v, vectors[8 + RATES :])
    depth_dir = depth_dir + WEIGHT_DECAY * depth_w
    depth_wnorm = jnp.sqrt(jnp.sum(depth_w * depth_w))
    depth_unorm = jnp.sqrt(jnp.sum(depth_dir * depth_dir))
    depth_new = depth_w - RATE_MATRIX * (depth_wnorm / depth_unorm) * depth_dir
    weight_norms = jnp.concatenate([shard_norms[:, 0], depth_wnorm[None]])
    update_norms = jnp.concatenate([shard_norms[:, 1], depth_unorm[None]])
    norm_grad = jnp.concatenate([vectors[0:8:2], vectors[1:8:2]], axis=0)
    norm_first, norm_second, norm_dir = adam_step(norm_m, norm_v, norm_grad)
    table_first, table_second, table_dir = adam_step(table_m, table_v, vectors[8 : 8 + RATES])
    bn_first, bn_second, bn_dir = adam_step(bn_m, bn_v, bn_grads)
    m_of = [entry[1][0] for entry in sets]
    v_of = [entry[1][1] for entry in sets]
    return (
        out,
        in_grad,
        new_weights[0],
        m_of[0],
        v_of[0][:3],
        v_of[0][3],
        new_weights[1],
        m_of[1],
        v_of[1],
        new_weights[2],
        m_of[2],
        v_of[2],
        new_weights[3],
        m_of[3],
        v_of[3],
        new_weights[4][0],
        m_of[4][0],
        v_of[4][0],
        depth_new,
        depth_first,
        depth_second,
        norm_w - RATE_VECTOR * norm_dir,
        norm_first,
        norm_second,
        bn_w - RATE_VECTOR * bn_dir,
        bn_first,
        bn_second,
        table_w - RATE_VECTOR * table_dir,
        table_first,
        table_second,
        weight_norms,
        update_norms,
    )


def solution(mesh):
    rows = P(("dp", "tensor"), None)
    last = P(None, None, "tensor")
    mid = P(None, "tensor", None)
    first = P("tensor", None)
    placed = (rows, rows, P("dp"), P("dp")) + (last,) * 6 + (mid,) * 3 + (last,) * 3 + (first,) * 3
    results = (rows, rows) + (last,) * 3 + (P(None, "tensor"),) + (last,) * 3 + (mid,) * 3
    return jax.shard_map(
        body,
        mesh=mesh,
        in_specs=placed + (P(),) * 12,
        out_specs=results + (last,) * 3 + (first,) * 3 + (P(),) * 14,
        check_vma=False,
    )
```

time: 1130 us -> 416 us (0.37)
  waiting for transfers between devices: 444 us -> 90.1 us
  blocking collectives: 184 us -> 0 us
  local copies, waits for them, and re-layouts: 208 us -> 76.5 us
  Pallas kernels: 0 us -> 129 us
  other arithmetic: 163 us -> 48.2 us
  matrix products: 95.2 us -> 2.13 us
  starting transfers between devices: 1.74 us -> 59.4 us
  between operations: 19.3 us -> 4.05 us
    unnamed x21 -> x0, waiting for transfers between devices: 239 us -> none
    psum x5 -> x0, blocking collectives: 172 us -> none  [the longest x1 41.4 us: body(): lax.psum(widen(jnp.sum(center * center * group_weight, axis=0)), ('dp', '...]
    all_gather x6 -> x0, waiting for transfers between devices: 150 us -> none  [the longest x3 78.1 us: spread_grads(): return lax.all_gather(grads_low, 'tensor', axis=0, tiled=True)]
    pallas_call x0 -> x15, Pallas kernels: none -> 129 us  [the longest x2 25.7 us: ffn_backward(): call(ffn_bwd_kernel, groups, [whole((rows, D)), whole((rows, D)), whole((...]
    reduce_sum x29 -> x2, other arithmetic: 103 us -> 1.59 us  [the longest x1 1.49 us: body(): depth_unorm = jnp.sqrt(jnp.sum(depth_dir * depth_dir))]
    dot_general x35 -> x3, matrix products: 95.2 us -> 2.13 us  [the longest x1 1 us: body(): lax.dot_general(bsum_all, pick_wide, (((1,), (0,)), ((), ())), precision=...]
    ppermute x0 -> x73, waiting for transfers between devices: none -> 90.1 us  [swap(): return lax.ppermute(value, axis, [(i, i ^ bit) for i in range(size)])]
    unnamed x426 -> x129, local copies, waits for them, and re-layouts: 112 us -> 46.3 us
  transfers between devices with their start and end apart: 14 -> 73, of which waited for: 14 -> 25; matrix products, arithmetic and copies ran while one was open for 5% -> 26% of each run, Pallas kernels for 0% -> 22%
where the time goes in v1:
time: 416 us; the launch traced here: 410 us
  Pallas kernels  129 us (31%)
  waiting for transfers between devices  90.1 us (22%)
  local copies, waits for them, and re-layouts  76.5 us (18%)
  starting transfers between devices  59.4 us (14%)
  other arithmetic  48.2 us (12%)
    ppermute x73, waiting for transfers between devices, swap(): return lax.ppermute(value, axis, [(i, i ^ bit) for i in range(size)])  90.1 us
    ppermute x73, starting transfers between devices, swap(): return lax.ppermute(value, axis, [(i, i ^ bit) for i in range(size)])  59.4 us
    unnamed x129, local copies, waits for them, and re-layouts  46.3 us
    pallas_call x2, Pallas kernels, ffn_backward(): call(ffn_bwd_kernel, groups, [whole((rows, D)), whole((rows, D)), whole((...  25.7 us
    pallas_call x1, Pallas kernels, body(): call(conv_bwd_kernel, utts, [SMEM, SMEM] + [chanspec] * 4 + [chan_two] *...  19 us
    pallas_call x5, Pallas kernels, lamb(): call(functools.partial(lamb_kernel, turn), count, [spec, spec, spec, lead...  17.1 us
    pallas_call x1, Pallas kernels, body(): call(attn_bwd_kernel, utts, [SMEM, SMEM, SMEM, rowspec, whole((RATES, D))...  16.9 us
    pallas_call x1, Pallas kernels, body(): call(attn_fwd_kernel, utts, [SMEM, SMEM, SMEM, rowspec, whole((RATES, D))...  12.1 us
  transfers between devices with their start and end apart: 73, of which 25 were waited for; matrix products, arithmetic and copies ran while one was open for 26% of the time, Pallas kernels for 22%

profile of v1, /device:TPU:0, one launch (start us, length us, event | category | flops | bytes accessed | tf_op | source)
XLA Modules:
  0.0 409.8 jit_solution(5663686842642826122)
XLA Ops:
  40.6 12.1 %shard_map.560 = (bf16[2,4,288,496]{3,2,1,0:T(8,128)(2,1)}, bf16[2,384,496]{2,1,0:T(8,128)(2,1)}, f32[2,4,1,496]{3,2,1,0:T(1,128)}, f32[992,324]{1,0:T(8,128)}, ...) custom-call(s32[1]{0:T(128)} %bitcast.rank_ref, s32[2]{0:T(128)} %copy-done.47, s32[2]{0:T(128)} %dynamic_slice.20.kind_ref, ...), custom_call_target="tpu_custom_call" | custom-call | flops 8000000000 | bytes 10000000 | tf_op jit(solution)/shard_map/pallas_call | solution.py:564
  52.7 9.8 %shard_map.561 = (bf16[4,992,324]{2,1,0:T(8,128)(2,1)}, bf16[4,992,324]{2,1,0:T(8,128)(2,1)}, f32[992,324]{1,0:T(8,128)}, f32[992,1]{1,0:T(8,128)}) custom-call(f32[992,324]{1,0:T(8,128)} %get-tuple-element.92.n_in, f32[2,324]{1,0:T(2,128)} %pad_maximum_fusion.18.norm.norm_in, f32[2,324]{1,0:T(2,128)} %pad_maximum_fusion.19.norm_out.norm_in, ...), custom_call_target="tpu_custom_call" | custom-call | flops 4000000000 | bytes 10000000 | tf_op jit(solution)/shard_map/pallas_call | solution.py:593
  62.6 8.3 %shard_map.562 = (f32[992,384]{1,0:T(8,128)}, f32[992,384]{1,0:T(8,128)}, f32[992,384]{1,0:T(8,128)}, f32[2,8,384]{2,1,0:T(8,128)}) custom-call(s32[1]{0:T(128)} %bitcast.rank_ref, s32[2]{0:T(128)} %copy-done.47, f32[992,324]{1,0:T(8,128)} %get-tuple-element.93.n_in, f32[2,324]{1,0:T(2,128)} %pad_maximum_fusion.19.norm_out.norm_in, ...), custom_call_target="tpu_custom_call" | custom-call | flops 4000000000 | bytes 10000000 | tf_op jit(solution)/shard_map/pallas_call | solution.py:609
  90.7 3.7 shard_map.563
  94.5 11.7 %shard_map.564 = (bf16[4,992,324]{2,1,0:T(8,128)(2,1)}, bf16[4,992,324]{2,1,0:T(8,128)(2,1)}, bf16[992,324]{1,0:T(8,128)(2,1)}, f32[992,324]{1,0:T(8,128)}, f32[8,324]{1,0:T(8,128)}) custom-call(f32[992,324]{1,0:T(8,128)} %get-tuple-element.96.n_in, f32[2,324]{1,0:T(2,128)} %get-tuple-element.305.norm_in, f32[2,324]{1,0:T(2,128)} %get-tuple-element.306.norm_out, ...), custom_call_target="tpu_custom_call" | custom-call | flops 4000000000 | bytes 10000000 | tf_op jit(solution)/shard_map/pallas_call | solution.py:640
  106.1 12.8 %shard_map.565 = (bf16[4,324,324]{2,1,0:T(8,128)(2,1)}, bf16[4,324,324]{2,1,0:T(8,128)(2,1)}, f32[992,324]{1,0:T(8,128)}, f32[8,324]{1,0:T(8,128)}) custom-call(f32[992,324]{1,0:T(8,128)} %get-tuple-element.103.up, f32[992,324]{1,0:T(8,128)} %get-tuple-element.96.n_in, f32[992,1]{1,0:T(8,128)} %get-tuple-element.104.s_in, ...), custom_call_target="tpu_custom_call" | custom-call | flops 8000000000 | bytes 10000000 | tf_op jit(solution)/shard_map/pallas_call | solution.py:657
  119.0 5.0 %shard_map.566 = (f32[992,384]{1,0:T(8,128)}, bf16[4,96,324]{2,1,0:T(8,128)(2,1)}, f32[8,384]{1,0:T(8,128)}) custom-call(s32[1]{0:T(128)} %bitcast.rank_ref, f32[992,384]{1,0:T(8,128)} %get-tuple-element.94.conv, f32[2,384]{1,0:T(2,128)} %pad_maximum_fusion.20.stats, f32[2,384]{1,0:T(2,128)} %slice.382.bn, bf16[992,384]{1,0:T(8,128)(2,1)} %get-tuple-element.102.act, ...), custom_call_target="tpu_custom_call" | custom-call | flops 2000000000 | bytes 10000000 | tf_op jit(solution)/shard_map/pallas_call | solution.py:682
  157.6 19.0 %shard_map.567 = (f32[992,324]{1,0:T(8,128)}, bf16[4,2,96,324]{3,2,1,0:T(8,128)(2,1)}, f32[31,8,384]{2,1,0:T(8,128)}, f32[8,324]{1,0:T(8,128)}) custom-call(s32[1]{0:T(128)} %bitcast.rank_ref, s32[2]{0:T(128)} %copy-done.47, f32[992,384]{1,0:T(8,128)} %get-tuple-element.108.b_in, f32[992,384]{1,0:T(8,128)} %get-tuple-element.94.conv, ...), custom_call_target="tpu_custom_call" | custom-call | flops 8000000000 | bytes 10000000 | tf_op jit(solution)/shard_map/pallas_call | solution.py:695
  176.6 12.9 %shard_map.568 = (bf16[4,324,324]{2,1,0:T(8,128)(2,1)}, bf16[4,324,324]{2,1,0:T(8,128)(2,1)}, f32[992,324]{1,0:T(8,128)}, f32[8,324]{1,0:T(8,128)}) custom-call(f32[992,324]{1,0:T(8,128)} %get-tuple-element.113.up, f32[992,324]{1,0:T(8,128)} %get-tuple-element.92.n_in, f32[992,1]{1,0:T(8,128)} %get-tuple-element.114.s_in, ...), custom_call_target="tpu_custom_call" | custom-call | flops 8000000000 | bytes 10000000 | tf_op jit(solution)/shard_map/pallas_call | solution.py:657
  189.5 16.9 %shard_map.569 = (f32[992,324]{1,0:T(8,128)}, bf16[4,4,96,324]{3,2,1,0:T(8,128)(2,1)}, f32[8,324]{1,0:T(8,128)}) custom-call(s32[1]{0:T(128)} %bitcast.rank_ref, s32[2]{0:T(128)} %copy-done.47, s32[2]{0:T(128)} %dynamic_slice.20.kind_ref, bf16[992,324]{1,0:T(8,128)(2,1)} %copy.167.frames, f32[3,324]{1,0:T(4,128)} %table.3, ...), custom_call_target="tpu_custom_call" | custom-call | flops 16000000000 | bytes 10000000 | tf_op jit(solution)/shard_map/pallas_call | solution.py:724
  234.6 3.5 collective-permute-done.72
  243.3 3.4 collective-permute-start.65
  267.0 4.8 %collective-permute-done.52 = bf16[1,324,324]{2,1,0:T(8,128)(2,1)S(1)} collective-permute-done((bf16[1,324,324]{2,1,0:T(8,128)(2,1)S(1)}, bf16[1,324,324]{2,1,0:T(8,128)(2,1)S(1)}, u32[]{:S(2)}, u32[]{:S(2)}) %collective-permute-start.52) | collective-permute-done | bytes 209984 | tf_op jit(solution)/shard_map/ppermute | solution.py:464
  274.0 3.2 collective-permute-done.37
  279.1 3.5 collective-permute-done.47
  308.9 11.5 %collective-permute-done.54 = bf16[324,324]{1,0:T(8,128)(2,1)S(1)} collective-permute-done((bf16[324,324]{1,0:T(8,128)(2,1)S(1)}, bf16[324,324]{1,0:T(8,128)(2,1)S(1)}, u32[]{:S(2)}, u32[]{:S(2)}) %collective-permute-start.54) | collective-permute-done | bytes 209984 | tf_op jit(solution)/shard_map/ppermute | solution.py:464
  321.4 6.4 %collective-permute-done.39 = bf16[324,324]{1,0:T(8,128)(2,1)S(1)} collective-permute-done((bf16[324,324]{1,0:T(8,128)(2,1)S(1)}, bf16[324,324]{1,0:T(8,128)(2,1)S(1)}, u32[]{:S(2)}, u32[]{:S(2)}) %collective-permute-start.39) | collective-permute-done | bytes 209984 | tf_op jit(solution)/shard_map/ppermute | solution.py:464
  327.9 6.5 %collective-permute-done.49 = bf16[324,324]{1,0:T(8,128)(2,1)S(1)} collective-permute-done((bf16[324,324]{1,0:T(8,128)(2,1)S(1)}, bf16[324,324]{1,0:T(8,128)(2,1)S(1)}, u32[]{:S(2)}, u32[]{:S(2)}) %collective-permute-start.49) | collective-permute-done | bytes 209984 | tf_op jit(solution)/shard_map/ppermute | solution.py:464
  334.6 4.1 %collective-permute-done.34 = bf16[4,96,324]{2,1,0:T(8,128)(2,1)S(1)} collective-permute-done((bf16[4,96,324]{2,1,0:T(8,128)(2,1)S(1)}, bf16[4,96,324]{2,1,0:T(8,128)(2,1)S(1)}, u32[]{:S(2)}, u32[]{:S(2)}) %collective-permute-start.34) | collective-permute-done | bytes 248864 | tf_op jit(solution)/shard_map/ppermute | solution.py:464
  339.0 19.1 %collective-permute-done.55 = bf16[324,324]{1,0:T(8,128)(2,1)S(1)} collective-permute-done((bf16[324,324]{1,0:T(8,128)(2,1)S(1)}, bf16[324,324]{1,0:T(8,128)(2,1)S(1)}, u32[]{:S(2)}, u32[]{:S(2)}) %collective-permute-start.55) | collective-permute-done | bytes 209984 | tf_op jit(solution)/shard_map/ppermute | solution.py:464
  358.1 5.3 %collective-permute-done.40 = bf16[324,324]{1,0:T(8,128)(2,1)S(1)} collective-permute-done((bf16[324,324]{1,0:T(8,128)(2,1)S(1)}, bf16[324,324]{1,0:T(8,128)(2,1)S(1)}, u32[]{:S(2)}, u32[]{:S(2)}) %collective-permute-start.40) | collective-permute-done | bytes 209984 | tf_op jit(solution)/shard_map/ppermute | solution.py:464
  364.4 4.4 %shard_map.571 = (f32[2,324,324]{2,1,0:T(8,128)}, f32[2,324,324]{2,1,0:T(8,128)}, f32[2,324,324]{2,1,0:T(8,128)}, f32[2,8,128]{2,1,0:T(8,128)}) custom-call(f32[2,324,324]{2,1,0:T(8,128)} %copy.168.weight, f32[2,324,324]{2,1,0:T(8,128)} %copy.185.first, f32[2,324,324]{2,1,0:T(8,128)} %copy.186.second, bf16[2,324,324]{2,1,0:T(8,128)(2,1)} %pad_maximum_fusion.6.grad), custom_call_target="tpu_custom_call" | custom-call | flops 1000000 | bytes 10000000 | tf_op jit(solution)/shard_map/pallas_call | solution.py:766
  370.6 3.7 shard_map.572
  384.3 4.2 %shard_map.570 = (f32[4,324,81]{2,1,0:T(8,128)}, f32[4,324,81]{2,1,0:T(8,128)}, f32[4,324,81]{2,1,0:T(8,128)}, f32[4,8,128]{2,1,0:T(8,128)}) custom-call(f32[4,324,81]{2,1,0:T(8,128)} %copy.205.weight, f32[4,324,81]{2,1,0:T(8,128)} %copy.177.first, f32[4,324,81]{2,1,0:T(8,128)} %copy.178.second, bf16[4,96,324]{2,1,0:T(8,128)(2,1)} %add_convert_fusion.grad), custom_call_target="tpu_custom_call" | custom-call | flops 1000000 | bytes 10000000 | tf_op jit(solution)/shard_map/pallas_call | solution.py:766
  (416 shorter events, 209.9 us)
Async XLA Ops:
  7.4 23.2 %collective-permute-start.1 = (bf16[4,96,324]{2,1,0:T(8,128)(2,1)}, bf16[4,96,324]{2,1,0:T(8,128)(2,1)}, u32[]{:S(2)}, u32[]{:S(2)}) collective-permute-start(bf16[4,96,324]{2,1,0:T(8,128)(2,1)} %get-tuple-element.284), channel_id=1, source_target_pairs={{0,2},{1,3},{2,0},{3,1},{4,6},{5,7},{6,4},{7,5},{8,10},{9,11},{10,... | collective-permute-start | bytes 746504 | tf_op jit(solution)/shard_map/ppermute | solution.py:464
  33.5 39.1 %collective-permute-start.17 = (bf16[96,324]{1,0:T(8,128)(2,1)S(1)}, bf16[96,324]{1,0:T(8,128)(2,1)S(1)}, u32[]{:S(2)}, u32[]{:S(2)}) collective-permute-start(bf16[96,324]{1,0:T(8,128)(2,1)S(1)} %copy-done.38), channel_id=1, source_target_pairs={{0,1},{1,0},{2,3},{3,2},{4,5},{5,4},{6,7},{7,6},{8,9},{9,8},{10,11... | collective-permute-start | bytes 186632 | tf_op jit(solution)/shard_map/ppermute | solution.py:464
  33.9 46.5 %collective-permute-start.21 = (bf16[324,324]{1,0:T(8,128)(2,1)S(1)}, bf16[324,324]{1,0:T(8,128)(2,1)S(1)}, u32[]{:S(2)}, u32[]{:S(2)}) collective-permute-start(bf16[324,324]{1,0:T(8,128)(2,1)S(1)} %copy-done.32), channel_id=1, source_target_pairs={{0,2},{1,3},{2,0},{3,1},{4,6},{5,7},{6,4},{7,5},{8,10},{9,11},{10,... | collective-permute-start | bytes 629864 | tf_op jit(solution)/shard_map/ppermute | solution.py:464
  37.6 45.9 %collective-permute-start.20 = (bf16[324,324]{1,0:T(8,128)(2,1)S(1)}, bf16[324,324]{1,0:T(8,128)(2,1)S(1)}, u32[]{:S(2)}, u32[]{:S(2)}) collective-permute-start(bf16[324,324]{1,0:T(8,128)(2,1)S(1)} %copy-done.32), channel_id=1, source_target_pairs={{0,1},{1,0},{2,3},{3,2},{4,5},{5,4},{6,7},{7,6},{8,9},{9,8},{10,11... | collective-permute-start | bytes 629864 | tf_op jit(solution)/shard_map/ppermute | solution.py:464
  37.6 42.8 %collective-permute-start.24 = (bf16[324,324]{1,0:T(8,128)(2,1)S(1)}, bf16[324,324]{1,0:T(8,128)(2,1)S(1)}, u32[]{:S(2)}, u32[]{:S(2)}) collective-permute-start(bf16[324,324]{1,0:T(8,128)(2,1)S(1)} %copy-done.31), channel_id=1, source_target_pairs={{0,2},{1,3},{2,0},{3,1},{4,6},{5,7},{6,4},{7,5},{8,10},{9,11},{10,... | collective-permute-start | bytes 629864 | tf_op jit(solution)/shard_map/ppermute | solution.py:464
  38.2 34.8 %collective-permute-start.19 = (bf16[96,324]{1,0:T(8,128)(2,1)S(1)}, bf16[96,324]{1,0:T(8,128)(2,1)S(1)}, u32[]{:S(2)}, u32[]{:S(2)}) collective-permute-start(bf16[96,324]{1,0:T(8,128)(2,1)S(1)} %collective-permute-done.18), channel_id=1, source_target_pairs={{0,1},{1,0},{2,3},{3,2},{4,5},{5,4},{6,7},{7,6},{8,9},{9,8},{10,11... | collective-permute-start | bytes 186632 | tf_op jit(solution)/shard_map/ppermute | solution.py:464
  148.6 106.7 %collective-permute-start.41 = (bf16[2,324,324]{2,1,0:T(8,128)(2,1)}, bf16[2,324,324]{2,1,0:T(8,128)(2,1)}, u32[]{:S(2)}, u32[]{:S(2)}) collective-permute-start(bf16[2,324,324]{2,1,0:T(8,128)(2,1)} %slice_bitcast_fusion.6), channel_id=1, source_target_pairs={{0,1},{1,0},{2,3},{3,2},{4,5},{5,4},{6,7},{7,6},{8,9},{9,8},{10,11... | collective-permute-start | bytes 1259720 | tf_op jit(solution)/shard_map/ppermute | solution.py:464
  152.1 105.3 %collective-permute-start.51 = (bf16[2,324,324]{2,1,0:T(8,128)(2,1)}, bf16[2,324,324]{2,1,0:T(8,128)(2,1)}, u32[]{:S(2)}, u32[]{:S(2)}) collective-permute-start(bf16[2,324,324]{2,1,0:T(8,128)(2,1)} %slice_bitcast_fusion.2), channel_id=1, source_target_pairs={{0,1},{1,0},{2,3},{3,2},{4,5},{5,4},{6,7},{7,6},{8,9},{9,8},{10,11... | collective-permute-start | bytes 1259720 | tf_op jit(solution)/shard_map/ppermute | solution.py:464
  155.5 63.1 %collective-permute-start.61 = (bf16[2,96,324]{2,1,0:T(8,128)(2,1)}, bf16[2,96,324]{2,1,0:T(8,128)(2,1)}, u32[]{:S(2)}, u32[]{:S(2)}) collective-permute-start(bf16[2,96,324]{2,1,0:T(8,128)(2,1)} %slice_bitcast_fusion.23), channel_id=1, source_target_pairs={{0,1},{1,0},{2,3},{3,2},{4,5},{5,4},{6,7},{7,6},{8,9},{9,8},{10,11... | collective-permute-start | bytes 373256 | tf_op jit(solution)/shard_map/ppermute | solution.py:464
  229.6 34.7 %collective-permute-start.31 = (bf16[2,4,96,324]{3,2,1,0:T(8,128)(2,1)}, bf16[2,4,96,324]{3,2,1,0:T(8,128)(2,1)S(1)}, u32[]{:S(2)}, u32[]{:S(2)}) collective-permute-start(bf16[2,4,96,324]{3,2,1,0:T(8,128)(2,1)} %slice_bitcast_fusion), channel_id=1, source_target_pairs={{0,1},{1,0},{2,3},{3,2},{4,5},{5,4},{6,7},{7,6},{8,9},{9,8},{10,11... | collective-permute-start | bytes 1493000 | tf_op jit(solution)/shard_map/ppermute | solution.py:464
  230.6 28.6 %collective-permute-start.36 = (bf16[2,324,324]{2,1,0:T(8,128)(2,1)}, bf16[2,324,324]{2,1,0:T(8,128)(2,1)}, u32[]{:S(2)}, u32[]{:S(2)}) collective-permute-start(bf16[2,324,324]{2,1,0:T(8,128)(2,1)} %slice_bitcast_fusion.8), channel_id=1, source_target_pairs={{0,1},{1,0},{2,3},{3,2},{4,5},{5,4},{6,7},{7,6},{8,9},{9,8},{10,11... | collective-permute-start | bytes 1259720 | tf_op jit(solution)/shard_map/ppermute | solution.py:464
  262.8 19.8 %collective-permute-start.47 = (bf16[1,324,324]{2,1,0:T(8,128)(2,1)S(1)}, bf16[1,324,324]{2,1,0:T(8,128)(2,1)S(1)}, u32[]{:S(2)}, u32[]{:S(2)}) collective-permute-start(bf16[1,324,324]{2,1,0:T(8,128)(2,1)S(1)} %slice_bitcast_fusion.16), channel_id=1, source_target_pairs={{0,2},{1,3},{2,0},{3,1},{4,6},{5,7},{6,4},{7,5},{8,10},{9,11},{10,... | collective-permute-start | bytes 629864 | tf_op jit(solution)/shard_map/ppermute | solution.py:464
  266.4 28.8 %collective-permute-start.32 = (bf16[1,4,96,324]{3,2,1,0:T(8,128)(2,1)}, bf16[1,4,96,324]{3,2,1,0:T(8,128)(2,1)}, u32[]{:S(2)}, u32[]{:S(2)}) collective-permute-start(bf16[1,4,96,324]{3,2,1,0:T(8,128)(2,1)} %slice_bitcast_fusion.12), channel_id=1, source_target_pairs={{0,2},{1,3},{2,0},{3,1},{4,6},{5,7},{6,4},{7,5},{8,10},{9,11},{10,... | collective-permute-start | bytes 746504 | tf_op jit(solution)/shard_map/ppermute | solution.py:464
  271.7 25.1 %collective-permute-start.43 = (bf16[324,324]{1,0:T(8,128)(2,1)S(1)}, bf16[324,324]{1,0:T(8,128)(2,1)}, u32[]{:S(2)}, u32[]{:S(2)}) collective-permute-start(bf16[324,324]{1,0:T(8,128)(2,1)S(1)} %fusion.25), channel_id=1, source_target_pairs={{0,4},{4,0},{8,12},{12,8},{16,20},{20,16},{24,28},{28,24},{1,5},{5... | collective-permute-start | bytes 629864 | tf_op jit(solution)/shard_map/ppermute | solution.py:464
  273.3 24.7 %collective-permute-start.53 = (bf16[324,324]{1,0:T(8,128)(2,1)S(1)}, bf16[324,324]{1,0:T(8,128)(2,1)}, u32[]{:S(2)}, u32[]{:S(2)}) collective-permute-start(bf16[324,324]{1,0:T(8,128)(2,1)S(1)} %fusion.27), channel_id=1, source_target_pairs={{0,4},{4,0},{8,12},{12,8},{16,20},{20,16},{24,28},{28,24},{1,5},{5... | collective-permute-start | bytes 629864 | tf_op jit(solution)/shard_map/ppermute | solution.py:464
  298.9 21.5 %collective-permute-start.54 = (bf16[324,324]{1,0:T(8,128)(2,1)S(1)}, bf16[324,324]{1,0:T(8,128)(2,1)S(1)}, u32[]{:S(2)}, u32[]{:S(2)}) collective-permute-start(bf16[324,324]{1,0:T(8,128)(2,1)S(1)} %add_convert_fusion.5), channel_id=1, source_target_pairs={{0,8},{4,12},{8,0},{12,4},{16,24},{20,28},{24,16},{28,20},{1,9},{5... | collective-permute-start | bytes 629864 | tf_op jit(solution)/shard_map/ppermute | solution.py:464
  302.0 25.7 %collective-permute-start.39 = (bf16[324,324]{1,0:T(8,128)(2,1)S(1)}, bf16[324,324]{1,0:T(8,128)(2,1)S(1)}, u32[]{:S(2)}, u32[]{:S(2)}) collective-permute-start(bf16[324,324]{1,0:T(8,128)(2,1)S(1)} %add_convert_fusion.14), channel_id=1, source_target_pairs={{0,8},{4,12},{8,0},{12,4},{16,24},{20,28},{24,16},{28,20},{1,9},{5... | collective-permute-start | bytes 629864 | tf_op jit(solution)/shard_map/ppermute | solution.py:464
  303.3 31.2 %collective-permute-start.49 = (bf16[324,324]{1,0:T(8,128)(2,1)S(1)}, bf16[324,324]{1,0:T(8,128)(2,1)S(1)}, u32[]{:S(2)}, u32[]{:S(2)}) collective-permute-start(bf16[324,324]{1,0:T(8,128)(2,1)S(1)} %add_convert_fusion.8), channel_id=1, source_target_pairs={{0,8},{4,12},{8,0},{12,4},{16,24},{20,28},{24,16},{28,20},{1,9},{5... | collective-permute-start | bytes 629864 | tf_op jit(solution)/shard_map/ppermute | solution.py:464
  305.4 33.3 %collective-permute-start.34 = (bf16[4,96,324]{2,1,0:T(8,128)(2,1)S(1)}, bf16[4,96,324]{2,1,0:T(8,128)(2,1)S(1)}, u32[]{:S(2)}, u32[]{:S(2)}) collective-permute-start(bf16[4,96,324]{2,1,0:T(8,128)(2,1)S(1)} %add_convert_fusion.2), channel_id=1, source_target_pairs={{0,8},{4,12},{8,0},{12,4},{16,24},{20,28},{24,16},{28,20},{1,9},{5... | collective-permute-start | bytes 746504 | tf_op jit(solution)/shard_map/ppermute | solution.py:464
  307.0 31.9 %collective-permute-start.45 = (bf16[324,324]{1,0:T(8,128)(2,1)S(1)}, bf16[324,324]{1,0:T(8,128)(2,1)S(1)}, u32[]{:S(2)}, u32[]{:S(2)}) collective-permute-start(bf16[324,324]{1,0:T(8,128)(2,1)S(1)} %add_convert_fusion.10), channel_id=1, source_target_pairs={{0,16},{4,20},{8,24},{12,28},{16,0},{20,4},{24,8},{28,12},{1,17},{... | collective-permute-start | bytes 629864 | tf_op jit(solution)/shard_map/ppermute | solution.py:464
  320.5 37.6 %collective-permute-start.55 = (bf16[324,324]{1,0:T(8,128)(2,1)S(1)}, bf16[324,324]{1,0:T(8,128)(2,1)S(1)}, u32[]{:S(2)}, u32[]{:S(2)}) collective-permute-start(bf16[324,324]{1,0:T(8,128)(2,1)S(1)} %add_convert_fusion.4), channel_id=1, source_target_pairs={{0,16},{4,20},{8,24},{12,28},{16,0},{20,4},{24,8},{28,12},{1,17},{... | collective-permute-start | bytes 629864 | tf_op jit(solution)/shard_map/ppermute | solution.py:464
  327.9 35.6 %collective-permute-start.40 = (bf16[324,324]{1,0:T(8,128)(2,1)S(1)}, bf16[324,324]{1,0:T(8,128)(2,1)S(1)}, u32[]{:S(2)}, u32[]{:S(2)}) collective-permute-start(bf16[324,324]{1,0:T(8,128)(2,1)S(1)} %add_convert_fusion.13), channel_id=1, source_target_pairs={{0,16},{4,20},{8,24},{12,28},{16,0},{20,4},{24,8},{28,12},{1,17},{... | collective-permute-start | bytes 629864 | tf_op jit(solution)/shard_map/ppermute | solution.py:464
  334.5 35.1 %collective-permute-start.50 = (bf16[324,324]{1,0:T(8,128)(2,1)S(1)}, bf16[324,324]{1,0:T(8,128)(2,1)S(1)}, u32[]{:S(2)}, u32[]{:S(2)}) collective-permute-start(bf16[324,324]{1,0:T(8,128)(2,1)S(1)} %add_convert_fusion.7), channel_id=1, source_target_pairs={{0,16},{4,20},{8,24},{12,28},{16,0},{20,4},{24,8},{28,12},{1,17},{... | collective-permute-start | bytes 629864 | tf_op jit(solution)/shard_map/ppermute | solution.py:464
  338.8 44.7 %collective-permute-start.35 = (bf16[4,96,324]{2,1,0:T(8,128)(2,1)S(1)}, bf16[4,96,324]{2,1,0:T(8,128)(2,1)S(1)}, u32[]{:S(2)}, u32[]{:S(2)}) collective-permute-start(bf16[4,96,324]{2,1,0:T(8,128)(2,1)S(1)} %add_convert_fusion.1), channel_id=1, source_target_pairs={{0,16},{4,20},{8,24},{12,28},{16,0},{20,4},{24,8},{28,12},{1,17},{... | collective-permute-start | bytes 746504 | tf_op jit(solution)/shard_map/ppermute | solution.py:464
  (98 other events, 690.5 us)

commit v2 on v0

v2 whole, which is shorter than its diff:
```python
import functools
import math

import jax
import jax.numpy as jnp
import numpy as np
from jax import lax
from jax.experimental import pallas as pl
from jax.experimental.pallas import tpu as pltpu
from jax.sharding import PartitionSpec as P

D = 324
HEADS = 4
KERNEL = 31
HALF = KERNEL // 2
RATES = 3
STEP = 10
SLOT = 496
HD = 81
PAD = 96
WIDE = HEADS * PAD
FF_ROWS = 336
TAIL = 2 * FF_ROWS
CONV_IN_ROWS = 2 * PAD
VECTOR_ROWS = 80
LOWER_VEC = FF_ROWS
LOWER_SPLIT = FF_ROWS + VECTOR_ROWS
LOWER_UP = LOWER_SPLIT
LOWER_CONV = LOWER_UP + FF_ROWS
LOWER_ROWS = LOWER_CONV + CONV_IN_ROWS + 16

EPS_NORM = 1e-05
BETA_ONE = 0.9
BETA_TWO = 0.999
ADAM_EPS = 1e-06
WEIGHT_DECAY = 0.01
RATE_MATRIX = 0.3
RATE_VECTOR = 0.5
MASK_FILL = -1e30
SCALE = 1.0 / math.sqrt(HD)
PRECISE = lax.Precision.HIGHEST

F32 = jnp.float32
BF16 = jnp.bfloat16
LEAD = 16
SPAN = 544


def dot_nn(left, right):
    return lax.dot_general(left, right, (((1,), (0,)), ((), ())), preferred_element_type=F32)


def dot_nt(left, right):
    return lax.dot_general(left, right, (((1,), (1,)), ((), ())), preferred_element_type=F32)


def dot_tn(left, right):
    return lax.dot_general(left, right, (((0,), (0,)), ((), ())), preferred_element_type=F32)


def sigmoid(value):
    return 0.5 * jnp.tanh(0.5 * value) + 0.5


def ln_forward(resid):
    center = resid - jnp.mean(resid, axis=-1, keepdims=True)
    inv = lax.rsqrt(jnp.mean(center * center, axis=-1, keepdims=True) + EPS_NORM)
    return center * inv, inv


def ln_backward(upstream, normal, inv, gain):
    scaled = upstream * gain
    grad = inv * (
        scaled
        - jnp.mean(scaled, axis=-1, keepdims=True)
        - normal * jnp.mean(scaled * normal, axis=-1, keepdims=True)
    )
    gain_sum = jnp.sum(upstream * normal, axis=0, keepdims=True)
    shift_sum = jnp.sum(upstream, axis=0, keepdims=True)
    return grad, gain_sum, shift_sum


def put_sums(ref, first, gain_sum, shift_sum):
    @pl.when(first)
    def _():
        ref[...] = jnp.zeros_like(ref)

    ref[0:1, :] += gain_sum
    ref[1:2, :] += shift_sum


def valid_rows(count):
    return lax.broadcasted_iota(jnp.int32, (SLOT, 1), 0) < count


def assemble(scratch, parts, rank, first, count):
    for place, part in enumerate(parts):
        scratch[place ^ rank] = part[first : first + count, 0:D]


def attn_fwd_kernel(
    rank_ref, len_ref, kind_ref, frames, table, w0, w1, w2, w3, pick, norm,
    low_out, qkv_out, prob_out, mixed_out, n1_out, s1_out, wout_out, low_rows, weights,
):
    utt = pl.program_id(0)
    rank = rank_ref[0]
    which = rank * pl.num_programs(0) + utt

    @pl.when(utt == 0)
    def _():
        assemble(weights, (w0, w1, w2, w3), rank, 0, 4 * PAD)
        turned = jnp.concatenate([weights[t, 3 * PAD :, :] for t in range(HEADS)], axis=0)
        spaced = dot_nt(pick[...], turned).astype(BF16)
        wout_out[...] = dot_nn(spaced, pick[...]).astype(BF16)
        low_rows[...] = frames[...].T

    base = low_rows[pl.ds(utt * SLOT, SLOT), :].astype(F32) + table[pl.ds(kind_ref[which], 1), :]
    base_low = base.astype(BF16)
    low_out[...] = base_low
    valid = valid_rows(len_ref[which])
    for head in range(HEADS):
        qkv = dot_nt(weights[head, 0 : 3 * PAD, :], base_low).astype(BF16)
        qkv_out[head] = qkv
        queries, keys, values = qkv[:PAD], qkv[PAD : 2 * PAD], qkv[2 * PAD :]
        scores = jnp.where(valid, dot_tn(keys, queries) * SCALE, MASK_FILL)
        top = jnp.max(scores, axis=0, keepdims=True)
        expo = jnp.exp(scores - top)
        total = jnp.sum(expo, axis=0, keepdims=True)
        probs = (expo * (1.0 / total)).astype(BF16)
        prob_out[head] = probs
        mixed_out[head * PAD : (head + 1) * PAD, :] = dot_nn(values, probs).astype(BF16)
    attn_out = dot_tn(mixed_out[...], wout_out[...])
    normal, inv = ln_forward(base + attn_out)
    n1_out[...] = normal
    s1_out[...] = inv


def shifted(scratch):
    for shift in range(1, 8):
        scratch[shift, 0 : SPAN - 8, :] = scratch[0, pl.ds(shift, SPAN - 8), :]


def load_padded(scratch, signal):
    scratch[0, 0:LEAD, :] = jnp.zeros((LEAD, WIDE), F32)
    scratch[0, pl.ds(LEAD + SLOT, SPAN - LEAD - SLOT), :] = jnp.zeros((SPAN - LEAD - SLOT, WIDE), F32)
    scratch[0, pl.ds(LEAD, SLOT), :] = signal
    shifted(scratch)


LANES = 128
BLOCKS = ((0, 128), (128, 128), (256, 128), (384, 112))


def depth_tiles(body_fn):
    for row, count in BLOCKS:
        for tile in range(WIDE // LANES):
            body_fn(row, count, slice(tile * LANES, (tile + 1) * LANES))


def depth_sum(padded, row_of, chan, put):
    def block(row, count, lanes):
        total = jnp.zeros((count // 8, 8, LANES), F32)
        for shift in range(8):
            rows = padded[shift, pl.ds(row, count + 24), lanes]
            for lift in range(4):
                place = 8 * lift + shift
                if 1 <= place <= KERNEL:
                    tap = row_of(place)
                    part = rows[8 * lift : 8 * lift + count].reshape(count // 8, 8, LANES)
                    total = total + part * chan[tap, :, lanes][None]
        put(row, count, lanes, total.reshape(count, LANES))

    depth_tiles(block)


def depth_products(padded, own, sums):
    def block(row, count, lanes):
        mine = own[pl.ds(row, count), lanes]
        for shift in range(8):
            rows = padded[shift, pl.ds(row, count + 24), lanes]
            for lift in range(4):
                place = 8 * lift + shift
                if 1 <= place <= KERNEL:
                    part = rows[8 * lift : 8 * lift + count] * mine
                    part = jnp.sum(part.reshape(count // 8, 8, LANES), axis=0)
                    sums[place - 1, :, lanes] += part

    depth_tiles(block)


def merge_stats(one, two):
    mean_one, dev_one, count_one = one[0:1], one[1:2], one[2:3]
    mean_two, dev_two, count_two = two[0:1], two[1:2], two[2:3]
    count = count_one + count_two
    mean = (mean_one * count_one + mean_two * count_two) / count
    gap = mean_one - mean_two
    dev = dev_one + dev_two + gap * gap * (count_one * count_two / count)
    return jnp.concatenate([mean, dev, count], axis=0)


def bn_parts(conv, stat, chan):
    inv = lax.rsqrt(stat[1:2, :] / stat[2:3, :] + EPS_NORM)
    normal = (conv - stat[0:1, :]) * inv
    return normal, inv, normal * chan[32, 0:1, :] + chan[33, 0:1, :]


def utt_rows(utt):
    return pl.ds(pl.multiple_of(utt * SLOT, 16), SLOT)


def each_utt(rows, body_fn):
    def step(utt, carry):
        body_fn(utt, utt_rows(utt))
        return carry

    lax.fori_loop(0, rows // SLOT, step, 0)


class Copies:
    def __init__(self, sems):
        self.sems = sems
        self.count = 0
        self.open = []

    def start(self, source, target):
        copy = pltpu.make_async_copy(source, target, self.sems.at[self.count])
        self.count += 1
        copy.start()
        return copy

    def out(self, source, target):
        self.open.append(self.start(source, target))

    def finish(self):
        for copy in self.open:
            copy.wait()


def pack_kernel(
    depth, bn, pick, attn_in, ffin_in, ffout_in, convin_in, convout_in,
    attn_out, one_out, two_out, chan_out,
    attn, ffin, ffout, convin, convout, attn_low, one, two, sems,
):
    copies = Copies(sems)
    pairs = (attn_in, attn), (ffin_in, ffin), (ffout_in, ffout), (convin_in, convin), (convout_in, convout)
    loads = [copies.start(source, target) for source, target in pairs]
    for out in (attn_low, one, two):
        out[...] = jnp.zeros_like(out)
    loads[0].wait()
    for j in range(4):
        attn_low[j * PAD : j * PAD + HD, 0:D] = attn[:, j, :].astype(BF16)
    copies.out(attn_low, attn_out)
    loads[1].wait()
    loads[2].wait()
    for j, out in ((0, one), (1, two)):
        out[0:D, 0:D] = ffin[:, j, :].astype(BF16)
        out[FF_ROWS : FF_ROWS + D, 0:D] = ffout[:, j, :].astype(BF16)
    loads[3].wait()
    loads[4].wait()
    for j in range(2):
        one[TAIL + j * PAD : TAIL + j * PAD + HD, 0:D] = convin[:, j, :].astype(BF16)
    two[TAIL : TAIL + HD, 0:D] = convout[...].astype(BF16)
    copies.out(one, one_out)
    copies.out(two, two_out)
    def spread(rows):
        return lax.dot_general(
            rows, pick[...], (((1,), (1,)), ((), ())), precision=PRECISE, preferred_element_type=F32
        )

    for first, rows in ((0, spread(depth[...])), (32, spread(bn[...]))):
        count = rows.shape[0]
        chan_out[first : first + count] = jnp.broadcast_to(rows[:, None, :], (count, 8, WIDE))
    copies.finish()


def ffn_forward(z_low, weights, hid, slope, acc, done=None):
    def block(p, carry):
        pre = dot_nn(z_low[...], weights[p, 0:D, 0:D])
        sig = sigmoid(pre)
        hidden = pre * sig
        hid_low = hidden.astype(BF16)
        hid[p] = hid_low
        slope[p] = (sig + hidden * (1.0 - sig)).astype(BF16)
        acc[...] += dot_nn(hid_low, weights[p, FF_ROWS : FF_ROWS + D, 0:D])
        return carry

    if done is None:
        lax.fori_loop(0, HEADS, block, 0)
    else:
        for p in range(HEADS):
            block(p, 0)
            done(p)


def ffn_backward(up_low, up_turn, z_turn, weights, hid, slope, acc, grads, up_row, down_row, done=None):
    def block(p, carry):
        back = dot_nt(up_low[...], weights[p, FF_ROWS : FF_ROWS + D, 0:D])
        pre_grad = (back * slope[p].astype(F32)).astype(BF16)
        grads[p, down_row : down_row + D, 0:D] = dot_nn(up_turn[...], hid[p]).astype(BF16)
        grads[p, up_row : up_row + D, 0:D] = dot_nn(z_turn[...], pre_grad).astype(BF16)
        if acc is None:
            slope[p] = pre_grad
        else:
            acc[...] += dot_nt(pre_grad, weights[p, 0:D, 0:D])
        return carry

    if done is None:
        lax.fori_loop(0, HEADS, block, 0)
    else:
        for p in range(HEADS):
            block(p, 0)
            done(p)


def send_out(copies, grads, send, keep):
    for i in range(HEADS // 2):
        copies.out(grads.at[2 * i + 1], send.at[i])
        copies.out(grads.at[2 * i], keep.at[i])


def lower_fwd_kernel(
    rank_ref, len_ref, norm, chan, n1_in, w0, w1, w2, w3,
    hid_out, slope_out, n2_out, s2_out, value_out, sig_out, conv_out, stat_out,
    n1, weights, hid, slope, n2, s2, value, sig, conv, conv_w, padded, acc, z_low, sems,
):
    copies = Copies(sems)
    rank = rank_ref[0]
    rows = n1_in.shape[0]
    loads = [copies.start(n1_in, n1)]
    loads += [copies.start(part, weights.at[p]) for p, part in enumerate((w0, w1, w2, w3))]
    for load in loads:
        load.wait()
    z = n1[...] * norm[0:1, :] + norm[4:5, :]
    acc[...] = z
    z_low[...] = z.astype(BF16)

    def done(p):
        copies.out(hid.at[p], hid_out.at[p])
        copies.out(slope.at[p], slope_out.at[p])

    ffn_forward(z_low, weights, hid, slope, acc, done)
    normal, inv = ln_forward(acc[...])
    n2[...] = normal
    s2[...] = inv
    copies.out(n2, n2_out)
    copies.out(s2, s2_out)
    z_low[...] = (normal * norm[1:2, :] + norm[5:6, :]).astype(BF16)
    for p in range(HEADS):
        conv_w[p ^ rank] = weights[p, TAIL : TAIL + CONV_IN_ROWS, 0:D]
    value[...] = dot_nt(z_low[...], conv_w[:, 0:PAD, :].reshape(WIDE, D))
    copies.out(value, value_out)
    sig[...] = sigmoid(dot_nt(z_low[...], conv_w[:, PAD:, :].reshape(WIDE, D)))
    copies.out(sig, sig_out)
    utts = rows // SLOT

    def utterance(utt, here):
        count = len_ref[rank * utts + utt]
        valid = valid_rows(count).astype(F32)
        load_padded(padded, value[here, :] * sig[here, :] * valid)

        def put(row, number, lanes, total):
            conv[pl.ds(pl.multiple_of(utt * SLOT + row, 16), number), lanes] = total

        depth_sum(padded, lambda place: place - 1, chan, put)
        own = conv[here, :]
        number = count.astype(F32)
        mean = jnp.sum(own * valid, axis=0, keepdims=True) / number
        center = (own - mean) * valid
        dev = jnp.sum(center * center, axis=0, keepdims=True)
        stat = jnp.concatenate([mean, dev, jnp.zeros_like(mean) + number], axis=0)

        @pl.when(utt == 0)
        def _():
            stat_out[...] = stat

        @pl.when(utt > 0)
        def _():
            stat_out[...] = merge_stats(stat_out[...], stat)

    each_utt(rows, utterance)
    copies.out(conv, conv_out)
    copies.finish()


def upper_kernel(
    rank_ref, len_ref, norm, chan, stat, conv_in, n2_in, cot_in, w0, w1, w2, w3,
    out_out, grad_out, b_out, send, keep, bsums, sums_three, sums_four,
    conv, n2, cot, weights, conv_w, act, hid, slope, acc, n3, s3, z_low, z_turn, up_low, up_turn,
    out, b_grad, grads, conv_acc, sems,
):
    copies = Copies(sems)
    rank = rank_ref[0]
    rows = conv_in.shape[0]
    utts = rows // SLOT
    loads = [copies.start(part, weights.at[p]) for p, part in enumerate((w0, w1, w2, w3))]
    loads += [copies.start(conv_in, conv), copies.start(n2_in, n2)]
    cot_load = copies.start(cot_in, cot)
    for load in loads:
        load.wait()
    for p in range(HEADS):
        conv_w[p ^ rank] = weights[p, TAIL : TAIL + PAD, 0:D]
    bsums[...] = jnp.zeros_like(bsums)
    sums_three[...] = jnp.zeros_like(sums_three)
    sums_four[...] = jnp.zeros_like(sums_four)
    conv_acc[...] = jnp.zeros_like(conv_acc)

    def utterance_fwd(utt, here):
        _, _, bn_out = bn_parts(conv[here, :], stat, chan)
        act_low = (bn_out * sigmoid(bn_out)).astype(BF16)
        act[here, :] = act_low
        second = n2[here, :] * norm[1:2, :] + norm[5:6, :]
        normal, inv = ln_forward(second + dot_nn(act_low, conv_w[...].reshape(WIDE, D)))
        n3[here, :] = normal
        s3[here, :] = inv
        z = normal * norm[2:3, :] + norm[6:7, :]
        acc[here, :] = z
        z_low[here, :] = z.astype(BF16)

    each_utt(rows, utterance_fwd)
    z_turn[...] = z_low[...].T
    ffn_forward(z_low, weights, hid, slope, acc)
    normal, inv = ln_forward(acc[...])
    gain = norm[3:4, :]
    out[...] = (normal * gain + norm[7:8, :]).astype(BF16).T
    copies.out(out, out_out)
    cot_load.wait()
    valid = jnp.concatenate([valid_rows(len_ref[rank * utts + u]) for u in range(utts)], axis=0)
    upstream = jnp.where(valid, cot[...].T.astype(F32), 0.0)
    grad, gain_sum, shift_sum = ln_backward(upstream, normal, inv, gain)
    sums_four[0:1, :] = gain_sum
    sums_four[1:2, :] = shift_sum
    acc[...] = grad
    up_low[...] = grad.astype(BF16)
    up_turn[...] = up_low[...].T
    ffn_backward(up_low, up_turn, z_turn, weights, hid, slope, acc, grads, 0, FF_ROWS)
    grad, gain_sum, shift_sum = ln_backward(acc[...], n3[...], s3[...], norm[2:3, :])
    sums_three[0:1, :] = gain_sum
    sums_three[1:2, :] = shift_sum
    acc[...] = grad
    copies.out(acc, grad_out)
    up_low[...] = grad.astype(BF16)

    def utterance_bwd(utt, here):
        normal, _, bn_out = bn_parts(conv[here, :], stat, chan)
        sig = sigmoid(bn_out)
        low = up_low[here, :]
        own = dot_nt(low, conv_w[...].reshape(WIDE, D)) * (sig * (1.0 + bn_out * (1.0 - sig)))
        b_grad[here, :] = own
        bsums[0:1, :] += jnp.sum(own * normal, axis=0, keepdims=True)
        bsums[1:2, :] += jnp.sum(own, axis=0, keepdims=True)
        conv_acc[...] += dot_tn(act[here, :], low)

    each_utt(rows, utterance_bwd)
    copies.out(b_grad, b_out)
    for t in range(HEADS):
        place = t ^ rank
        grads[place, TAIL : TAIL + PAD, 0:D] = conv_acc[t * PAD : (t + 1) * PAD, :].astype(BF16)
    send_out(copies, grads, send, keep)
    copies.finish()


def conv_bwd_kernel(
    rank_ref, len_ref, norm, chan, stat, bsums, pick, sums_three, sums_four,
    b_in, conv_in, value_in, sig_in, n2_in, s2_in, grad_in, w0, w1, w2, w3,
    grad_out, wgrad_out, vec_out,
    b_grad, conv, value, sig, n2, s2, grad, parts, weights, glu_pad, cg_pad, cg_ref, gg_ref,
    conv_acc, tap_sums, sums_ref, sems,
):
    copies = Copies(sems)
    rank = rank_ref[0]
    rows = b_in.shape[0]
    utts = rows // SLOT
    first = pl.ds(0, SLOT)
    pairs = [(value_in, value), (sig_in, sig), (conv_in, conv), (b_in, b_grad)]
    loads = [copies.start(source.at[first], target.at[first]) for source, target in pairs]
    others = pl.ds(SLOT, rows - SLOT)
    later = [copies.start(source.at[others], target.at[others]) for source, target in pairs]
    later += [copies.start(n2_in, n2), copies.start(s2_in, s2), copies.start(grad_in, grad)]
    later += [
        copies.start(part.at[pl.ds(TAIL, CONV_IN_ROWS)], parts.at[p])
        for p, part in enumerate((w0, w1, w2, w3))
    ]
    tap_sums[...] = jnp.zeros_like(tap_sums)
    conv_acc[...] = jnp.zeros_like(conv_acc)
    sums_ref[...] = jnp.zeros_like(sums_ref)
    for load in loads:
        load.wait()

    def utterance(utt, here):
        valid = valid_rows(len_ref[rank * utts + utt]).astype(F32)
        gain = chan[32, 0:1, :]
        count = stat[2:3, :]
        load_padded(glu_pad, value[here, :] * sig[here, :] * valid)
        normal, inv, _ = bn_parts(conv[here, :], stat, chan)
        conv_grad = (valid * inv) * (
            b_grad[here, :] * gain
            - gain * (bsums[1:2, :] / count)
            - normal * (gain * (bsums[0:1, :] / count))
        )
        cg_ref[...] = conv_grad
        load_padded(cg_pad, conv_grad)
        depth_products(glu_pad, cg_ref, tap_sums)

        def put(row, number, lanes, total):
            gg_ref[pl.ds(row, number), lanes] = total

        depth_sum(cg_pad, lambda place: KERNEL - place, chan, put)

        @pl.when(utt == 0)
        def _():
            for load in later:
                load.wait()
            for p in range(HEADS):
                weights[p ^ rank] = parts[p, :, 0:D]

        glu_grad = gg_ref[...] * valid
        sig_now = sig[here, :]
        value_grad = (glu_grad * sig_now).astype(BF16)
        gate_grad = (glu_grad * value[here, :] * sig_now * (1.0 - sig_now)).astype(BF16)
        normal = n2[here, :]
        z_low = (normal * norm[1:2, :] + norm[5:6, :]).astype(BF16)
        conv_acc[0] += dot_tn(value_grad, z_low)
        conv_acc[1] += dot_tn(gate_grad, z_low)
        upstream = (
            grad[here, :]
            + dot_nn(value_grad, weights[:, 0:PAD, :].reshape(WIDE, D))
            + dot_nn(gate_grad, weights[:, PAD:, :].reshape(WIDE, D))
        )
        own, gain_sum, shift_sum = ln_backward(upstream, normal, s2[here, :], norm[1:2, :])
        grad[here, :] = own
        sums_ref[0:1, :] += gain_sum
        sums_ref[1:2, :] += shift_sum

    each_utt(rows, utterance)
    copies.out(grad, grad_out)
    for t in range(HEADS):
        for j in range(2):
            part = conv_acc[j, t * PAD : (t + 1) * PAD, :].astype(BF16)
            wgrad_out[t ^ rank, j * PAD : (j + 1) * PAD, :] = part
    taps = jnp.sum(tap_sums[...], axis=1).astype(BF16)
    vec = [dot_nn(taps, pick[...]), jnp.zeros((1, D), F32)]
    vec += [sums_ref[0:2, :], sums_three[0:2, :], sums_four[0:2, :]]
    vec += [jnp.zeros((VECTOR_ROWS - 38, D), F32)]
    vec_out[...] = jnp.concatenate(vec, axis=0).astype(BF16)
    copies.finish()


def lower_weights_kernel(
    norm, cin_grad, vectors, up_in, n1_in, w0, w1, w2, w3, hid_in, slope_in,
    pre_out, send, keep,
    up, n1, weights, hid, slope, up_low, up_turn, z_turn, grads, sems,
):
    copies = Copies(sems)
    loads = [copies.start(up_in, up), copies.start(n1_in, n1)]
    down = pl.ds(FF_ROWS, FF_ROWS)
    loads += [
        copies.start(part.at[down], weights.at[p, down]) for p, part in enumerate((w0, w1, w2, w3))
    ]
    loads += [copies.start(slope_in, slope), copies.start(hid_in, hid)]
    for load in loads[:2]:
        load.wait()
    up_low[...] = up[...].astype(BF16)
    up_turn[...] = up_low[...].T
    z_turn[...] = (n1[...] * norm[0:1, :] + norm[4:5, :]).astype(BF16).T
    for load in loads[2:]:
        load.wait()

    def done(p):
        copies.out(slope.at[p], pre_out.at[p])

    ffn_backward(up_low, up_turn, z_turn, weights, hid, slope, None, grads, LOWER_UP, 0, done)
    for p in range(HEADS):
        grads[p, LOWER_CONV : LOWER_CONV + CONV_IN_ROWS, 0:D] = cin_grad[p]
        grads[p, LOWER_VEC : LOWER_VEC + VECTOR_ROWS, 0:D] = vectors[...]
    send_out(copies, grads, send, keep)
    copies.finish()


def lower_bwd_kernel(
    norm, up_in, n1_in, s1_in, w0, w1, w2, w3, pre_in, grad_out, sums_one,
    acc, n1, s1, weights, pre, sems,
):
    copies = Copies(sems)
    up_rows = pl.ds(0, FF_ROWS)
    loads = [copies.start(up_in, acc)]
    for p, part in enumerate((w0, w1, w2, w3)):
        loads += [copies.start(part.at[up_rows], weights.at[p]), copies.start(pre_in.at[p], pre.at[p])]
    late = [copies.start(n1_in, n1), copies.start(s1_in, s1)]
    loads[0].wait()
    for p in range(HEADS):
        loads[2 * p + 1].wait()
        loads[2 * p + 2].wait()
        acc[...] += dot_nt(pre[p], weights[p, 0:D, 0:D])
    for load in late:
        load.wait()
    grad, gain_sum, shift_sum = ln_backward(acc[...], n1[...], s1[...], norm[0:1, :])
    acc[...] = grad
    copies.out(acc, grad_out)
    sums_one[...] = jnp.zeros_like(sums_one)
    sums_one[0:1, :] = gain_sum
    sums_one[1:2, :] = shift_sum
    copies.finish()


def attn_bwd_kernel(
    rank_ref, kind_ref, low_in, w0, w1, w2, w3, wout, pick, qkv_in, probs_in, mixed, grad, sums_one,
    grad_out, send, keep, acc, acc_out, rows_out, table_sums, weights,
):
    utt = pl.program_id(0)
    rank = rank_ref[0]

    @pl.when(utt == 0)
    def _():
        assemble(weights, (w0, w1, w2, w3), rank, 0, 3 * PAD)
        acc[...] = jnp.zeros_like(acc)
        acc_out[...] = jnp.zeros_like(acc_out)
        table_sums[...] = jnp.zeros_like(table_sums)

    base_low = low_in[...]
    upstream = grad[...]
    up_low = upstream.astype(BF16)
    acc_out[...] += dot_nn(mixed[...], up_low)
    mixed_grad = dot_nt(wout[...], up_low).astype(BF16)
    total = upstream
    for head in range(HEADS):
        queries = qkv_in[head, 0:PAD, :]
        keys = qkv_in[head, PAD : 2 * PAD, :]
        values = qkv_in[head, 2 * PAD :, :]
        up_head = mixed_grad[head * PAD : (head + 1) * PAD, :]
        probs_low = probs_in[head]
        probs = probs_low.astype(F32)
        prob_grad = dot_tn(values, up_head)
        delta = jnp.sum(prob_grad * probs, axis=0, keepdims=True)
        score_grad = (probs * (prob_grad - delta)).astype(BF16)
        query_grad = (dot_nn(keys, score_grad) * SCALE).astype(BF16)
        key_grad = (dot_nt(queries, score_grad) * SCALE).astype(BF16)
        value_grad = dot_nt(up_head, probs_low).astype(BF16)
        grads = jnp.concatenate([query_grad, key_grad, value_grad], axis=0)
        acc[head] += dot_nn(grads, base_low)
        total = total + dot_tn(grads, weights[head])
    rows_out[pl.ds(utt * SLOT, SLOT), :] = total
    column = jnp.sum(total, axis=0, keepdims=True)
    kind = kind_ref[rank * pl.num_programs(0) + utt]
    place = lax.broadcasted_iota(jnp.int32, table_sums.shape, 0)
    table_sums[...] += jnp.where(place == kind, column, 0.0)

    @pl.when(utt == pl.num_programs(0) - 1)
    def _():
        grad_out[...] = rows_out[...].T
        turned = dot_nt(pick[...], acc_out[...].astype(BF16)).astype(BF16)
        turned = dot_nn(turned, pick[...]).astype(BF16)
        extra = [table_sums[0:RATES, :], sums_one[0:2, :]]
        extra += [jnp.zeros((PAD - HD - RATES - 2, D), F32)]
        extra = jnp.concatenate(extra, axis=0).astype(BF16)
        rows_out[0:WIDE, :] = turned.astype(F32)
        for place in range(HEADS):
            t = place ^ rank
            out = send if place % 2 else keep
            out[place // 2, 0 : 3 * PAD, 0:D] = acc[t].astype(BF16)
            out[place // 2, HD:PAD, 0:D] = extra
            block = rows_out[pl.ds(pl.multiple_of(t * PAD, PAD), PAD), :]
            out[place // 2, 3 * PAD :, 0:D] = block.astype(BF16)


def adam_step(first, second, grad_full):
    first_new = BETA_ONE * first + (1.0 - BETA_ONE) * grad_full
    second_new = BETA_TWO * second + (1.0 - BETA_TWO) * grad_full * grad_full
    scaled = jnp.maximum(second_new * (1.0 / (1.0 - BETA_TWO**STEP)), 1e-30)
    below = scaled * lax.rsqrt(scaled) + ADAM_EPS
    inverse = pl.reciprocal(below, approx=True)
    inverse = inverse * (2.0 - below * inverse)
    direction = (first_new * (1.0 / (1.0 - BETA_ONE**STEP))) * inverse
    return (first_new, second_new, direction)


def total_of(array):
    return jnp.sum(jnp.sum(array, axis=1, keepdims=True), axis=0, keepdims=True)


def put_squares(sums_out, row, own, direction):
    if own.ndim == 3:
        own = jnp.sum(own * own, axis=0)
        direction = jnp.sum(direction * direction, axis=0)
        count = own.shape[0]
    else:
        own = jnp.sum(own * own, axis=0, keepdims=True)
        direction = jnp.sum(direction * direction, axis=0, keepdims=True)
        count = 1
    sums_out[row : row + count, :] = jnp.broadcast_to(
        jnp.sum(own, axis=1, keepdims=True), (count, 128)
    )
    sums_out[16 + row : 16 + row + count, :] = jnp.broadcast_to(
        jnp.sum(direction, axis=1, keepdims=True), (count, 128)
    )


def join_halves(spot, mine, other, scratch):
    half = mine.shape[0]
    scratch[pl.ds(pl.multiple_of(spot * half, 16), half), :] = mine[...].astype(F32)
    scratch[pl.ds(pl.multiple_of((1 - spot) * half, 16), half), :] = other[...].astype(F32)


def lamb_stack(weight, first, second, grads, stacked, sums_out, row):
    for j, grad in enumerate(grads):
        stacked[:, j, :] = grad
    own = weight[...]
    first_new, second_new, direction = adam_step(first[...], second[...], stacked[...])
    direction = direction + WEIGHT_DECAY * own
    put_squares(sums_out, row, own, direction)
    return first_new, second_new, direction


def lamb_down_kernel(
    spot_ref, one_mine, one_other, two_mine, two_other, fout_w, fout_m, fout_v, cout_w, cout_m, cout_v,
    fout_mo, fout_vo, fout_u, cout_mo, cout_vo, cout_u, fin_grad, vec_out, sums_out, one, two, wide,
):
    spot = spot_ref[0]
    join_halves(spot, one_mine, one_other, one)
    join_halves(spot, two_mine, two_other, two)
    sums_out[...] = jnp.zeros_like(sums_out)
    fin_grad[...] = one[0:D, 0:D]
    vec_out[...] = two[FF_ROWS : FF_ROWS + VECTOR_ROWS, 0:D]
    grads = (two[0:D, 0:D].T, one[FF_ROWS : FF_ROWS + D, 0:D].T)
    fout_mo[...], fout_vo[...], fout_u[...] = lamb_stack(
        fout_w, fout_m, fout_v, grads, wide, sums_out, 6
    )
    own = cout_w[...]
    grad = one[TAIL : TAIL + HD, 0:D]
    first_new, second_new, direction = adam_step(cout_m[...], cout_v[...], grad)
    direction = direction + WEIGHT_DECAY * own
    cout_mo[...], cout_vo[...], cout_u[...] = first_new, second_new, direction
    put_squares(sums_out, 10, own, direction)


def lamb_up_kernel(
    spot_ref, mine, other, fin_grad, fin_w, fin_m, fin_v, cin_w, cin_m, cin_v,
    fin_mo, fin_vo, fin_u, cin_mo, cin_vo, cin_u, sums_out, full, wide, narrow,
):
    join_halves(spot_ref[0], mine, other, full)
    sums_out[...] = jnp.zeros_like(sums_out)
    grads = (full[0:D, 0:D], fin_grad[...])
    fin_mo[...], fin_vo[...], fin_u[...] = lamb_stack(fin_w, fin_m, fin_v, grads, wide, sums_out, 4)
    grads = [full[FF_ROWS + j * PAD : FF_ROWS + j * PAD + HD, 0:D] for j in range(2)]
    cin_mo[...], cin_vo[...], cin_u[...] = lamb_stack(
        cin_w, cin_m, cin_v, grads, narrow, sums_out, 8
    )


def lamb_attn_kernel(
    share, spot_ref, mine, other, vec, bsums, pick, attn_w, attn_m, attn_v, depth_w, depth_m, depth_v,
    norm_w, norm_m, norm_v, bn_w, bn_m, bn_v, table_w, table_m, table_v,
    attn_mo, attn_vo, out_vo, attn_u, depth_wo, depth_mo, depth_vo, norm_wo, norm_mo, norm_vo,
    bn_wo, bn_mo, bn_vo, table_wo, table_mo, table_vo, sums_out, full, stacked,
):
    join_halves(spot_ref[0], mine, other, full)
    sums_out[...] = jnp.zeros_like(sums_out)
    grads = [full[j * PAD : j * PAD + HD, 0:D] for j in range(4)]
    first_new, second_new, direction = lamb_stack(
        attn_w, attn_m, attn_v, grads, stacked, sums_out, 0
    )
    attn_mo[...] = first_new
    attn_u[...] = direction
    for j in range(3):
        attn_vo[j] = second_new[:, j, :]
    out_vo[...] = second_new[:, 3, :]

    own = depth_w[...]
    depth_mo[...], depth_vo[...], direction = adam_step(depth_m[...], depth_v[...], vec[0:KERNEL, :])
    direction = direction + WEIGHT_DECAY * own
    own_norm = jnp.sqrt(total_of(own * own))
    step_norm = jnp.sqrt(total_of(direction * direction))
    depth_wo[...] = own - RATE_MATRIX * (own_norm / step_norm) * direction
    put_squares(sums_out, 11, own, direction)
    for row in (11, 27):
        sums_out[row : row + 1, :] = sums_out[row : row + 1, :] * share

    def vector(weight, first, second, grad, w_out, m_out, v_out):
        m_out[...], v_out[...], move = adam_step(first[...], second[...], grad)
        w_out[...] = weight[...] - RATE_VECTOR * move

    one = full[HD + RATES : HD + RATES + 2, 0:D]
    rows = [one[0:1]] + [vec[32 + 2 * i : 33 + 2 * i, :] for i in range(3)]
    rows += [one[1:2]] + [vec[33 + 2 * i : 34 + 2 * i, :] for i in range(3)]
    vector(norm_w, norm_m, norm_v, jnp.concatenate(rows, axis=0), norm_wo, norm_mo, norm_vo)
    bn_grad = lax.dot_general(
        bsums[...], pick[...], (((1,), (0,)), ((), ())), precision=PRECISE,
        preferred_element_type=F32,
    )
    vector(bn_w, bn_m, bn_v, bn_grad, bn_wo, bn_mo, bn_vo)
    table_grad = full[HD : HD + RATES, 0:D]
    vector(table_w, table_m, table_v, table_grad, table_wo, table_mo, table_vo)


def step_kernel(sums, *refs):
    weights, moves_in, outs, norm_outs = refs[:5], refs[5:10], refs[10:15], refs[15:17]
    moves, sems = refs[17:22], refs[22]
    copies = Copies(sems)
    loads = [copies.start(moves_in[i], moves[i]) for i in range(5)]
    norms = jnp.sqrt(sums[...])
    factor = RATE_MATRIX * (norms[0:16] / jnp.maximum(norms[16:32], 1e-37))
    shape = (16, 128)
    diagonal = lax.broadcasted_iota(jnp.int32, shape, 0) == lax.broadcasted_iota(jnp.int32, shape, 1)
    for i, out in enumerate(norm_outs):
        across = jnp.where(diagonal, norms[16 * i : 16 * i + 16], 0.0)
        out[...] = jnp.sum(across, axis=0, keepdims=True)[:, 0:12]
    for i, row in enumerate((4, 6, 0, 8, 10)):
        weight, move = weights[i], moves[i]
        stacked = len(weight.shape) == 3
        number = weight.shape[1] if stacked else 1
        loads[i].wait()
        scale = factor[row : row + number, 0:1]
        move[...] = weight[...] - (scale[None] if stacked else scale) * move[...]
        copies.out(move, outs[i])
    copies.finish()


SMEM = pl.BlockSpec(memory_space=pltpu.SMEM)


def whole(shape):
    return pl.BlockSpec(shape, lambda *_: (0,) * len(shape))


def lead(shape, rest, place=None):
    def index(i):
        return ((i if place is None else place(i)),) + (0,) * rest

    return pl.BlockSpec(shape, index)


def placed(entries, pinned):
    return [
        pltpu.HBM(*entry) if place in pinned else jax.ShapeDtypeStruct(*entry)
        for place, entry in enumerate(entries)
    ]


def call(kernel, grid, in_specs, out_specs, out_shape, scratch=(), cost=1_000_000, limit=40, pinned=()):
    return pl.pallas_call(
        kernel,
        grid=(grid,),
        in_specs=in_specs,
        out_specs=out_specs,
        out_shape=placed(out_shape, pinned),
        scratch_shapes=list(scratch),
        cost_estimate=pl.CostEstimate(flops=cost, bytes_accessed=10_000_000, transcendentals=0),
        compiler_params=pltpu.CompilerParams(vmem_limit_bytes=limit * 1024 * 1024),
    )


def call_whole(kernel, scalars, arrays, out_shape, scratch=(), limit=14):
    return pl.pallas_call(
        kernel,
        in_specs=[SMEM] * len(scalars) + [pl.BlockSpec(memory_space=pltpu.VMEM)] * len(arrays),
        out_specs=[pl.BlockSpec(memory_space=pltpu.VMEM)] * len(out_shape),
        out_shape=[jax.ShapeDtypeStruct(*entry) for entry in out_shape],
        scratch_shapes=list(scratch),
        cost_estimate=pl.CostEstimate(flops=1_000_000, bytes_accessed=2_000_000, transcendentals=0),
        compiler_params=pltpu.CompilerParams(vmem_limit_bytes=limit * 1024 * 1024),
    )(*scalars, *arrays)


ANY = pl.BlockSpec(memory_space=pl.ANY)
VMEM = pl.BlockSpec(memory_space=pltpu.VMEM)


def call_mixed(kernel, scalars, small, large, large_out, small_out, scratch, copies, cost, limit=56, pinned=()):
    return pl.pallas_call(
        kernel,
        in_specs=[SMEM] * len(scalars) + [VMEM] * len(small) + [ANY] * len(large),
        out_specs=[ANY] * len(large_out) + [VMEM] * len(small_out),
        out_shape=placed(large_out + small_out, pinned),
        scratch_shapes=[pltpu.VMEM(*entry) for entry in scratch] + [pltpu.SemaphoreType.DMA((copies,))],
        cost_estimate=pl.CostEstimate(flops=cost, bytes_accessed=10_000_000, transcendentals=0),
        compiler_params=pltpu.CompilerParams(vmem_limit_bytes=limit * 1024 * 1024),
    )(*scalars, *small, *large)


def swap(value, axis, bit):
    size = lax.axis_size(axis)
    return lax.ppermute(value, axis, [(i, i ^ bit) for i in range(size)])


def combine_all(value, merge, pause=None):
    for bit in bits_of("tensor"):
        value = merge(value, swap(value, "tensor", bit))
    if pause is not None:
        value = pause(value)
    for bit in bits_of("dp"):
        value = merge(value, swap(value, "dp", bit))
    return value


def bits_of(axis):
    size = lax.axis_size(axis)
    assert size & (size - 1) == 0
    return [1 << i for i in range(size.bit_length() - 1)]


def tie(*values):
    return lax.optimization_barrier(values)


def gather_tensor(shard):
    return gather_near(gather_far(shard))


def gather_far(shard):
    return shard, swap(shard, "tensor", 2)


def gather_near(parts):
    blocks = [parts[0], swap(parts[0], "tensor", 1), parts[1], swap(parts[1], "tensor", 1)]
    return [pltpu.with_memory_space_constraint(block, pltpu.HBM) for block in blocks]


def add_low(one, two):
    return (one.astype(F32) + two.astype(F32)).astype(BF16)


def dp_steps(mine, got, first=0, count=None):
    spot = lax.axis_index("dp") & 1
    half = (mine.shape[0] if count is None else count) // 2

    def cut(array, place):
        return lax.dynamic_slice_in_dim(array, first + place * half, half, 0)

    kept = add_low(cut(mine, spot), cut(got, spot))
    got = yield swap(add_low(cut(mine, 1 - spot), cut(got, 1 - spot)), "dp", 1)
    kept = add_low(kept, got)
    for bit in bits_of("dp")[1:]:
        got = yield swap(kept, "dp", bit)
        kept = add_low(kept, got)
    got = yield swap(kept, "dp", 1)
    return kept, got


def tensor_steps(send, keep):
    got = yield swap(send, "tensor", 1)
    mine = add_low(keep[0], got[0])
    got = yield swap(add_low(keep[1], got[1]), "tensor", 2)
    return mine, got


def reduce_steps(send, keep):
    mine, got = yield from tensor_steps(send, keep)
    return (yield from dp_steps(mine, got))


class Reduction:
    def __init__(self, steps):
        self.steps = steps
        self.flight = next(steps)
        self.result = None

    def advance(self, value):
        value, got = tie(value, self.flight)
        self.send(got)
        return value

    def send(self, got):
        try:
            self.flight = self.steps.send(got)
        except StopIteration as end:
            self.result = end.value

    def finish(self):
        while self.result is None:
            self.send(self.flight)
        return self.result


def pick_matrix():
    pick = np.zeros((WIDE, D), np.float32)
    for column in range(D):
        pick[column // HD * PAD + column % HD, column] = 1.0
    return pick


def body(
    frames, cotangent, lengths, rate_kind, attn_w, attn_m, attn_v, ffin_w, ffin_m, ffin_v,
    ffout_w, ffout_m, ffout_v, convin_w, convin_m, convin_v, convout_w, convout_m, convout_v,
    depth_w, depth_m, depth_v, norm_w, norm_m, norm_v, bn_w, bn_m, bn_v, table_w, table_m, table_v,
):
    rank = lax.axis_index("tensor")
    rank_one = rank.reshape(1).astype(jnp.int32)
    spot_one = (lax.axis_index("dp") & 1).reshape(1).astype(jnp.int32)
    rows = frames.shape[0]
    utts = rows // SLOT
    groups = lax.axis_size("tensor")
    hid = ffin_w.shape[2]
    pick = jnp.asarray(pick_matrix(), BF16)
    pick_wide = jnp.asarray(pick_matrix(), F32)

    attn_w, attn_m, attn_v = (jnp.transpose(a, (2, 0, 1)) for a in (attn_w, attn_m, attn_v))
    ffin_w, ffin_m, ffin_v = (jnp.transpose(a, (1, 0, 2)) for a in (ffin_w, ffin_m, ffin_v))
    ffout_w, ffout_m, ffout_v = (jnp.transpose(a, (1, 0, 2)) for a in (ffout_w, ffout_m, ffout_v))
    convin_w, convin_m, convin_v = (jnp.transpose(a, (2, 0, 1)) for a in (convin_w, convin_m, convin_v))

    pack_one_rows = TAIL + CONV_IN_ROWS
    pack_two_rows = TAIL + PAD
    shards = (attn_w, ffin_w, ffout_w, convin_w, convout_w)
    packs = [((count, WIDE), BF16) for count in (4 * PAD, pack_one_rows, pack_two_rows)]
    attn_low, pack_one, pack_two, chan = call_mixed(
        pack_kernel,
        (),
        (depth_w, bn_w, pick_wide),
        shards,
        packs,
        [((34, 8, WIDE), F32)],
        [(shard.shape, F32) for shard in shards] + packs,
        8,
        4_000_000_000,
    )
    attn_parts = gather_tensor(attn_low)
    attn_parts[2], pack_one = tie(attn_parts[2], pack_one)
    one_pair = gather_far(pack_one)

    rowspec = lead((SLOT, D), 1)
    chanspec = lead((SLOT, WIDE), 1)
    onespec = lead((SLOT, 1), 1)
    normspec = whole((8, D))
    allspec = whole((rows, D))
    turnspec = whole((D, rows))
    statspec = whole((3, WIDE))
    attn_specs = [whole((4 * PAD, WIDE))] * groups
    qkvspec = pl.BlockSpec((None, HEADS, 3 * PAD, SLOT), lambda i: (i, 0, 0, 0))
    mixspec = pl.BlockSpec((None, WIDE, SLOT), lambda i: (i, 0, 0))
    probspec = pl.BlockSpec((None, HEADS, SLOT, SLOT), lambda i: (i, 0, 0, 0))
    row_f32 = ((rows, D), F32)
    one_f32 = ((rows, 1), F32)
    sums_f32 = ((8, D), F32)
    base_low, qkv, probs, mixed, n1, s1, wout = call(
        attn_fwd_kernel,
        utts,
        [SMEM, SMEM, SMEM, turnspec, whole((RATES, D))] + attn_specs + [whole((WIDE, D)), normspec],
        [rowspec, qkvspec, probspec, mixspec, rowspec, onespec, whole((WIDE, D))],
        [
            ((rows, D), BF16),
            ((utts, HEADS, 3 * PAD, SLOT), BF16),
            ((utts, HEADS, SLOT, SLOT), BF16),
            ((utts, WIDE, SLOT), BF16),
            row_f32,
            one_f32,
            ((WIDE, D), BF16),
        ],
        [pltpu.VMEM((rows, D), BF16), pltpu.VMEM((HEADS, 4 * PAD, D), BF16)],
        cost=10_000_000_000,
        limit=56,
        pinned=range(6),
    )(rank_one, lengths, rate_kind, frames.T, table_w, *attn_parts, pick, norm_w)

    row_low = ((rows, D), BF16)
    turn_low = ((D, rows), BF16)
    hid_low = ((groups, rows, hid), BF16)
    chan_f32 = ((rows, WIDE), F32)
    one_rows = (groups, pack_one_rows, WIDE)
    two_rows = (groups, pack_two_rows, WIDE)
    conv_pad = ((8, SPAN, WIDE), F32)
    far, pack_two, n1 = tie(one_pair[1], pack_two, n1)
    one_parts = gather_near((one_pair[0], far))
    two_pair = gather_far(pack_two)
    hid_one, slope_one, n2, s2, value_pre, gate_sig, conv, stat = call_mixed(
        lower_fwd_kernel,
        (rank_one, lengths),
        (norm_w, chan),
        (n1, *one_parts),
        [hid_low, hid_low, row_f32, one_f32, chan_f32, chan_f32, chan_f32],
        [((3, WIDE), F32)],
        [
            row_f32, (one_rows, BF16), hid_low, hid_low, row_f32, one_f32, chan_f32, chan_f32, chan_f32,
            ((HEADS, CONV_IN_ROWS, D), BF16), conv_pad, row_f32, row_low,
        ],
        20,
        18_000_000_000,
        pinned=(2, 3),
    )

    far, stat = tie(two_pair[1], stat)
    two_parts = gather_near((two_pair[0], far))
    stat = combine_all(stat, merge_stats)

    out, grad_three, b_grad, send_one, keep_one, bsums, sums_three, sums_four = call_mixed(
        upper_kernel,
        (rank_one, lengths),
        (norm_w, chan, stat),
        (conv, n2, cotangent.T, *two_parts),
        [turn_low, row_f32, chan_f32] + [((groups // 2, pack_two_rows, WIDE), BF16)] * 2,
        [((8, WIDE), F32), sums_f32, sums_f32],
        [
            chan_f32, row_f32, turn_low, (two_rows, BF16), ((HEADS, PAD, D), BF16),
            ((rows, WIDE), BF16), hid_low, hid_low, row_f32, row_f32, one_f32, row_low, turn_low,
            row_low, turn_low, turn_low, chan_f32, (two_rows, BF16), ((WIDE, D), F32),
        ],
        16,
        30_000_000_000,
    )
    reduce_one = Reduction(reduce_steps(send_one, keep_one))
    bsums = bsums[:2]
    bsums = combine_all(bsums, jnp.add, reduce_one.advance)

    convin_block = (HEADS, CONV_IN_ROWS, D)
    grad_two, cin_grad, vectors = call_mixed(
        conv_bwd_kernel,
        (rank_one, lengths),
        (norm_w, chan, stat, bsums, pick, sums_three, sums_four),
        (b_grad, conv, value_pre, gate_sig, n2, s2, grad_three, *one_parts),
        [row_f32],
        [(convin_block, BF16), ((VECTOR_ROWS, D), BF16)],
        [
            chan_f32, chan_f32, chan_f32, chan_f32, row_f32, one_f32, row_f32,
            ((HEADS, CONV_IN_ROWS, WIDE), BF16), (convin_block, BF16), conv_pad, conv_pad,
            ((SLOT, WIDE), F32), ((SLOT, WIDE), F32), ((2, WIDE, D), F32), ((KERNEL, 8, WIDE), F32),
            sums_f32,
        ],
        16,
        14_000_000_000,
        pinned=(0,),
    )
    grad_two = reduce_one.advance(grad_two)

    lower_rows = (groups, LOWER_ROWS, WIDE)
    pre_one, send_two, keep_two = call_mixed(
        lower_weights_kernel,
        (),
        (norm_w, cin_grad, vectors),
        (grad_two, n1, *one_parts, hid_one, slope_one),
        [hid_low] + [((groups // 2, LOWER_ROWS, WIDE), BF16)] * 2,
        [],
        [
            row_f32, row_f32, ((groups, TAIL, WIDE), BF16), hid_low, hid_low, row_low, turn_low,
            turn_low, (lower_rows, BF16),
        ],
        16,
        12_000_000_000,
    )
    reduce_two = Reduction(tensor_steps(send_two, keep_two))
    pre_one = reduce_one.advance(pre_one)
    grad_one, sums_one = call_mixed(
        lower_bwd_kernel,
        (),
        (norm_w,),
        (grad_two, n1, s1, *one_parts, pre_one),
        [row_f32],
        [sums_f32],
        [row_f32, row_f32, one_f32, ((groups, FF_ROWS, WIDE), BF16), hid_low],
        12,
        8_000_000_000,
    )
    grad_one = reduce_one.advance(grad_one)
    grad_one = reduce_two.advance(grad_one)
    in_grad, attn_send, attn_keep = call(
        attn_bwd_kernel,
        utts,
        [SMEM, SMEM, rowspec] + attn_specs + [whole((WIDE, D)), whole((WIDE, D))]
        + [qkvspec, probspec, mixspec, rowspec, whole((8, D))],
        [turnspec, whole((2, 4 * PAD, WIDE)), whole((2, 4 * PAD, WIDE))],
        [((D, rows), F32)] + [((2, 4 * PAD, WIDE), BF16)] * 2,
        [
            pltpu.VMEM((HEADS, 3 * PAD, D), F32),
            pltpu.VMEM((WIDE, D), F32),
            pltpu.VMEM((rows, D), F32),
            pltpu.VMEM((8, D), F32),
            pltpu.VMEM((HEADS, 3 * PAD, D), BF16),
        ],
        cost=16_000_000_000,
    )(
        rank_one, rate_kind, base_low, *attn_parts, wout, pick, qkv, probs, mixed, grad_one, sums_one,
    )
    attn_send = reduce_one.advance(attn_send)
    attn_send = reduce_two.advance(attn_send)
    reduce_attn = Reduction(reduce_steps(attn_send, attn_keep))
    mine, got = reduce_two.result
    reduce_down = Reduction(dp_steps(mine, got, 0, LOWER_SPLIT))
    reduce_up = Reduction(dp_steps(mine, got, LOWER_SPLIT, LOWER_ROWS - LOWER_SPLIT))
    token = bsums
    chains = (reduce_attn, reduce_down, reduce_up, reduce_down, reduce_attn, reduce_up, reduce_attn)
    for chain in chains + (reduce_one, reduce_down, reduce_attn, reduce_up, reduce_down):
        token = chain.advance(token)
    one_halves = reduce_one.finish()
    down_halves = reduce_down.finish()

    def like(*arrays):
        return [(a.shape, F32) for a in arrays]

    down = call_whole(
        lamb_down_kernel,
        (spot_one,),
        (*one_halves, *down_halves, ffout_w, ffout_m, ffout_v, convout_w, convout_m, convout_v),
        like(*[ffout_w] * 3, *[convout_w] * 3)
        + [((D, D), F32), ((VECTOR_ROWS, D), F32), ((32, 128), F32)],
        [
            pltpu.VMEM((pack_two_rows, WIDE), F32),
            pltpu.VMEM((LOWER_SPLIT, WIDE), F32),
            pltpu.VMEM(ffout_w.shape, F32),
        ],
    )
    token = reduce_attn.advance(tie(token, down[8])[0])
    token = reduce_up.advance(token)
    up_halves = reduce_up.finish()
    while reduce_attn.result is None:
        token = reduce_attn.advance(token)
    up = call_whole(
        lamb_up_kernel,
        (spot_one,),
        (*up_halves, down[6], ffin_w, ffin_m, ffin_v, convin_w, convin_m, convin_v),
        like(*[ffin_w] * 3, *[convin_w] * 3) + [((32, 128), F32)],
        [
            pltpu.VMEM((LOWER_ROWS - LOWER_SPLIT, WIDE), F32),
            pltpu.VMEM(ffin_w.shape, F32),
            pltpu.VMEM(convin_w.shape, F32),
        ],
    )
    attn_halves = reduce_attn.result
    small = (depth_w, depth_m, depth_v, norm_w, norm_m, norm_v, bn_w, bn_m, bn_v, table_w, table_m, table_v)
    last = call_whole(
        functools.partial(lamb_attn_kernel, 1.0 / groups),
        (spot_one,),
        (*attn_halves, down[7], bsums, pick_wide, attn_w, attn_m, attn_v) + small,
        like(attn_w) + [((3, HD, D), F32), ((HD, D), F32)] + like(attn_w, *small) + [((32, 128), F32)],
        [pltpu.VMEM((4 * PAD, WIDE), F32), pltpu.VMEM(attn_w.shape, F32)],
    )
    squares = down[8] + up[6] + last[16]
    for bit in bits_of("tensor"):
        squares = squares + swap(squares, "tensor", bit)
    matrices = (ffin_w, ffout_w, attn_w, convin_w, convout_w)
    moves = (up[2], down[2], last[3], up[5], down[5])
    ffin_new, ffout_new, attn_new, convin_new, convout_new, weight_norms, update_norms = call_mixed(
        step_kernel,
        (),
        (squares, *matrices),
        moves,
        like(*matrices),
        [((1, 12), F32)] * 2,
        like(*matrices),
        10,
        1_000_000,
        limit=14,
    )

    def back_chan(array):
        return jnp.transpose(array, (1, 2, 0))

    def back_mid(array):
        return jnp.transpose(array, (1, 0, 2))

    small_new = last[4:16]
    return (
        out.T,
        in_grad.T,
        back_chan(attn_new),
        back_chan(last[0]),
        jnp.transpose(last[1], (0, 2, 1)),
        last[2].T,
        back_mid(ffin_new),
        back_mid(up[0]),
        back_mid(up[1]),
        back_mid(ffout_new),
        back_mid(down[0]),
        back_mid(down[1]),
        back_chan(convin_new),
        back_chan(up[3]),
        back_chan(up[4]),
        convout_new,
        down[3],
        down[4],
        *small_new,
        weight_norms.reshape(12),
        update_norms.reshape(12),
    )


def solution(mesh):
    rows = P(("dp", "tensor"), None)
    last = P(None, None, "tensor")
    mid = P(None, "tensor", None)
    first = P("tensor", None)
    placed = (rows, rows, P("dp"), P("dp")) + (last,) * 6 + (mid,) * 3 + (last,) * 3 + (first,) * 3
    results = (rows, rows) + (last,) * 3 + (P(None, "tensor"),) + (last,) * 3 + (mid,) * 3
    return jax.shard_map(
        body,
        mesh=mesh,
        in_specs=placed + (P(),) * 12,
        out_specs=results + (last,) * 3 + (first,) * 3 + (P(),) * 14,
        check_vma=False,
    )
```

time: 1130 us -> 259 us (0.23)
  waiting for transfers between devices: 444 us -> 65.6 us
  local copies, waits for them, and re-layouts: 208 us -> 3.56 us
  blocking collectives: 184 us -> 0 us
  other arithmetic: 163 us -> 8.17 us
  Pallas kernels: 0 us -> 131 us
  matrix products: 95.2 us -> 0 us
  starting transfers between devices: 1.74 us -> 44.2 us
  between operations: 19.3 us -> 2 us
    unnamed x21 -> x0, waiting for transfers between devices: 239 us -> none
    psum x5 -> x0, blocking collectives: 172 us -> none  [the longest x1 41.4 us: body(): lax.psum(widen(jnp.sum(center * center * group_weight, axis=0)), ('dp', '...]
    all_gather x6 -> x0, waiting for transfers between devices: 150 us -> none  [the longest x3 78.1 us: spread_grads(): return lax.all_gather(grads_low, 'tensor', axis=0, tiled=True)]
    pallas_call x0 -> x12, Pallas kernels: none -> 131 us  [the longest x7 91.4 us: call_mixed(): pl.pallas_call(kernel, in_specs=[SMEM] * len(scalars) + [VMEM] * len(smal...]
    unnamed x426 -> x98, local copies, waits for them, and re-layouts: 112 us -> 2.85 us
    reduce_sum x29 -> x0, other arithmetic: 103 us -> none  [the longest x1 32 us: body(): sum_local = widen(jnp.sum(conv_out * group_weight, axis=0))]
    dot_general x35 -> x0, matrix products: 95.2 us -> none  [the longest x8 26.9 us: product_nt(): lax.dot_general(left_side, right_side, (((1,), (1,)), ((), ())), preferre...]
    ppermute x0 -> x43, waiting for transfers between devices: none -> 65.6 us  [swap(): return lax.ppermute(value, axis, [(i, i ^ bit) for i in range(size)])]
  transfers between devices with their start and end apart: 14 -> 43, of which waited for: 14 -> 22; matrix products, arithmetic and copies ran while one was open for 5% -> 3% of each run, Pallas kernels for 0% -> 36%
where the time goes in v2:
time: 259 us; the launch traced here: 255 us
  Pallas kernels  131 us (51%)
  waiting for transfers between devices  65.6 us (25%)
  starting transfers between devices  44.2 us (17%)
  other arithmetic  8.17 us (3%)
  local copies, waits for them, and re-layouts  3.56 us (1%)
    pallas_call x7, Pallas kernels, call_mixed(): pl.pallas_call(kernel, in_specs=[SMEM] * len(scalars) + [VMEM] * len(smal...  91.4 us
    ppermute x43, waiting for transfers between devices, swap(): return lax.ppermute(value, axis, [(i, i ^ bit) for i in range(size)])  65.6 us
    ppermute x43, starting transfers between devices, swap(): return lax.ppermute(value, axis, [(i, i ^ bit) for i in range(size)])  44.2 us
    pallas_call x1, Pallas kernels, body(): call(attn_bwd_kernel, utts, [SMEM, SMEM, rowspec] + attn_specs + [whole((...  14.6 us
    pallas_call x1, Pallas kernels, body(): call(attn_fwd_kernel, utts, [SMEM, SMEM, SMEM, turnspec, whole((RATES, D)...  12.9 us
    pallas_call x3, Pallas kernels, call_whole(): pl.pallas_call(kernel, in_specs=[SMEM] * len(scalars) + [pl.BlockSpec(mem...  12.5 us
  transfers between devices with their start and end apart: 43, of which 22 were waited for; matrix products, arithmetic and copies ran while one was open for 3% of the time, Pallas kernels for 36%

profile of v2, /device:TPU:0, one launch (start us, length us, event | category | flops | bytes accessed | tf_op | source)
XLA Modules:
  0.0 255.0 jit_solution(17932550264241959894)
XLA Ops:
  0.7 8.0 %shard_map.560 = (bf16[384,384]{1,0:T(8,128)(2,1)}, bf16[864,384]{1,0:T(8,128)(2,1)}, bf16[768,384]{1,0:T(8,128)(2,1)}, f32[34,8,384]{2,1,0:T(8,128)}) custom-call(f32[31,324]{1,0:T(8,128)} %depth_w.1, f32[2,324]{1,0:T(2,128)} %bn_w.1, f32[384,324]{1,0:T(8,128)} %constant.43.clone.pick, f32[81,4,324]{2,1,0:T(4,128)} %bitcast.69, f32[324,2,324]{2,1,0:T(2,128)} %bitcast.66, ...), custom_call_target="tpu_custom_call" | custom-call | flops 4000000000 | bytes 10000000 | tf_op jit(solution)/shard_map/pallas_call | solution.py:868
  8.7 3.0 %collective-permute-start = (bf16[384,384]{1,0:T(8,128)(2,1)}, bf16[384,384]{1,0:T(8,128)(2,1)S(1)}, u32[]{:S(2)}, u32[]{:S(2)}) collective-permute-start(bf16[384,384]{1,0:T(8,128)(2,1)} %get-tuple-element.133.w0), channel_id=1, source_target_pairs={{0,2},{1,3},{2,0},{3,1},{4,6},{5,7},{6,4},{7,5},{8,10},{9,11},{10,... | collective-permute-start | bytes 884744 | tf_op jit(solution)/shard_map/ppermute | solution.py:881
  11.7 7.2 %collective-permute-done.w2 = bf16[384,384]{1,0:T(8,128)(2,1)S(1)} collective-permute-done((bf16[384,384]{1,0:T(8,128)(2,1)}, bf16[384,384]{1,0:T(8,128)(2,1)S(1)}, u32[]{:S(2)}, u32[]{:S(2)}) %collective-permute-start) | collective-permute-done | bytes 294944 | tf_op jit(solution)/shard_map/ppermute | solution.py:881
  21.7 12.9 %shard_map.561 = (bf16[992,324]{1,0:T(8,128)(2,1)}, bf16[2,4,288,496]{3,2,1,0:T(8,128)(2,1)}, bf16[2,4,496,496]{3,2,1,0:T(8,128)(2,1)}, bf16[2,384,496]{2,1,0:T(...) custom-call(s32[1]{0:T(128)} %bitcast.rank_ref, s32[8]{0:T(128)} %len_ref.7, ...), custom_call_target="tpu_custom_call" | custom-call | flops 10000000000 | bytes 10000000 | tf_op jit(solution)/shard_map/pallas_call | solution.py:1033
  39.4 16.4 %shard_map.562 = (bf16[4,992,324]{2,1,0:T(8,128)(2,1)}, bf16[4,992,324]{2,1,0:T(8,128)(2,1)}, f32[992,324]{1,0:T(8,128)}, f32[992,1]{1,0:T(8,128)}, f32[992,384]...) custom-call(s32[1]{0:T(128)} %bitcast.rank_ref, s32[8]{0:T(128)} %len_ref.7, ...), custom_call_target="tpu_custom_call" | custom-call | flops 17999998976 | bytes 10000000 | tf_op jit(solution)/shard_map/pallas_call | solution.py:868
  70.2 2.9 %collective-permute-start.11 = (f32[3,384]{1,0:T(4,128)S(1)}, f32[3,384]{1,0:T(4,128)S(1)}, u32[]{:S(2)}, u32[]{:S(2)}) collective-permute-start(f32[3,384]{1,0:T(4,128)S(1)} %pad_maximum_fusion.3), channel_id=1, source_target_pairs={{0,16},{4,20},{8,24},{12,28},{16,0},{20,4},{24,8},{28,12},{1,17},{... | collective-permute-start | bytes 13832 | tf_op jit(solution)/shard_map/ppermute | solution.py:881
  76.4 24.9 %shard_map.563 = (bf16[324,992]{1,0:T(8,128)(2,1)}, f32[992,324]{1,0:T(8,128)}, f32[992,384]{1,0:T(8,128)}, bf16[2,768,384]{2,1,0:T(8,128)(2,1)}, bf16[2,768,384...) custom-call(s32[1]{0:T(128)} %bitcast.rank_ref, s32[8]{0:T(128)} %len_ref.7, ...), custom_call_target="tpu_custom_call" | custom-call | flops 30000001024 | bytes 10000000 | tf_op jit(solution)/shard_map/pallas_call | solution.py:868
  115.7 2.9 %collective-permute-start.19 = (f32[2,384]{1,0:T(2,128)S(1)}, f32[2,384]{1,0:T(2,128)S(1)}, u32[]{:S(2)}, u32[]{:S(2)}) collective-permute-start(f32[2,384]{1,0:T(2,128)S(1)} %add.238), channel_id=1, source_target_pairs={{0,16},{4,20},{8,24},{12,28},{16,0},{20,4},{24,8},{28,12},{1,17},{... | collective-permute-start | bytes 9224 | tf_op jit(solution)/shard_map/ppermute | solution.py:881
  122.2 17.0 %shard_map.564 = (f32[992,324]{1,0:T(8,128)}, bf16[4,192,324]{2,1,0:T(8,128)(2,1)}, bf16[80,324]{1,0:T(8,128)(2,1)}) custom-call(s32[1]{0:T(128)} %bitcast.rank_ref, s32[8]{0:T(128)} %len_ref.7, f32[8,324]{1,0:T(8,128)} %norm_w.1, f32[34,8,384]{2,1,0:T(8,128)} %get-tuple-element.132.chan, f32[3,384]{1,0:T(4,128)} %pad_maximum_fusion.4.stat, ...), custom_call_target="tpu_custom_call" | custom-call | flops 14000000000 | bytes 10000000 | tf_op jit(solution)/shard_map/pallas_call | solution.py:868
  140.9 11.7 %shard_map.565 = (bf16[4,992,324]{2,1,0:T(8,128)(2,1)}, bf16[2,960,384]{2,1,0:T(8,128)(2,1)}, bf16[2,960,384]{2,1,0:T(8,128)(2,1)}) custom-call(f32[8,324]{1,0:T(8,128)} %norm_w.1, bf16[4,192,324]{2,1,0:T(8,128)(2,1)} %get-tuple-element.168.cin_grad, bf16[80,324]{1,0:T(8,128)(2,1)} %get-tuple-element.169.vectors, f32[992,324]{1,0:T(8,128)} %get-tuple-element.166.up_in, ...), custom_call_target="tpu_custom_call" | custom-call | flops 12000000000 | bytes 10000000 | tf_op jit(solution)/shard_map/pallas_call | solution.py:868
  154.5 8.4 %shard_map.566 = (f32[992,324]{1,0:T(8,128)}, f32[8,324]{1,0:T(8,128)}) custom-call(f32[8,324]{1,0:T(8,128)} %norm_w.1, f32[992,324]{1,0:T(8,128)} %get-tuple-element.166.up_in, f32[992,324]{1,0:T(8,128)} %get-tuple-element.140.n1_in, f32[992,1]{1,0:T(8,128)} %get-tuple-element.167.s1_in, bf16[864,384]{1,0:T(8,128)(2,1)} %get-tuple-element.135.w0, ...), custom_call_target="tpu_custom_call" | custom-call | flops 8000000000 | bytes 10000000 | tf_op jit(solution)/shard_map/pallas_call | solution.py:868
  168.0 14.6 %shard_map.567 = (f32[324,992]{1,0:T(8,128)}, bf16[2,384,384]{2,1,0:T(8,128)(2,1)S(1)}, bf16[2,384,384]{2,1,0:T(8,128)(2,1)S(1)}) custom-call(s32[1]{0:T(128)} %bitcast.rank_ref, s32[8]{0:T(128)S(1)} %copy-done.29, bf16[992,324]{1,0:T(8,128)(2,1)S(1)} %copy-done.35, bf16[384,384]{1,0:T(8,128)(2,1)} %get-tuple-element.133.w0, bf16[384,384]{1,0:T(8,128)(2,1)} %copy-done.47, ...), custom_call_target="tpu_custom_call" | custom-call | flops 16000000000 | bytes 10000000 | tf_op jit(solution)/shard_map/pallas_call | solution.py:1152
  182.6 2.1 collective-permute-done.26
  187.6 4.0 %collective-permute-done.27 = bf16[208,384]{1,0:T(8,128)(2,1)S(1)} collective-permute-done((bf16[208,384]{1,0:T(8,128)(2,1)S(1)}, bf16[208,384]{1,0:T(8,128)(2,1)S(1)}, u32[]{:S(2)}, u32[]{:S(2)}) %collective-permute-start.27) | collective-permute-done | bytes 159776 | tf_op jit(solution)/shard_map/ppermute | solution.py:881
  192.3 8.6 %collective-permute-done.31 = bf16[272,384]{1,0:T(8,128)(2,1)S(1)} collective-permute-done((bf16[272,384]{1,0:T(8,128)(2,1)S(1)}, bf16[272,384]{1,0:T(8,128)(2,1)S(1)}, u32[]{:S(2)}, u32[]{:S(2)}) %collective-permute-start.31) | collective-permute-done | bytes 208928 | tf_op jit(solution)/shard_map/ppermute | solution.py:881
  204.0 7.5 %collective-permute-done.32 = bf16[272,384]{1,0:T(8,128)(2,1)S(1)} collective-permute-done((bf16[272,384]{1,0:T(8,128)(2,1)S(1)}, bf16[272,384]{1,0:T(8,128)(2,1)S(1)}, u32[]{:S(2)}, u32[]{:S(2)}) %collective-permute-start.32) | collective-permute-done | bytes 208928 | tf_op jit(solution)/shard_map/ppermute | solution.py:881
  213.3 3.4 %collective-permute-done.37 = bf16[192,384]{1,0:T(8,128)(2,1)S(1)} collective-permute-done((bf16[192,384]{1,0:T(8,128)(2,1)S(1)}, bf16[192,384]{1,0:T(8,128)(2,1)S(1)}, u32[]{:S(2)}, u32[]{:S(2)}) %collective-permute-start.37) | collective-permute-done | bytes 147488 | tf_op jit(solution)/shard_map/ppermute | solution.py:881
  218.6 4.2 %collective-permute-done.33 = bf16[272,384]{1,0:T(8,128)(2,1)S(1)} collective-permute-done((bf16[272,384]{1,0:T(8,128)(2,1)S(1)}, bf16[272,384]{1,0:T(8,128)(2,1)S(1)}, u32[]{:S(2)}, u32[]{:S(2)}) %collective-permute-start.33) | collective-permute-done | bytes 208928 | tf_op jit(solution)/shard_map/ppermute | solution.py:881
  224.9 6.0 %collective-permute-done.39 = bf16[192,384]{1,0:T(8,128)(2,1)S(1)} collective-permute-done((bf16[192,384]{1,0:T(8,128)(2,1)S(1)}, bf16[192,384]{1,0:T(8,128)(2,1)S(1)}, u32[]{:S(2)}, u32[]{:S(2)}) %collective-permute-start.39) | collective-permute-done | bytes 147488 | tf_op jit(solution)/shard_map/ppermute | solution.py:881
  231.6 4.1 %shard_map.568 = (f32[324,2,324]{2,1,0:T(2,128)}, f32[324,2,324]{2,1,0:T(2,128)}, f32[324,2,324]{2,1,0:T(2,128)S(1)}, f32[81,324]{1,0:T(8,128)}, f32[81,324]{1,0...) custom-call(s32[1]{0:T(128)} %bitcast.12.spot_ref, ...), custom_call_target="tpu_custom_call" | custom-call | flops 1000000 | bytes 2000000 | tf_op jit(solution)/shard_map/pallas_call | solution.py:852
  236.0 5.7 %shard_map.569 = (f32[324,2,324]{2,1,0:T(2,128)}, f32[324,2,324]{2,1,0:T(2,128)}, f32[324,2,324]{2,1,0:T(2,128)S(1)}, f32[81,2,324]{2,1,0:T(2,128)}, f32[81,2,32...) custom-call(s32[1]{0:T(128)} %bitcast.12.spot_ref, bf16[272,384]{1,0:T(8,128)(2,1)S(1)} %add_convert_fusion.9.mine, ...), custom_call_target="tpu_custom_call" | custom-call | flops 1000000 | bytes 2000000 | tf_op jit(solution)/shard_map/pallas_call | solution.py:852
  241.9 2.6 %shard_map.570 = (f32[81,4,324]{2,1,0:T(4,128)}, f32[3,81,324]{2,1,0:T(8,128)}, f32[81,324]{1,0:T(8,128)}, f32[81,4,324]{2,1,0:T(4,128)S(1)}, f32[31,324]{1,0:T(...) custom-call(s32[1]{0:T(128)} %bitcast.12.spot_ref, ...), custom_call_target="tpu_custom_call" | custom-call | flops 1000000 | bytes 2000000 | tf_op jit(solution)/shard_map/pallas_call | solution.py:852
  246.8 2.8 %collective-permute-done.42 = f32[32,128]{1,0:T(8,128)S(1)} collective-permute-done((f32[32,128]{1,0:T(8,128)S(1)}, f32[32,128]{1,0:T(8,128)S(1)}, u32[]{:S(2)}, u32[]{:S(2)}) %collective-permute-start.42) | collective-permute-done | bytes 16416 | tf_op jit(solution)/shard_map/ppermute | solution.py:881
  249.6 5.0 %shard_map.571 = (f32[324,2,324]{2,1,0:T(2,128)}, f32[324,2,324]{2,1,0:T(2,128)}, f32[81,4,324]{2,1,0:T(4,128)}, f32[81,2,324]{2,1,0:T(2,128)}, f32[81,324]{1,0:...) custom-call(f32[32,128]{1,0:T(8,128)S(1)} %add.279.sums, f32[324,2,324]{2,1,0:T(2,128)S(1)} %bitcast.68, ...), custom_call_target="tpu_custom_call" | custom-call | flops 1000000 | bytes 10000000 | tf_op jit(solution)/shard_map/pallas_call | solution.py:868
  (214 shorter events, 66.9 us)
Async XLA Ops:
  8.7 10.2 %collective-permute-start = (bf16[384,384]{1,0:T(8,128)(2,1)}, bf16[384,384]{1,0:T(8,128)(2,1)S(1)}, u32[]{:S(2)}, u32[]{:S(2)}) collective-permute-start(bf16[384,384]{1,0:T(8,128)(2,1)} %get-tuple-element.133.w0), channel_id=1, source_target_pairs={{0,2},{1,3},{2,0},{3,1},{4,6},{5,7},{6,4},{7,5},{8,10},{9,11},{10,... | collective-permute-start | bytes 884744 | tf_op jit(solution)/shard_map/ppermute | solution.py:881
  11.7 9.2 %collective-permute-start.2 = (bf16[384,384]{1,0:T(8,128)(2,1)}, bf16[384,384]{1,0:T(8,128)(2,1)S(1)}, u32[]{:S(2)}, u32[]{:S(2)}) collective-permute-start(bf16[384,384]{1,0:T(8,128)(2,1)} %get-tuple-element.133.w0), channel_id=1, source_target_pairs={{0,1},{1,0},{2,3},{3,2},{4,5},{5,4},{6,7},{7,6},{8,9},{9,8},{10,11... | collective-permute-start | bytes 884744 | tf_op jit(solution)/shard_map/ppermute | solution.py:881
  18.9 17.5 %collective-permute-start.1 = (bf16[864,384]{1,0:T(8,128)(2,1)}, bf16[864,384]{1,0:T(8,128)(2,1)S(1)}, u32[]{:S(2)}, u32[]{:S(2)}) collective-permute-start(bf16[864,384]{1,0:T(8,128)(2,1)} %get-tuple-element.135.w0), channel_id=1, source_target_pairs={{0,2},{1,3},{2,0},{3,1},{4,6},{5,7},{6,4},{7,5},{8,10},{9,11},{10,... | collective-permute-start | bytes 1990664 | tf_op jit(solution)/shard_map/ppermute | solution.py:881
  20.7 17.6 %collective-permute-start.5 = (bf16[864,384]{1,0:T(8,128)(2,1)}, bf16[864,384]{1,0:T(8,128)(2,1)S(1)}, u32[]{:S(2)}, u32[]{:S(2)}) collective-permute-start(bf16[864,384]{1,0:T(8,128)(2,1)} %get-tuple-element.135.w0), channel_id=1, source_target_pairs={{0,1},{1,0},{2,3},{3,2},{4,5},{5,4},{6,7},{7,6},{8,9},{9,8},{10,11... | collective-permute-start | bytes 1990664 | tf_op jit(solution)/shard_map/ppermute | solution.py:881
  36.5 19.4 %collective-permute-start.4 = (bf16[768,384]{1,0:T(8,128)(2,1)S(1)}, bf16[768,384]{1,0:T(8,128)(2,1)S(1)}, u32[]{:S(2)}, u32[]{:S(2)}) collective-permute-start(bf16[768,384]{1,0:T(8,128)(2,1)S(1)} %copy-done.42), channel_id=1, source_target_pairs={{0,2},{1,3},{2,0},{3,1},{4,6},{5,7},{6,4},{7,5},{8,10},{9,11},{10,... | collective-permute-start | bytes 1769480 | tf_op jit(solution)/shard_map/ppermute | solution.py:881
  101.2 7.2 %collective-permute-start.16 = (bf16[2,768,384]{2,1,0:T(8,128)(2,1)}, bf16[2,768,384]{2,1,0:T(8,128)(2,1)S(1)}, u32[]{:S(2)}, u32[]{:S(2)}) collective-permute-start(bf16[2,768,384]{2,1,0:T(8,128)(2,1)} %get-tuple-element.154), channel_id=1, source_target_pairs={{0,1},{1,0},{2,3},{3,2},{4,5},{5,4},{6,7},{7,6},{8,9},{9,8},{10,11... | collective-permute-start | bytes 3538952 | tf_op jit(solution)/shard_map/ppermute | solution.py:881
  120.1 19.2 %collective-permute-start.20 = (bf16[768,384]{1,0:T(8,128)(2,1)S(1)}, bf16[768,384]{1,0:T(8,128)(2,1)S(1)}, u32[]{:S(2)}, u32[]{:S(2)}) collective-permute-start(bf16[768,384]{1,0:T(8,128)(2,1)S(1)} %get-tuple-element.243), channel_id=1, source_target_pairs={{0,2},{1,3},{2,0},{3,1},{4,6},{5,7},{6,4},{7,5},{8,10},{9,11},{10,... | collective-permute-start | bytes 1769480 | tf_op jit(solution)/shard_map/ppermute | solution.py:881
  139.3 13.4 %collective-permute-start.21 = (bf16[384,384]{1,0:T(8,128)(2,1)S(1)}, bf16[384,384]{1,0:T(8,128)(2,1)S(1)}, u32[]{:S(2)}, u32[]{:S(2)}) collective-permute-start(bf16[384,384]{1,0:T(8,128)(2,1)S(1)} %fusion.3), channel_id=1, source_target_pairs={{0,4},{4,0},{8,12},{12,8},{16,20},{20,16},{24,28},{28,24},{1,5},{5... | collective-permute-start | bytes 884744 | tf_op jit(solution)/shard_map/ppermute | solution.py:881
  152.6 11.8 %collective-permute-start.23 = (bf16[2,960,384]{2,1,0:T(8,128)(2,1)}, bf16[2,960,384]{2,1,0:T(8,128)(2,1)}, u32[]{:S(2)}, u32[]{:S(2)}) collective-permute-start(bf16[2,960,384]{2,1,0:T(8,128)(2,1)} %get-tuple-element.178), channel_id=1, source_target_pairs={{0,1},{1,0},{2,3},{3,2},{4,5},{5,4},{6,7},{7,6},{8,9},{9,8},{10,11... | collective-permute-start | bytes 4423688 | tf_op jit(solution)/shard_map/ppermute | solution.py:881
  152.9 10.0 %collective-permute-start.22 = (bf16[384,384]{1,0:T(8,128)(2,1)S(1)}, bf16[384,384]{1,0:T(8,128)(2,1)S(1)}, u32[]{:S(2)}, u32[]{:S(2)}) collective-permute-start(bf16[384,384]{1,0:T(8,128)(2,1)S(1)} %add_convert_fusion.8), channel_id=1, source_target_pairs={{0,8},{4,12},{8,0},{12,4},{16,24},{20,28},{24,16},{28,20},{1,9},{5... | collective-permute-start | bytes 884744 | tf_op jit(solution)/shard_map/ppermute | solution.py:881
  163.0 19.6 %collective-permute-start.24 = (bf16[384,384]{1,0:T(8,128)(2,1)S(1)}, bf16[384,384]{1,0:T(8,128)(2,1)S(1)}, u32[]{:S(2)}, u32[]{:S(2)}) collective-permute-start(bf16[384,384]{1,0:T(8,128)(2,1)S(1)} %add_convert_fusion.7), channel_id=1, source_target_pairs={{0,16},{4,20},{8,24},{12,28},{16,0},{20,4},{24,8},{28,12},{1,17},{... | collective-permute-start | bytes 884744 | tf_op jit(solution)/shard_map/ppermute | solution.py:881
  166.4 18.4 %collective-permute-start.26 = (bf16[960,384]{1,0:T(8,128)(2,1)S(1)}, bf16[960,384]{1,0:T(8,128)(2,1)S(1)}, u32[]{:S(2)}, u32[]{:S(2)}) collective-permute-start(bf16[960,384]{1,0:T(8,128)(2,1)S(1)} %get-tuple-element.241), channel_id=1, source_target_pairs={{0,2},{1,3},{2,0},{3,1},{4,6},{5,7},{6,4},{7,5},{8,10},{9,11},{10,... | collective-permute-start | bytes 2211848 | tf_op jit(solution)/shard_map/ppermute | solution.py:881
  185.3 15.6 %collective-permute-start.35 = (bf16[2,384,384]{2,1,0:T(8,128)(2,1)S(1)}, bf16[2,384,384]{2,1,0:T(8,128)(2,1)S(1)}, u32[]{:S(2)}, u32[]{:S(2)}) collective-permute-start(bf16[2,384,384]{2,1,0:T(8,128)(2,1)S(1)} %get-tuple-element.193), channel_id=1, source_target_pairs={{0,1},{1,0},{2,3},{3,2},{4,5},{5,4},{6,7},{7,6},{8,9},{9,8},{10,11... | collective-permute-start | bytes 1769480 | tf_op jit(solution)/shard_map/ppermute | solution.py:881
  185.4 46.1 %collective-permute-start.25 = (bf16[384,384]{1,0:T(8,128)(2,1)S(1)}, bf16[384,384]{1,0:T(8,128)(2,1)S(1)}, u32[]{:S(2)}, u32[]{:S(2)}) collective-permute-start(bf16[384,384]{1,0:T(8,128)(2,1)S(1)} %add_convert_fusion.6.one_mine), channel_id=1, source_target_pairs={{0,4},{4,0},{8,12},{12,8},{16,20},{20,16},{24,28},{28,24},{1,5},{5... | collective-permute-start | bytes 884744 | tf_op jit(solution)/shard_map/ppermute | solution.py:881
  187.1 13.8 %collective-permute-start.31 = (bf16[272,384]{1,0:T(8,128)(2,1)S(1)}, bf16[272,384]{1,0:T(8,128)(2,1)S(1)}, u32[]{:S(2)}, u32[]{:S(2)}) collective-permute-start(bf16[272,384]{1,0:T(8,128)(2,1)S(1)} %fusion.4), channel_id=1, source_target_pairs={{0,4},{4,0},{8,12},{12,8},{16,20},{20,16},{24,28},{28,24},{1,5},{5... | collective-permute-start | bytes 626696 | tf_op jit(solution)/shard_map/ppermute | solution.py:881
  191.7 11.5 %collective-permute-start.28 = (bf16[208,384]{1,0:T(8,128)(2,1)S(1)}, bf16[208,384]{1,0:T(8,128)(2,1)S(1)}, u32[]{:S(2)}, u32[]{:S(2)}) collective-permute-start(bf16[208,384]{1,0:T(8,128)(2,1)S(1)} %add_convert_fusion.14), channel_id=1, source_target_pairs={{0,8},{4,12},{8,0},{12,4},{16,24},{20,28},{24,16},{28,20},{1,9},{5... | collective-permute-start | bytes 479240 | tf_op jit(solution)/shard_map/ppermute | solution.py:881
  201.1 10.3 %collective-permute-start.36 = (bf16[384,384]{1,0:T(8,128)(2,1)S(1)}, bf16[384,384]{1,0:T(8,128)(2,1)S(1)}, u32[]{:S(2)}, u32[]{:S(2)}) collective-permute-start(bf16[384,384]{1,0:T(8,128)(2,1)S(1)} %get-tuple-element.245), channel_id=1, source_target_pairs={{0,2},{1,3},{2,0},{3,1},{4,6},{5,7},{6,4},{7,5},{8,10},{9,11},{10,... | collective-permute-start | bytes 884744 | tf_op jit(solution)/shard_map/ppermute | solution.py:881
  202.7 8.7 %collective-permute-start.32 = (bf16[272,384]{1,0:T(8,128)(2,1)S(1)}, bf16[272,384]{1,0:T(8,128)(2,1)S(1)}, u32[]{:S(2)}, u32[]{:S(2)}) collective-permute-start(bf16[272,384]{1,0:T(8,128)(2,1)S(1)} %add_convert_fusion.11), channel_id=1, source_target_pairs={{0,8},{4,12},{8,0},{12,4},{16,24},{20,28},{24,16},{28,20},{1,9},{5... | collective-permute-start | bytes 626696 | tf_op jit(solution)/shard_map/ppermute | solution.py:881
  203.3 10.0 %collective-permute-start.29 = (bf16[208,384]{1,0:T(8,128)(2,1)S(1)}, bf16[208,384]{1,0:T(8,128)(2,1)S(1)}, u32[]{:S(2)}, u32[]{:S(2)}) collective-permute-start(bf16[208,384]{1,0:T(8,128)(2,1)S(1)} %add_convert_fusion.13), channel_id=1, source_target_pairs={{0,16},{4,20},{8,24},{12,28},{16,0},{20,4},{24,8},{28,12},{1,17},{... | collective-permute-start | bytes 479240 | tf_op jit(solution)/shard_map/ppermute | solution.py:881
  213.3 9.6 %collective-permute-start.33 = (bf16[272,384]{1,0:T(8,128)(2,1)S(1)}, bf16[272,384]{1,0:T(8,128)(2,1)S(1)}, u32[]{:S(2)}, u32[]{:S(2)}) collective-permute-start(bf16[272,384]{1,0:T(8,128)(2,1)S(1)} %add_convert_fusion.10), channel_id=1, source_target_pairs={{0,16},{4,20},{8,24},{12,28},{16,0},{20,4},{24,8},{28,12},{1,17},{... | collective-permute-start | bytes 626696 | tf_op jit(solution)/shard_map/ppermute | solution.py:881
  216.8 7.4 %collective-permute-start.38 = (bf16[192,384]{1,0:T(8,128)(2,1)S(1)}, bf16[192,384]{1,0:T(8,128)(2,1)S(1)}, u32[]{:S(2)}, u32[]{:S(2)}) collective-permute-start(bf16[192,384]{1,0:T(8,128)(2,1)S(1)} %add_convert_fusion.17), channel_id=1, source_target_pairs={{0,8},{4,12},{8,0},{12,4},{16,24},{20,28},{24,16},{28,20},{1,9},{5... | collective-permute-start | bytes 442376 | tf_op jit(solution)/shard_map/ppermute | solution.py:881
  216.9 14.6 %collective-permute-start.30 = (bf16[208,384]{1,0:T(8,128)(2,1)S(1)}, bf16[208,384]{1,0:T(8,128)(2,1)S(1)}, u32[]{:S(2)}, u32[]{:S(2)}) collective-permute-start(bf16[208,384]{1,0:T(8,128)(2,1)S(1)} %add_convert_fusion.12.two_mine), channel_id=1, source_target_pairs={{0,4},{4,0},{8,12},{12,8},{16,20},{20,16},{24,28},{28,24},{1,5},{5... | collective-permute-start | bytes 479240 | tf_op jit(solution)/shard_map/ppermute | solution.py:881
  224.4 11.3 %collective-permute-start.34 = (bf16[272,384]{1,0:T(8,128)(2,1)S(1)}, bf16[272,384]{1,0:T(8,128)(2,1)S(1)}, u32[]{:S(2)}, u32[]{:S(2)}) collective-permute-start(bf16[272,384]{1,0:T(8,128)(2,1)S(1)} %add_convert_fusion.9.mine), channel_id=1, source_target_pairs={{0,4},{4,0},{8,12},{12,8},{16,20},{20,16},{24,28},{28,24},{1,5},{5... | collective-permute-start | bytes 626696 | tf_op jit(solution)/shard_map/ppermute | solution.py:881
  231.0 10.8 %collective-permute-start.40 = (bf16[192,384]{1,0:T(8,128)(2,1)S(1)}, bf16[192,384]{1,0:T(8,128)(2,1)S(1)}, u32[]{:S(2)}, u32[]{:S(2)}) collective-permute-start(bf16[192,384]{1,0:T(8,128)(2,1)S(1)} %add_convert_fusion.15.mine), channel_id=1, source_target_pairs={{0,4},{4,0},{8,12},{12,8},{16,20},{20,16},{24,28},{28,24},{1,5},{5... | collective-permute-start | bytes 442376 | tf_op jit(solution)/shard_map/ppermute | solution.py:881
  (68 other events, 448.9 us)

commit v3 on v2

--- a/solution.py
+++ b/solution.py
@@ -22,7 +22,7 @@
 FF_ROWS = 336
 TAIL = 2 * FF_ROWS
 CONV_IN_ROWS = 2 * PAD
-VECTOR_ROWS = 80
+VECTOR_ROWS = 48
 LOWER_VEC = FF_ROWS
 LOWER_SPLIT = FF_ROWS + VECTOR_ROWS
 LOWER_UP = LOWER_SPLIT
@@ -93,6 +93,9 @@
     return lax.broadcasted_iota(jnp.int32, (SLOT, 1), 0) < count
 
 
+FOLD = (False, False, False)
+
+
 def assemble(scratch, parts, rank, first, count):
     for place, part in enumerate(parts):
         scratch[place ^ rank] = part[first : first + count, 0:D]
@@ -118,17 +121,24 @@
     base_low = base.astype(BF16)
     low_out[...] = base_low
     valid = valid_rows(len_ref[which])
-    for head in range(HEADS):
+
+    def project(head):
         qkv = dot_nt(weights[head, 0 : 3 * PAD, :], base_low).astype(BF16)
         qkv_out[head] = qkv
-        queries, keys, values = qkv[:PAD], qkv[PAD : 2 * PAD], qkv[2 * PAD :]
-        scores = jnp.where(valid, dot_tn(keys, queries) * SCALE, MASK_FILL)
+        return qkv, dot_tn(qkv[PAD : 2 * PAD], qkv[:PAD])
+
+    later = project(0)
+    for head in range(HEADS):
+        qkv, products = later
+        if head + 1 < HEADS:
+            later = project(head + 1)
+        scores = jnp.where(valid, products * SCALE, MASK_FILL)
         top = jnp.max(scores, axis=0, keepdims=True)
         expo = jnp.exp(scores - top)
         total = jnp.sum(expo, axis=0, keepdims=True)
         probs = (expo * (1.0 / total)).astype(BF16)
         prob_out[head] = probs
-        mixed_out[head * PAD : (head + 1) * PAD, :] = dot_nn(values, probs).astype(BF16)
+        mixed_out[head * PAD : (head + 1) * PAD, :] = dot_nn(qkv[2 * PAD :], probs).astype(BF16)
     attn_out = dot_tn(mixed_out[...], wout_out[...])
     normal, inv = ln_forward(base + attn_out)
     n1_out[...] = normal
@@ -236,40 +246,45 @@
             copy.wait()
 
 
-def pack_kernel(
-    depth, bn, pick, attn_in, ffin_in, ffout_in, convin_in, convout_in,
-    attn_out, one_out, two_out, chan_out,
-    attn, ffin, ffout, convin, convout, attn_low, one, two, sems,
+def attn_pack_kernel(attn_in, out, attn, low, sems):
+    copies = Copies(sems)
+    load = copies.start(attn_in, attn)
+    low[...] = jnp.zeros_like(low)
+    load.wait()
+    for j in range(4):
+        low[j * PAD : j * PAD + HD, 0:D] = attn[:, j, :].astype(BF16)
+    copies.out(low, out)
+    copies.finish()
+
+
+def rest_pack_kernel(
+    depth, bn, pick, ffin_in, ffout_in, convin_in, convout_in, one_out, two_out, chan_out,
+    ffin, ffout, convin, convout, one, two, sems,
 ):
     copies = Copies(sems)
-    pairs = (attn_in, attn), (ffin_in, ffin), (ffout_in, ffout), (convin_in, convin), (convout_in, convout)
+    pairs = (ffin_in, ffin), (ffout_in, ffout), (convin_in, convin), (convout_in, convout)
     loads = [copies.start(source, target) for source, target in pairs]
-    for out in (attn_low, one, two):
+
+    def spread(rows):
+        return lax.dot_general(
+            rows, pick[...], (((1,), (1,)), ((), ())), precision=PRECISE, preferred_element_type=F32
+        )
+
+    for first, rows in ((0, spread(depth[...])), (32, spread(bn[...]))):
+        count = rows.shape[0]
+        chan_out[first : first + count] = jnp.broadcast_to(rows[:, None, :], (count, 8, WIDE))
+    for out in (one, two):
         out[...] = jnp.zeros_like(out)
-    loads[0].wait()
-    for j in range(4):
-        attn_low[j * PAD : j * PAD + HD, 0:D] = attn[:, j, :].astype(BF16)
-    copies.out(attn_low, attn_out)
-    loads[1].wait()
-    loads[2].wait()
+    for load in loads:
+        load.wait()
     for j, out in ((0, one), (1, two)):
         out[0:D, 0:D] = ffin[:, j, :].astype(BF16)
         out[FF_ROWS : FF_ROWS + D, 0:D] = ffout[:, j, :].astype(BF16)
-    loads[3].wait()
-    loads[4].wait()
     for j in range(2):
         one[TAIL + j * PAD : TAIL + j * PAD + HD, 0:D] = convin[:, j, :].astype(BF16)
     two[TAIL : TAIL + HD, 0:D] = convout[...].astype(BF16)
     copies.out(one, one_out)
     copies.out(two, two_out)
-    def spread(rows):
-        return lax.dot_general(
-            rows, pick[...], (((1,), (1,)), ((), ())), precision=PRECISE, preferred_element_type=F32
-        )
-
-    for first, rows in ((0, spread(depth[...])), (32, spread(bn[...]))):
-        count = rows.shape[0]
-        chan_out[first : first + count] = jnp.broadcast_to(rows[:, None, :], (count, 8, WIDE))
     copies.finish()
 
 
@@ -619,25 +634,37 @@
     base_low = low_in[...]
     upstream = grad[...]
     up_low = upstream.astype(BF16)
+    mixed_grad = dot_nt(wout[...], up_low).astype(BF16)
+
+    def up_head(head):
+        return mixed_grad[head * PAD : (head + 1) * PAD, :]
+
+    def prob_product(head):
+        return dot_tn(qkv_in[head, 2 * PAD :, :], up_head(head))
+
+    later = prob_product(0)
     acc_out[...] += dot_nn(mixed[...], up_low)
-    mixed_grad = dot_nt(wout[...], up_low).astype(BF16)
     total = upstream
-    for head in range(HEADS):
-        queries = qkv_in[head, 0:PAD, :]
-        keys = qkv_in[head, PAD : 2 * PAD, :]
-        values = qkv_in[head, 2 * PAD :, :]
-        up_head = mixed_grad[head * PAD : (head + 1) * PAD, :]
-        probs_low = probs_in[head]
-        probs = probs_low.astype(F32)
-        prob_grad = dot_tn(values, up_head)
-        delta = jnp.sum(prob_grad * probs, axis=0, keepdims=True)
-        score_grad = (probs * (prob_grad - delta)).astype(BF16)
-        query_grad = (dot_nn(keys, score_grad) * SCALE).astype(BF16)
-        key_grad = (dot_nt(queries, score_grad) * SCALE).astype(BF16)
-        value_grad = dot_nt(up_head, probs_low).astype(BF16)
-        grads = jnp.concatenate([query_grad, key_grad, value_grad], axis=0)
-        acc[head] += dot_nn(grads, base_low)
-        total = total + dot_tn(grads, weights[head])
+    waiting = None
+    for head in range(HEADS + 1):
+        if head < HEADS:
+            prob_grad = later
+            if head + 1 < HEADS:
+                later = prob_product(head + 1)
+            probs_low = probs_in[head]
+            probs = probs_low.astype(F32)
+            delta = jnp.sum(prob_grad * probs, axis=0, keepdims=True)
+            score_grad = (probs * (prob_grad - delta)).astype(BF16)
+        if waiting is not None:
+            acc[head - 1] += dot_nn(waiting, base_low)
+            total = total + dot_tn(waiting, weights[head - 1])
+        if head < HEADS:
+            queries = qkv_in[head, 0:PAD, :]
+            keys = qkv_in[head, PAD : 2 * PAD, :]
+            value_grad = dot_nt(up_head(head), probs_low).astype(BF16)
+            query_grad = (dot_nn(keys, score_grad) * SCALE).astype(BF16)
+            key_grad = (dot_nt(queries, score_grad) * SCALE).astype(BF16)
+            waiting = jnp.concatenate([query_grad, key_grad, value_grad], axis=0)
     rows_out[pl.ds(utt * SLOT, SLOT), :] = total
     column = jnp.sum(total, axis=0, keepdims=True)
     kind = kind_ref[rank * pl.num_programs(0) + utt]
@@ -843,7 +870,7 @@
         out_specs=out_specs,
         out_shape=placed(out_shape, pinned),
         scratch_shapes=list(scratch),
-        cost_estimate=pl.CostEstimate(flops=cost, bytes_accessed=10_000_000, transcendentals=0),
+        cost_estimate=pl.CostEstimate(flops=cost, bytes_accessed=cost // 1000, transcendentals=0),
         compiler_params=pltpu.CompilerParams(vmem_limit_bytes=limit * 1024 * 1024),
     )
 
@@ -871,7 +898,7 @@
         out_specs=[ANY] * len(large_out) + [VMEM] * len(small_out),
         out_shape=placed(large_out + small_out, pinned),
         scratch_shapes=[pltpu.VMEM(*entry) for entry in scratch] + [pltpu.SemaphoreType.DMA((copies,))],
-        cost_estimate=pl.CostEstimate(flops=cost, bytes_accessed=10_000_000, transcendentals=0),
+        cost_estimate=pl.CostEstimate(flops=cost, bytes_accessed=cost // 1000, transcendentals=0),
         compiler_params=pltpu.CompilerParams(vmem_limit_bytes=limit * 1024 * 1024),
     )(*scalars, *small, *large)
 
@@ -882,13 +909,26 @@
 
 
 def combine_all(value, merge, pause=None):
-    for bit in bits_of("tensor"):
-        value = merge(value, swap(value, "tensor", bit))
+    def over(value, axis, bits):
+        if len(bits) == 1:
+            return merge(value, swap(value, axis, bits[0]))
+        one, two = bits
+        others = [swap(value, axis, bit) for bit in (one, two, one ^ two)]
+        return merge(merge(value, others[0]), merge(others[1], others[2]))
+
+    def axis_sum(value, axis):
+        bits = bits_of(axis)
+        first = len(bits) % 2
+        if first:
+            value = over(value, axis, bits[:1])
+        for i in range(first, len(bits), 2):
+            value = over(value, axis, bits[i : i + 2])
+        return value
+
+    value = axis_sum(value, "tensor")
     if pause is not None:
         value = pause(value)
-    for bit in bits_of("dp"):
-        value = merge(value, swap(value, "dp", bit))
-    return value
+    return axis_sum(value, "dp")
 
 
 def bits_of(axis):
@@ -918,19 +958,46 @@
     return (one.astype(F32) + two.astype(F32)).astype(BF16)
 
 
-def dp_steps(mine, got, first=0, count=None):
+def vanish(value):
+    return jnp.minimum(jnp.abs(value[0, 0].astype(F32)), 0.0)
+
+
+def put_after(array, value):
+    return (array.astype(F32) + vanish(value)).astype(array.dtype)
+
+
+def dp_steps(mine, got, first=0, count=None, fold=False, after=None):
     spot = lax.axis_index("dp") & 1
-    half = (mine.shape[0] if count is None else count) // 2
+    half = (mine.shape[0] - first if count is None else count) // 2
+    if after is not None:
+        got = put_after(got, after)
 
     def cut(array, place):
         return lax.dynamic_slice_in_dim(array, first + place * half, half, 0)
 
     kept = add_low(cut(mine, spot), cut(got, spot))
     got = yield swap(add_low(cut(mine, 1 - spot), cut(got, 1 - spot)), "dp", 1)
-    kept = add_low(kept, got)
-    for bit in bits_of("dp")[1:]:
-        got = yield swap(kept, "dp", bit)
+    bits = bits_of("dp")[1:]
+    if fold:
+        zed = lax.axis_index("dp") // 2 & 1
+        part = half // 2
+
+        def cut_again(array, place):
+            return lax.dynamic_slice_in_dim(array, place * part, part, 0)
+
+        mine = add_low(cut_again(kept, zed), cut_again(got, zed))
+        got = yield swap(add_low(cut_again(kept, 1 - zed), cut_again(got, 1 - zed)), "dp", bits[0])
+        kept = add_low(mine, got)
+        for bit in bits[1:]:
+            got = yield swap(kept, "dp", bit)
+            kept = add_low(kept, got)
+        got = yield swap(kept, "dp", bits[0])
+        kept = jnp.where(zed == 0, jnp.concatenate([kept, got]), jnp.concatenate([got, kept]))
+    else:
         kept = add_low(kept, got)
+        for bit in bits:
+            got = yield swap(kept, "dp", bit)
+            kept = add_low(kept, got)
     got = yield swap(kept, "dp", 1)
     return kept, got
 
@@ -942,9 +1009,9 @@
     return mine, got
 
 
-def reduce_steps(send, keep):
+def reduce_steps(send, keep, fold=False):
     mine, got = yield from tensor_steps(send, keep)
-    return (yield from dp_steps(mine, got))
+    return (yield from dp_steps(mine, got, fold=fold))
 
 
 class Reduction:
@@ -953,12 +1020,17 @@
         self.flight = next(steps)
         self.result = None
 
-    def advance(self, value):
+    def advance(self, value, after=None):
+        if self.result is not None:
+            return value
         value, got = tie(value, self.flight)
+        if after is not None:
+            got = put_after(got, after)
         self.send(got)
         return value
 
     def send(self, got):
+        self.last = got
         try:
             self.flight = self.steps.send(got)
         except StopIteration as end:
@@ -999,18 +1071,31 @@
 
     pack_one_rows = TAIL + CONV_IN_ROWS
     pack_two_rows = TAIL + PAD
-    shards = (attn_w, ffin_w, ffout_w, convin_w, convout_w)
-    packs = [((count, WIDE), BF16) for count in (4 * PAD, pack_one_rows, pack_two_rows)]
-    attn_low, pack_one, pack_two, chan = call_mixed(
-        pack_kernel,
+    attn_pack = ((4 * PAD, WIDE), BF16)
+    (attn_low,) = call_mixed(
+        attn_pack_kernel,
         (),
-        (depth_w, bn_w, pick_wide),
+        (),
+        (attn_w,),
+        [attn_pack],
+        [],
+        [(attn_w.shape, F32), attn_pack],
+        2,
+        1_000,
+    )
+    shards = (ffin_w, ffout_w, convin_w, convout_w)
+    packs = [((count, WIDE), BF16) for count in (pack_one_rows, pack_two_rows)]
+    attn_low, depth_early = tie(attn_low, depth_w)
+    pack_one, pack_two, chan = call_mixed(
+        rest_pack_kernel,
+        (),
+        (depth_early, bn_w, pick_wide),
         shards,
         packs,
         [((34, 8, WIDE), F32)],
         [(shard.shape, F32) for shard in shards] + packs,
-        8,
-        4_000_000_000,
+        6,
+        1_000,
     )
     attn_parts = gather_tensor(attn_low)
     attn_parts[2], pack_one = tie(attn_parts[2], pack_one)
@@ -1045,7 +1130,7 @@
             ((WIDE, D), BF16),
         ],
         [pltpu.VMEM((rows, D), BF16), pltpu.VMEM((HEADS, 4 * PAD, D), BF16)],
-        cost=10_000_000_000,
+        cost=1_000,
         limit=56,
         pinned=range(6),
     )(rank_one, lengths, rate_kind, frames.T, table_w, *attn_parts, pick, norm_w)
@@ -1072,7 +1157,7 @@
             ((HEADS, CONV_IN_ROWS, D), BF16), conv_pad, row_f32, row_low,
         ],
         20,
-        18_000_000_000,
+        1_000,
         pinned=(2, 3),
     )
 
@@ -1086,17 +1171,16 @@
         (norm_w, chan, stat),
         (conv, n2, cotangent.T, *two_parts),
         [turn_low, row_f32, chan_f32] + [((groups // 2, pack_two_rows, WIDE), BF16)] * 2,
-        [((8, WIDE), F32), sums_f32, sums_f32],
+        [((2, WIDE), F32), sums_f32, sums_f32],
         [
             chan_f32, row_f32, turn_low, (two_rows, BF16), ((HEADS, PAD, D), BF16),
             ((rows, WIDE), BF16), hid_low, hid_low, row_f32, row_f32, one_f32, row_low, turn_low,
             row_low, turn_low, turn_low, chan_f32, (two_rows, BF16), ((WIDE, D), F32),
         ],
         16,
-        30_000_000_000,
+        1_000,
     )
     reduce_one = Reduction(reduce_steps(send_one, keep_one))
-    bsums = bsums[:2]
     bsums = combine_all(bsums, jnp.add, reduce_one.advance)
 
     convin_block = (HEADS, CONV_IN_ROWS, D)
@@ -1167,15 +1251,16 @@
     )(
         rank_one, rate_kind, base_low, *attn_parts, wout, pick, qkv, probs, mixed, grad_one, sums_one,
     )
-    attn_send = reduce_one.advance(attn_send)
     attn_send = reduce_two.advance(attn_send)
-    reduce_attn = Reduction(reduce_steps(attn_send, attn_keep))
     mine, got = reduce_two.result
-    reduce_down = Reduction(dp_steps(mine, got, 0, LOWER_SPLIT))
-    reduce_up = Reduction(dp_steps(mine, got, LOWER_SPLIT, LOWER_ROWS - LOWER_SPLIT))
-    token = bsums
-    chains = (reduce_attn, reduce_down, reduce_up, reduce_down, reduce_attn, reduce_up, reduce_attn)
-    for chain in chains + (reduce_one, reduce_down, reduce_attn, reduce_up, reduce_down):
+    reduce_attn = Reduction(reduce_steps(attn_send, attn_keep, FOLD[0]))
+    reduce_down = Reduction(dp_steps(mine, got, 0, LOWER_SPLIT, FOLD[1]))
+    token = reduce_attn.advance(bsums)
+    token = reduce_down.advance(token)
+    reduce_up = Reduction(dp_steps(mine, got, LOWER_SPLIT, None, FOLD[2], reduce_down.last))
+    token = reduce_up.advance(token)
+    token = reduce_one.advance(token, reduce_up.last)
+    for chain in (reduce_down, reduce_attn, reduce_up, reduce_down, reduce_attn, reduce_up, reduce_down):
         token = chain.advance(token)
     one_halves = reduce_one.finish()
     down_halves = reduce_down.finish()
@@ -1195,11 +1280,10 @@
             pltpu.VMEM(ffout_w.shape, F32),
         ],
     )
-    token = reduce_attn.advance(tie(token, down[8])[0])
-    token = reduce_up.advance(token)
+    token = reduce_attn.advance(token)
+    token = reduce_attn.advance(token, down[8])
     up_halves = reduce_up.finish()
-    while reduce_attn.result is None:
-        token = reduce_attn.advance(token)
+    attn_halves = reduce_attn.finish()
     up = call_whole(
         lamb_up_kernel,
         (spot_one,),
@@ -1211,7 +1295,6 @@
             pltpu.VMEM(convin_w.shape, F32),
         ],
     )
-    attn_halves = reduce_attn.result
     small = (depth_w, depth_m, depth_v, norm_w, norm_m, norm_v, bn_w, bn_m, bn_v, table_w, table_m, table_v)
     last = call_whole(
         functools.partial(lamb_attn_kernel, 1.0 / groups),

time: 259 us -> 242 us (0.934)
  waiting for transfers between devices: 65.6 us -> 48.2 us
    ppermute x43 -> x47, waiting for transfers between devices: 65.6 us -> 48.2 us  [swap(): return lax.ppermute(value, axis, [(i, i ^ bit) for i in range(size)])]
    ppermute x43 -> x47, starting transfers between devices: 44.2 us -> 42 us  [swap(): return lax.ppermute(value, axis, [(i, i ^ bit) for i in range(size)])]
    pallas_call x7 -> x8, Pallas kernels: 91.4 us -> 92.1 us  [call_mixed(): pl.pallas_call(kernel, in_specs=[SMEM] * len(scalars) + [VMEM] * len(smal...]
  transfers between devices with their start and end apart: 43 -> 47, of which waited for: 22 -> 26; matrix products, arithmetic and copies ran while one was open for 3% -> 4% of each run, Pallas kernels for 36% -> 40%
where the time goes in v3:
time: 242 us; the launch traced here: 237 us
  Pallas kernels  129 us (53%)
  waiting for transfers between devices  48.2 us (20%)
  starting transfers between devices  42 us (17%)
  other arithmetic  8.72 us (4%)
  local copies, waits for them, and re-layouts  5.69 us (2%)
  between operations  3.73 us (2%)
    pallas_call x8, Pallas kernels, call_mixed(): pl.pallas_call(kernel, in_specs=[SMEM] * len(scalars) + [VMEM] * len(smal...  92.1 us
    ppermute x47, waiting for transfers between devices, swap(): return lax.ppermute(value, axis, [(i, i ^ bit) for i in range(size)])  48.2 us
    ppermute x47, starting transfers between devices, swap(): return lax.ppermute(value, axis, [(i, i ^ bit) for i in range(size)])  42 us
    pallas_call x1, Pallas kernels, body(): call(attn_bwd_kernel, utts, [SMEM, SMEM, rowspec] + attn_specs + [whole((...  13 us
    pallas_call x3, Pallas kernels, call_whole(): pl.pallas_call(kernel, in_specs=[SMEM] * len(scalars) + [pl.BlockSpec(mem...  12.5 us
    pallas_call x1, Pallas kernels, body(): call(attn_fwd_kernel, utts, [SMEM, SMEM, SMEM, turnspec, whole((RATES, D)...  11.5 us
    convert_element_type x19, other arithmetic, add_low(): return (one.astype(F32) + two.astype(F32)).astype(BF16)  4.98 us
  transfers between devices with their start and end apart: 47, of which 26 were waited for; matrix products, arithmetic and copies ran while one was open for 4% of the time, Pallas kernels for 40%

profile of v3, /device:TPU:0, one launch (start us, length us, event | category | flops | bytes accessed | tf_op | source)
XLA Modules:
  0.0 237.5 jit_solution(17001429956834280254)
XLA Ops:
  0.7 2.3 shard_map.560.w0
  2.9 3.0 %collective-permute-start = (bf16[384,384]{1,0:T(8,128)(2,1)}, bf16[384,384]{1,0:T(8,128)(2,1)S(1)}, u32[]{:S(2)}, u32[]{:S(2)}) collective-permute-start(bf16[384,384]{1,0:T(8,128)(2,1)} %shard_map.560.w0), channel_id=1, source_target_pairs={{0,2},{1,3},{2,0},{3,1},{4,6},{5,7},{6,4},{7,5},{8,10},{9,11},{10,... | collective-permute-start | bytes 884744 | tf_op jit(solution)/shard_map/ppermute | solution.py:908
  5.9 6.6 %shard_map.561 = (bf16[864,384]{1,0:T(8,128)(2,1)}, bf16[768,384]{1,0:T(8,128)(2,1)}, f32[34,8,384]{2,1,0:T(8,128)}) custom-call(f32[31,324]{1,0:T(8,128)} %depth_w.1, f32[2,324]{1,0:T(2,128)} %bn_w.1, f32[384,324]{1,0:T(8,128)} %constant.44.clone.pick, f32[324,2,324]{2,1,0:T(2,128)} %bitcast.69, f32[324,2,324]{2,1,0:T(2,128)} %bitcast.66, ...), custom_call_target="tpu_custom_call" | custom-call | flops 1000 | bytes 1 | tf_op jit(solution)/shard_map/pallas_call | solution.py:895
  17.7 11.5 %shard_map.562 = (bf16[992,324]{1,0:T(8,128)(2,1)}, bf16[2,4,288,496]{3,2,1,0:T(8,128)(2,1)}, bf16[2,4,496,496]{3,2,1,0:T(8,128)(2,1)}, bf16[2,384,496]{2,1,0:T(...) custom-call(s32[1]{0:T(128)} %bitcast.rank_ref, s32[8]{0:T(128)} %len_ref.7, ...), custom_call_target="tpu_custom_call" | custom-call | flops 1000 | bytes 1 | tf_op jit(solution)/shard_map/pallas_call | solution.py:1118
  32.4 16.2 %shard_map.563 = (bf16[4,992,324]{2,1,0:T(8,128)(2,1)}, bf16[4,992,324]{2,1,0:T(8,128)(2,1)}, f32[992,324]{1,0:T(8,128)}, f32[992,1]{1,0:T(8,128)}, f32[992,384]...) custom-call(s32[1]{0:T(128)} %bitcast.rank_ref, s32[8]{0:T(128)} %len_ref.7, ...), custom_call_target="tpu_custom_call" | custom-call | flops 1000 | bytes 1 | tf_op jit(solution)/shard_map/pallas_call | solution.py:895
  50.6 2.2 collective-permute-done.8
  60.6 2.6 %collective-permute-start.12 = (f32[3,384]{1,0:T(4,128)S(1)}, f32[3,384]{1,0:T(4,128)S(1)}, u32[]{:S(2)}, u32[]{:S(2)}) collective-permute-start(f32[3,384]{1,0:T(4,128)S(1)} %pad_maximum_fusion.1), channel_id=1, source_target_pairs={{0,16},{4,20},{8,24},{12,28},{16,0},{20,4},{24,8},{28,12},{1,17},{... | collective-permute-start | bytes 13832 | tf_op jit(solution)/shard_map/ppermute | solution.py:908
  65.1 3.5 %collective-permute-done.13 = f32[3,384]{1,0:T(4,128)S(1)} collective-permute-done((f32[3,384]{1,0:T(4,128)S(1)}, f32[3,384]{1,0:T(4,128)S(1)}, u32[]{:S(2)}, u32[]{:S(2)}) %collective-permute-start.13) | collective-permute-done | bytes 4640 | tf_op jit(solution)/shard_map/ppermute | solution.py:908
  70.3 24.9 %shard_map.564 = (bf16[324,992]{1,0:T(8,128)(2,1)}, f32[992,324]{1,0:T(8,128)}, f32[992,384]{1,0:T(8,128)}, bf16[2,768,384]{2,1,0:T(8,128)(2,1)}, bf16[2,768,384...) custom-call(s32[1]{0:T(128)} %bitcast.rank_ref, s32[8]{0:T(128)} %len_ref.7, ...), custom_call_target="tpu_custom_call" | custom-call | flops 1000 | bytes 1 | tf_op jit(solution)/shard_map/pallas_call | solution.py:895
  104.8 3.6 %collective-permute-start.23 = (f32[2,384]{1,0:T(2,128)S(1)}, f32[2,384]{1,0:T(2,128)S(1)}, u32[]{:S(2)}, u32[]{:S(2)}) collective-permute-start(f32[2,384]{1,0:T(2,128)S(1)} %add.294), channel_id=1, source_target_pairs={{0,24},{4,28},{8,16},{12,20},{16,8},{20,12},{24,0},{28,4},{1,25},{... | collective-permute-start | bytes 9224 | tf_op jit(solution)/shard_map/ppermute | solution.py:908
  111.9 17.0 %shard_map.565 = (f32[992,324]{1,0:T(8,128)}, bf16[4,192,324]{2,1,0:T(8,128)(2,1)}, bf16[48,324]{1,0:T(8,128)(2,1)}) custom-call(s32[1]{0:T(128)} %bitcast.rank_ref, s32[8]{0:T(128)} %len_ref.7, f32[8,324]{1,0:T(8,128)} %norm_w.1, f32[34,8,384]{2,1,0:T(8,128)} %get-tuple-element.132.chan, f32[3,384]{1,0:T(4,128)} %pad_maximum_fusion.2.stat, ...), custom_call_target="tpu_custom_call" | custom-call | flops 14000000000 | bytes 14000000 | tf_op jit(solution)/shard_map/pallas_call | solution.py:895
  130.6 11.7 %shard_map.566 = (bf16[4,992,324]{2,1,0:T(8,128)(2,1)}, bf16[2,928,384]{2,1,0:T(8,128)(2,1)}, bf16[2,928,384]{2,1,0:T(8,128)(2,1)}) custom-call(f32[8,324]{1,0:T(8,128)} %norm_w.1, bf16[4,192,324]{2,1,0:T(8,128)(2,1)} %get-tuple-element.168.cin_grad, bf16[48,324]{1,0:T(8,128)(2,1)} %get-tuple-element.169.vectors, f32[992,324]{1,0:T(8,128)} %get-tuple-element.166.up_in, ...), custom_call_target="tpu_custom_call" | custom-call | flops 12000000000 | bytes 12000000 | tf_op jit(solution)/shard_map/pallas_call | solution.py:895
  142.6 8.5 %shard_map.567 = (f32[992,324]{1,0:T(8,128)}, f32[8,324]{1,0:T(8,128)}) custom-call(f32[8,324]{1,0:T(8,128)} %norm_w.1, f32[992,324]{1,0:T(8,128)} %get-tuple-element.166.up_in, f32[992,324]{1,0:T(8,128)} %get-tuple-element.140.n1_in, f32[992,1]{1,0:T(8,128)} %get-tuple-element.167.s1_in, bf16[864,384]{1,0:T(8,128)(2,1)} %get-tuple-element.135.w0, ...), custom_call_target="tpu_custom_call" | custom-call | flops 8000000000 | bytes 8000000 | tf_op jit(solution)/shard_map/pallas_call | solution.py:895
  152.8 2.1 collective-permute-start.28
  158.1 13.0 %shard_map.568 = (f32[324,992]{1,0:T(8,128)}, bf16[2,384,384]{2,1,0:T(8,128)(2,1)S(1)}, bf16[2,384,384]{2,1,0:T(8,128)(2,1)S(1)}) custom-call(s32[1]{0:T(128)} %bitcast.rank_ref, s32[8]{0:T(128)S(1)} %copy-done.30, bf16[992,324]{1,0:T(8,128)(2,1)S(1)} %copy-done.34, bf16[384,384]{1,0:T(8,128)(2,1)} %shard_map.560.w0, bf16[384,384]{1,0:T(8,128)(2,1)} %copy-done.48, ...), custom_call_target="tpu_custom_call" | custom-call | flops 16000000000 | bytes 16000000 | tf_op jit(solution)/shard_map/pallas_call | solution.py:1236
  173.8 4.6 %collective-permute-done.30 = bf16[192,384]{1,0:T(8,128)(2,1)S(1)} collective-permute-done((bf16[192,384]{1,0:T(8,128)(2,1)S(1)}, bf16[192,384]{1,0:T(8,128)(2,1)S(1)}, u32[]{:S(2)}, u32[]{:S(2)}) %collective-permute-start.30) | collective-permute-done | bytes 147488 | tf_op jit(solution)/shard_map/ppermute | solution.py:908
  180.9 3.9 %collective-permute-done.33 = bf16[192,384]{1,0:T(8,128)(2,1)S(1)} collective-permute-done((bf16[192,384]{1,0:T(8,128)(2,1)S(1)}, bf16[192,384]{1,0:T(8,128)(2,1)S(1)}, u32[]{:S(2)}, u32[]{:S(2)}) %collective-permute-start.33) | collective-permute-done | bytes 147488 | tf_op jit(solution)/shard_map/ppermute | solution.py:908
  198.0 5.5 %collective-permute-done.41 = bf16[192,384]{1,0:T(8,128)(2,1)S(1)} collective-permute-done((bf16[192,384]{1,0:T(8,128)(2,1)S(1)}, bf16[192,384]{1,0:T(8,128)(2,1)S(1)}, u32[]{:S(2)}, u32[]{:S(2)}) %collective-permute-start.41) | collective-permute-done | bytes 147488 | tf_op jit(solution)/shard_map/ppermute | solution.py:908
  204.0 4.1 %shard_map.569 = (f32[324,2,324]{2,1,0:T(2,128)}, f32[324,2,324]{2,1,0:T(2,128)}, f32[324,2,324]{2,1,0:T(2,128)S(1)}, f32[81,324]{1,0:T(8,128)}, f32[81,324]{1,0...) custom-call(s32[1]{0:T(128)} %bitcast.12.spot_ref, ...), custom_call_target="tpu_custom_call" | custom-call | flops 1000000 | bytes 2000000 | tf_op jit(solution)/shard_map/pallas_call | solution.py:879
  211.6 6.1 %collective-permute-done.43 = bf16[192,384]{1,0:T(8,128)(2,1)S(1)} collective-permute-done((bf16[192,384]{1,0:T(8,128)(2,1)S(1)}, bf16[192,384]{1,0:T(8,128)(2,1)S(1)}, u32[]{:S(2)}, u32[]{:S(2)}) %collective-permute-start.43) | collective-permute-done | bytes 147488 | tf_op jit(solution)/shard_map/ppermute | solution.py:908
  218.6 5.7 %shard_map.570 = (f32[324,2,324]{2,1,0:T(2,128)}, f32[324,2,324]{2,1,0:T(2,128)}, f32[324,2,324]{2,1,0:T(2,128)S(1)}, f32[81,2,324]{2,1,0:T(2,128)}, f32[81,2,32...) custom-call(s32[1]{0:T(128)} %bitcast.12.spot_ref, bf16[272,384]{1,0:T(8,128)(2,1)S(1)} %add_convert_fusion.11.mine, ...), custom_call_target="tpu_custom_call" | custom-call | flops 1000000 | bytes 2000000 | tf_op jit(solution)/shard_map/pallas_call | solution.py:879
  224.5 2.6 %shard_map.571 = (f32[81,4,324]{2,1,0:T(4,128)}, f32[3,81,324]{2,1,0:T(8,128)}, f32[81,324]{1,0:T(8,128)}, f32[81,4,324]{2,1,0:T(4,128)S(1)}, f32[31,324]{1,0:T(...) custom-call(s32[1]{0:T(128)} %bitcast.12.spot_ref, ...), custom_call_target="tpu_custom_call" | custom-call | flops 1000000 | bytes 2000000 | tf_op jit(solution)/shard_map/pallas_call | solution.py:879
  229.1 3.0 %collective-permute-done.46 = f32[32,128]{1,0:T(8,128)S(1)} collective-permute-done((f32[32,128]{1,0:T(8,128)S(1)}, f32[32,128]{1,0:T(8,128)S(1)}, u32[]{:S(2)}, u32[]{:S(2)}) %collective-permute-start.46) | collective-permute-done | bytes 16416 | tf_op jit(solution)/shard_map/ppermute | solution.py:908
  232.2 5.1 %shard_map.572 = (f32[324,2,324]{2,1,0:T(2,128)}, f32[324,2,324]{2,1,0:T(2,128)}, f32[81,4,324]{2,1,0:T(4,128)}, f32[81,2,324]{2,1,0:T(2,128)}, f32[81,324]{1,0:...) custom-call(f32[32,128]{1,0:T(8,128)S(1)} %add.343.sums, f32[324,2,324]{2,1,0:T(2,128)S(1)} %bitcast.71, ...), custom_call_target="tpu_custom_call" | custom-call | flops 1000000 | bytes 1000 | tf_op jit(solution)/shard_map/pallas_call | solution.py:895
  (221 shorter events, 64.4 us)
Async XLA Ops:
  2.9 10.2 %collective-permute-start = (bf16[384,384]{1,0:T(8,128)(2,1)}, bf16[384,384]{1,0:T(8,128)(2,1)S(1)}, u32[]{:S(2)}, u32[]{:S(2)}) collective-permute-start(bf16[384,384]{1,0:T(8,128)(2,1)} %shard_map.560.w0), channel_id=1, source_target_pairs={{0,2},{1,3},{2,0},{3,1},{4,6},{5,7},{6,4},{7,5},{8,10},{9,11},{10,... | collective-permute-start | bytes 884744 | tf_op jit(solution)/shard_map/ppermute | solution.py:908
  13.2 16.3 %collective-permute-start.1 = (bf16[864,384]{1,0:T(8,128)(2,1)}, bf16[864,384]{1,0:T(8,128)(2,1)S(1)}, u32[]{:S(2)}, u32[]{:S(2)}) collective-permute-start(bf16[864,384]{1,0:T(8,128)(2,1)} %get-tuple-element.135.w0), channel_id=1, source_target_pairs={{0,2},{1,3},{2,0},{3,1},{4,6},{5,7},{6,4},{7,5},{8,10},{9,11},{10,... | collective-permute-start | bytes 1990664 | tf_op jit(solution)/shard_map/ppermute | solution.py:908
  15.4 15.6 %collective-permute-start.5 = (bf16[864,384]{1,0:T(8,128)(2,1)}, bf16[864,384]{1,0:T(8,128)(2,1)S(1)}, u32[]{:S(2)}, u32[]{:S(2)}) collective-permute-start(bf16[864,384]{1,0:T(8,128)(2,1)} %get-tuple-element.135.w0), channel_id=1, source_target_pairs={{0,1},{1,0},{2,3},{3,2},{4,5},{5,4},{6,7},{7,6},{8,9},{9,8},{10,11... | collective-permute-start | bytes 1990664 | tf_op jit(solution)/shard_map/ppermute | solution.py:908
  29.7 18.9 %collective-permute-start.4 = (bf16[768,384]{1,0:T(8,128)(2,1)S(1)}, bf16[768,384]{1,0:T(8,128)(2,1)S(1)}, u32[]{:S(2)}, u32[]{:S(2)}) collective-permute-start(bf16[768,384]{1,0:T(8,128)(2,1)S(1)} %copy-done.43), channel_id=1, source_target_pairs={{0,2},{1,3},{2,0},{3,1},{4,6},{5,7},{6,4},{7,5},{8,10},{9,11},{10,... | collective-permute-start | bytes 1769480 | tf_op jit(solution)/shard_map/ppermute | solution.py:908
  56.8 12.5 %collective-permute-start.14 = (bf16[768,384]{1,0:T(8,128)(2,1)S(1)}, bf16[768,384]{1,0:T(8,128)(2,1)S(1)}, u32[]{:S(2)}, u32[]{:S(2)}) collective-permute-start(bf16[768,384]{1,0:T(8,128)(2,1)S(1)} %copy-done.43), channel_id=1, source_target_pairs={{0,1},{1,0},{2,3},{3,2},{4,5},{5,4},{6,7},{7,6},{8,9},{9,8},{10,11... | collective-permute-start | bytes 1769480 | tf_op jit(solution)/shard_map/ppermute | solution.py:908
  56.8 12.5 %collective-permute-start.15 = (bf16[768,384]{1,0:T(8,128)(2,1)S(1)}, bf16[768,384]{1,0:T(8,128)(2,1)S(1)}, u32[]{:S(2)}, u32[]{:S(2)}) collective-permute-start(bf16[768,384]{1,0:T(8,128)(2,1)S(1)} %collective-permute-done.4.w2), channel_id=1, source_target_pairs={{0,1},{1,0},{2,3},{3,2},{4,5},{5,4},{6,7},{7,6},{8,9},{9,8},{10,11... | collective-permute-start | bytes 1769480 | tf_op jit(solution)/shard_map/ppermute | solution.py:908
  104.0 7.3 %collective-permute-start.21 = (f32[2,384]{1,0:T(2,128)S(1)}, f32[2,384]{1,0:T(2,128)S(1)}, u32[]{:S(2)}, u32[]{:S(2)}) collective-permute-start(f32[2,384]{1,0:T(2,128)S(1)} %add.294), channel_id=1, source_target_pairs={{0,8},{4,12},{8,0},{12,4},{16,24},{20,28},{24,16},{28,20},{1,9},{5... | collective-permute-start | bytes 9224 | tf_op jit(solution)/shard_map/ppermute | solution.py:908
  104.0 7.3 %collective-permute-start.22 = (f32[2,384]{1,0:T(2,128)S(1)}, f32[2,384]{1,0:T(2,128)S(1)}, u32[]{:S(2)}, u32[]{:S(2)}) collective-permute-start(f32[2,384]{1,0:T(2,128)S(1)} %add.294), channel_id=1, source_target_pairs={{0,16},{4,20},{8,24},{12,28},{16,0},{20,4},{24,8},{28,12},{1,17},{... | collective-permute-start | bytes 9224 | tf_op jit(solution)/shard_map/ppermute | solution.py:908
  110.0 19.0 %collective-permute-start.24 = (bf16[768,384]{1,0:T(8,128)(2,1)S(1)}, bf16[768,384]{1,0:T(8,128)(2,1)S(1)}, u32[]{:S(2)}, u32[]{:S(2)}) collective-permute-start(bf16[768,384]{1,0:T(8,128)(2,1)S(1)} %get-tuple-element.237), channel_id=1, source_target_pairs={{0,2},{1,3},{2,0},{3,1},{4,6},{5,7},{6,4},{7,5},{8,10},{9,11},{10,... | collective-permute-start | bytes 1769480 | tf_op jit(solution)/shard_map/ppermute | solution.py:908
  129.0 13.3 %collective-permute-start.25 = (bf16[384,384]{1,0:T(8,128)(2,1)S(1)}, bf16[384,384]{1,0:T(8,128)(2,1)S(1)}, u32[]{:S(2)}, u32[]{:S(2)}) collective-permute-start(bf16[384,384]{1,0:T(8,128)(2,1)S(1)} %fusion.3), channel_id=1, source_target_pairs={{0,4},{4,0},{8,12},{12,8},{16,20},{20,16},{24,28},{28,24},{1,5},{5... | collective-permute-start | bytes 884744 | tf_op jit(solution)/shard_map/ppermute | solution.py:908
  142.3 12.6 %collective-permute-start.27 = (bf16[2,928,384]{2,1,0:T(8,128)(2,1)}, bf16[2,928,384]{2,1,0:T(8,128)(2,1)S(1)}, u32[]{:S(2)}, u32[]{:S(2)}) collective-permute-start(bf16[2,928,384]{2,1,0:T(8,128)(2,1)} %get-tuple-element.178), channel_id=1, source_target_pairs={{0,1},{1,0},{2,3},{3,2},{4,5},{5,4},{6,7},{7,6},{8,9},{9,8},{10,11... | collective-permute-start | bytes 4276232 | tf_op jit(solution)/shard_map/ppermute | solution.py:908
  142.5 9.5 %collective-permute-start.26 = (bf16[384,384]{1,0:T(8,128)(2,1)S(1)}, bf16[384,384]{1,0:T(8,128)(2,1)S(1)}, u32[]{:S(2)}, u32[]{:S(2)}) collective-permute-start(bf16[384,384]{1,0:T(8,128)(2,1)S(1)} %add_convert_fusion.10), channel_id=1, source_target_pairs={{0,8},{4,12},{8,0},{12,4},{16,24},{20,28},{24,16},{28,20},{1,9},{5... | collective-permute-start | bytes 884744 | tf_op jit(solution)/shard_map/ppermute | solution.py:908
  152.8 21.0 %collective-permute-start.28 = (bf16[384,384]{1,0:T(8,128)(2,1)}, bf16[384,384]{1,0:T(8,128)(2,1)}, u32[]{:S(2)}, u32[]{:S(2)}) collective-permute-start(bf16[384,384]{1,0:T(8,128)(2,1)} %add_convert_fusion.9), channel_id=1, source_target_pairs={{0,16},{4,20},{8,24},{12,28},{16,0},{20,4},{24,8},{28,12},{1,17},{... | collective-permute-start | bytes 884744 | tf_op jit(solution)/shard_map/ppermute | solution.py:908
  155.3 17.9 %collective-permute-start.29 = (bf16[928,384]{1,0:T(8,128)(2,1)S(1)}, bf16[928,384]{1,0:T(8,128)(2,1)S(1)}, u32[]{:S(2)}, u32[]{:S(2)}) collective-permute-start(bf16[928,384]{1,0:T(8,128)(2,1)S(1)} %get-tuple-element.235), channel_id=1, source_target_pairs={{0,2},{1,3},{2,0},{3,1},{4,6},{5,7},{6,4},{7,5},{8,10},{9,11},{10,... | collective-permute-start | bytes 2138120 | tf_op jit(solution)/shard_map/ppermute | solution.py:908
  173.8 15.4 %collective-permute-start.39 = (bf16[2,384,384]{2,1,0:T(8,128)(2,1)S(1)}, bf16[2,384,384]{2,1,0:T(8,128)(2,1)S(1)}, u32[]{:S(2)}, u32[]{:S(2)}) collective-permute-start(bf16[2,384,384]{2,1,0:T(8,128)(2,1)S(1)} %get-tuple-element.191), channel_id=1, source_target_pairs={{0,1},{1,0},{2,3},{3,2},{4,5},{5,4},{6,7},{7,6},{8,9},{9,8},{10,11... | collective-permute-start | bytes 1769480 | tf_op jit(solution)/shard_map/ppermute | solution.py:908
  184.9 7.8 %collective-permute-start.34 = (bf16[192,384]{1,0:T(8,128)(2,1)S(1)}, bf16[192,384]{1,0:T(8,128)(2,1)S(1)}, u32[]{:S(2)}, u32[]{:S(2)}) collective-permute-start(bf16[192,384]{1,0:T(8,128)(2,1)S(1)} %add_convert_fusion.19), channel_id=1, source_target_pairs={{0,16},{4,20},{8,24},{12,28},{16,0},{20,4},{24,8},{28,12},{1,17},{... | collective-permute-start | bytes 442376 | tf_op jit(solution)/shard_map/ppermute | solution.py:908
  186.8 7.4 %collective-permute-start.36 = (bf16[272,384]{1,0:T(8,128)(2,1)S(1)}, bf16[272,384]{1,0:T(8,128)(2,1)S(1)}, u32[]{:S(2)}, u32[]{:S(2)}) collective-permute-start(bf16[272,384]{1,0:T(8,128)(2,1)S(1)} %add_convert_fusion.13), channel_id=1, source_target_pairs={{0,8},{4,12},{8,0},{12,4},{16,24},{20,28},{24,16},{28,20},{1,9},{5... | collective-permute-start | bytes 626696 | tf_op jit(solution)/shard_map/ppermute | solution.py:908
  189.3 6.8 %collective-permute-start.40 = (bf16[384,384]{1,0:T(8,128)(2,1)S(1)}, bf16[384,384]{1,0:T(8,128)(2,1)S(1)}, u32[]{:S(2)}, u32[]{:S(2)}) collective-permute-start(bf16[384,384]{1,0:T(8,128)(2,1)S(1)} %get-tuple-element.239), channel_id=1, source_target_pairs={{0,2},{1,3},{2,0},{3,1},{4,6},{5,7},{6,4},{7,5},{8,10},{9,11},{10,... | collective-permute-start | bytes 884744 | tf_op jit(solution)/shard_map/ppermute | solution.py:908
  192.0 11.9 %collective-permute-start.32 = (bf16[384,384]{1,0:T(8,128)(2,1)S(1)}, bf16[384,384]{1,0:T(8,128)(2,1)S(1)}, u32[]{:S(2)}, u32[]{:S(2)}) collective-permute-start(bf16[384,384]{1,0:T(8,128)(2,1)S(1)} %add_convert_fusion.7.one_mine), channel_id=1, source_target_pairs={{0,4},{4,0},{8,12},{12,8},{16,20},{20,16},{24,28},{28,24},{1,5},{5... | collective-permute-start | bytes 884744 | tf_op jit(solution)/shard_map/ppermute | solution.py:908
  192.7 11.2 %collective-permute-start.35 = (bf16[192,384]{1,0:T(8,128)(2,1)S(1)}, bf16[192,384]{1,0:T(8,128)(2,1)S(1)}, u32[]{:S(2)}, u32[]{:S(2)}) collective-permute-start(bf16[192,384]{1,0:T(8,128)(2,1)S(1)} %add_convert_fusion.18.two_mine), channel_id=1, source_target_pairs={{0,4},{4,0},{8,12},{12,8},{16,20},{20,16},{24,28},{28,24},{1,5},{5... | collective-permute-start | bytes 442376 | tf_op jit(solution)/shard_map/ppermute | solution.py:908
  196.1 7.4 %collective-permute-start.41 = (bf16[192,384]{1,0:T(8,128)(2,1)S(1)}, bf16[192,384]{1,0:T(8,128)(2,1)S(1)}, u32[]{:S(2)}, u32[]{:S(2)}) collective-permute-start(bf16[192,384]{1,0:T(8,128)(2,1)S(1)} %fusion.7), channel_id=1, source_target_pairs={{0,4},{4,0},{8,12},{12,8},{16,20},{20,16},{24,28},{28,24},{1,5},{5... | collective-permute-start | bytes 442376 | tf_op jit(solution)/shard_map/ppermute | solution.py:908
  196.8 12.6 %collective-permute-start.37 = (bf16[272,384]{1,0:T(8,128)(2,1)S(1)}, bf16[272,384]{1,0:T(8,128)(2,1)S(1)}, u32[]{:S(2)}, u32[]{:S(2)}) collective-permute-start(bf16[272,384]{1,0:T(8,128)(2,1)S(1)} %add_convert_fusion.12), channel_id=1, source_target_pairs={{0,16},{4,20},{8,24},{12,28},{16,0},{20,4},{24,8},{28,12},{1,17},{... | collective-permute-start | bytes 626696 | tf_op jit(solution)/shard_map/ppermute | solution.py:908
  210.0 7.7 %collective-permute-start.43 = (bf16[192,384]{1,0:T(8,128)(2,1)S(1)}, bf16[192,384]{1,0:T(8,128)(2,1)S(1)}, u32[]{:S(2)}, u32[]{:S(2)}) collective-permute-start(bf16[192,384]{1,0:T(8,128)(2,1)S(1)} %add_convert_fusion.16), channel_id=1, source_target_pairs={{0,16},{4,20},{8,24},{12,28},{16,0},{20,4},{24,8},{28,12},{1,17},{... | collective-permute-start | bytes 442376 | tf_op jit(solution)/shard_map/ppermute | solution.py:908
  211.1 7.3 %collective-permute-start.38 = (bf16[272,384]{1,0:T(8,128)(2,1)S(1)}, bf16[272,384]{1,0:T(8,128)(2,1)S(1)}, u32[]{:S(2)}, u32[]{:S(2)}) collective-permute-start(bf16[272,384]{1,0:T(8,128)(2,1)S(1)} %add_convert_fusion.11.mine), channel_id=1, source_target_pairs={{0,4},{4,0},{8,12},{12,8},{16,20},{20,16},{24,28},{28,24},{1,5},{5... | collective-permute-start | bytes 626696 | tf_op jit(solution)/shard_map/ppermute | solution.py:908
  (73 other events, 474.0 us)

commit v4 on v3

--- a/solution.py
+++ b/solution.py
@@ -288,7 +288,7 @@
     copies.finish()
 
 
-def ffn_forward(z_low, weights, hid, slope, acc, done=None):
+def ffn_forward(z_low, weights, hid, slope, acc, ready=None, done=None):
     def block(p, carry):
         pre = dot_nn(z_low[...], weights[p, 0:D, 0:D])
         sig = sigmoid(pre)
@@ -303,11 +303,12 @@
         lax.fori_loop(0, HEADS, block, 0)
     else:
         for p in range(HEADS):
+            ready(p)
             block(p, 0)
             done(p)
 
 
-def ffn_backward(up_low, up_turn, z_turn, weights, hid, slope, acc, grads, up_row, down_row, done=None):
+def ffn_backward(up_low, up_turn, z_turn, weights, hid, slope, acc, grads, up_row, down_row, ready=None, done=None):
     def block(p, carry):
         back = dot_nt(up_low[...], weights[p, FF_ROWS : FF_ROWS + D, 0:D])
         pre_grad = (back * slope[p].astype(F32)).astype(BF16)
@@ -323,6 +324,7 @@
         lax.fori_loop(0, HEADS, block, 0)
     else:
         for p in range(HEADS):
+            ready(p)
             block(p, 0)
             done(p)
 
@@ -341,25 +343,32 @@
     copies = Copies(sems)
     rank = rank_ref[0]
     rows = n1_in.shape[0]
-    loads = [copies.start(n1_in, n1)]
-    loads += [copies.start(part, weights.at[p]) for p, part in enumerate((w0, w1, w2, w3))]
-    for load in loads:
-        load.wait()
+    parts = (w0, w1, w2, w3)
+    first = copies.start(n1_in, n1)
+    ffn_rows, conv_rows = pl.ds(0, TAIL), pl.ds(TAIL, CONV_IN_ROWS)
+    loads = [copies.start(part.at[ffn_rows], weights.at[p, ffn_rows]) for p, part in enumerate(parts)]
+    later = [copies.start(part.at[conv_rows], weights.at[p, conv_rows]) for p, part in enumerate(parts)]
+    first.wait()
     z = n1[...] * norm[0:1, :] + norm[4:5, :]
     acc[...] = z
     z_low[...] = z.astype(BF16)
 
+    def ready(p):
+        loads[p].wait()
+
     def done(p):
         copies.out(hid.at[p], hid_out.at[p])
         copies.out(slope.at[p], slope_out.at[p])
 
-    ffn_forward(z_low, weights, hid, slope, acc, done)
+    ffn_forward(z_low, weights, hid, slope, acc, ready, done)
     normal, inv = ln_forward(acc[...])
     n2[...] = normal
     s2[...] = inv
     copies.out(n2, n2_out)
     copies.out(s2, s2_out)
     z_low[...] = (normal * norm[1:2, :] + norm[5:6, :]).astype(BF16)
+    for load in later:
+        load.wait()
     for p in range(HEADS):
         conv_w[p ^ rank] = weights[p, TAIL : TAIL + CONV_IN_ROWS, 0:D]
     value[...] = dot_nt(z_low[...], conv_w[:, 0:PAD, :].reshape(WIDE, D))
@@ -407,8 +416,11 @@
     rank = rank_ref[0]
     rows = conv_in.shape[0]
     utts = rows // SLOT
-    loads = [copies.start(part, weights.at[p]) for p, part in enumerate((w0, w1, w2, w3))]
+    parts = (w0, w1, w2, w3)
+    ffn_rows, conv_rows = pl.ds(0, TAIL), pl.ds(TAIL, PAD)
+    loads = [copies.start(part.at[conv_rows], weights.at[p, conv_rows]) for p, part in enumerate(parts)]
     loads += [copies.start(conv_in, conv), copies.start(n2_in, n2)]
+    later = [copies.start(part.at[ffn_rows], weights.at[p, ffn_rows]) for p, part in enumerate(parts)]
     cot_load = copies.start(cot_in, cot)
     for load in loads:
         load.wait()
@@ -433,6 +445,8 @@
 
     each_utt(rows, utterance_fwd)
     z_turn[...] = z_low[...].T
+    for load in later:
+        load.wait()
     ffn_forward(z_low, weights, hid, slope, acc)
     normal, inv = ln_forward(acc[...])
     gain = norm[3:4, :]
@@ -571,19 +585,24 @@
     loads += [
         copies.start(part.at[down], weights.at[p, down]) for p, part in enumerate((w0, w1, w2, w3))
     ]
-    loads += [copies.start(slope_in, slope), copies.start(hid_in, hid)]
+    later = [
+        (copies.start(slope_in.at[p], slope.at[p]), copies.start(hid_in.at[p], hid.at[p]))
+        for p in range(HEADS)
+    ]
     for load in loads[:2]:
         load.wait()
     up_low[...] = up[...].astype(BF16)
     up_turn[...] = up_low[...].T
     z_turn[...] = (n1[...] * norm[0:1, :] + norm[4:5, :]).astype(BF16).T
-    for load in loads[2:]:
-        load.wait()
+
+    def ready(p):
+        for load in (loads[2 + p], *later[p]):
+            load.wait()
 
     def done(p):
         copies.out(slope.at[p], pre_out.at[p])
 
-    ffn_backward(up_low, up_turn, z_turn, weights, hid, slope, None, grads, LOWER_UP, 0, done)
+    ffn_backward(up_low, up_turn, z_turn, weights, hid, slope, None, grads, LOWER_UP, 0, ready, done)
     for p in range(HEADS):
         grads[p, LOWER_CONV : LOWER_CONV + CONV_IN_ROWS, 0:D] = cin_grad[p]
         grads[p, LOWER_VEC : LOWER_VEC + VECTOR_ROWS, 0:D] = vectors[...]
@@ -1156,7 +1175,7 @@
             row_f32, (one_rows, BF16), hid_low, hid_low, row_f32, one_f32, chan_f32, chan_f32, chan_f32,
             ((HEADS, CONV_IN_ROWS, D), BF16), conv_pad, row_f32, row_low,
         ],
-        20,
+        24,
         1_000,
         pinned=(2, 3),
     )
@@ -1177,7 +1196,7 @@
             ((rows, WIDE), BF16), hid_low, hid_low, row_f32, row_f32, one_f32, row_low, turn_low,
             row_low, turn_low, turn_low, chan_f32, (two_rows, BF16), ((WIDE, D), F32),
         ],
-        16,
+        20,
         1_000,
     )
     reduce_one = Reduction(reduce_steps(send_one, keep_one))
@@ -1215,7 +1234,7 @@
             row_f32, row_f32, ((groups, TAIL, WIDE), BF16), hid_low, hid_low, row_low, turn_low,
             turn_low, (lower_rows, BF16),
         ],
-        16,
+        24,
         12_000_000_000,
     )
     reduce_two = Reduction(tensor_steps(send_two, keep_two))

time: 242 us -> 241 us (level)
  no operation moved by 1% of the time
where the time goes in v4:
time: 241 us; the launch traced here: 237 us
  Pallas kernels  128 us (53%)
  waiting for transfers between devices  48.3 us (20%)
  starting transfers between devices  41.9 us (17%)
  other arithmetic  8.72 us (4%)
  local copies, waits for them, and re-layouts  5.69 us (2%)
  between operations  3.73 us (2%)
    pallas_call x8, Pallas kernels, call_mixed(): pl.pallas_call(kernel, in_specs=[SMEM] * len(scalars) + [VMEM] * len(smal...  91.4 us
    ppermute x47, waiting for transfers between devices, swap(): return lax.ppermute(value, axis, [(i, i ^ bit) for i in range(size)])  48.3 us
    ppermute x47, starting transfers between devices, swap(): return lax.ppermute(value, axis, [(i, i ^ bit) for i in range(size)])  41.9 us
    pallas_call x1, Pallas kernels, body(): call(attn_bwd_kernel, utts, [SMEM, SMEM, rowspec] + attn_specs + [whole((...  13 us
    pallas_call x3, Pallas kernels, call_whole(): pl.pallas_call(kernel, in_specs=[SMEM] * len(scalars) + [pl.BlockSpec(mem...  12.5 us
    pallas_call x1, Pallas kernels, body(): call(attn_fwd_kernel, utts, [SMEM, SMEM, SMEM, turnspec, whole((RATES, D)...  11.5 us
    convert_element_type x19, other arithmetic, add_low(): return (one.astype(F32) + two.astype(F32)).astype(BF16)  4.98 us
  transfers between devices with their start and end apart: 47, of which 26 were waited for; matrix products, arithmetic and copies ran while one was open for 4% of the time, Pallas kernels for 40%

profile of v4, /device:TPU:0, one launch (start us, length us, event | category | flops | bytes accessed | tf_op | source)
XLA Modules:
  0.0 236.8 jit_solution(6385961965533342525)
XLA Ops:
  0.7 2.3 shard_map.560.w0
  2.9 3.0 %collective-permute-start = (bf16[384,384]{1,0:T(8,128)(2,1)}, bf16[384,384]{1,0:T(8,128)(2,1)S(1)}, u32[]{:S(2)}, u32[]{:S(2)}) collective-permute-start(bf16[384,384]{1,0:T(8,128)(2,1)} %shard_map.560.w0), channel_id=1, source_target_pairs={{0,2},{1,3},{2,0},{3,1},{4,6},{5,7},{6,4},{7,5},{8,10},{9,11},{10,... | collective-permute-start | bytes 884744 | tf_op jit(solution)/shard_map/ppermute | solution.py:927
  5.9 6.6 %shard_map.561 = (bf16[864,384]{1,0:T(8,128)(2,1)}, bf16[768,384]{1,0:T(8,128)(2,1)}, f32[34,8,384]{2,1,0:T(8,128)}) custom-call(f32[31,324]{1,0:T(8,128)} %depth_w.1, f32[2,324]{1,0:T(2,128)} %bn_w.1, f32[384,324]{1,0:T(8,128)} %constant.44.clone.pick, f32[324,2,324]{2,1,0:T(2,128)} %bitcast.69, f32[324,2,324]{2,1,0:T(2,128)} %bitcast.66, ...), custom_call_target="tpu_custom_call" | custom-call | flops 1000 | bytes 1 | tf_op jit(solution)/shard_map/pallas_call | solution.py:914
  17.7 11.5 %shard_map.562 = (bf16[992,324]{1,0:T(8,128)(2,1)}, bf16[2,4,288,496]{3,2,1,0:T(8,128)(2,1)}, bf16[2,4,496,496]{3,2,1,0:T(8,128)(2,1)}, bf16[2,384,496]{2,1,0:T(...) custom-call(s32[1]{0:T(128)} %bitcast.rank_ref, s32[8]{0:T(128)} %len_ref.7, ...), custom_call_target="tpu_custom_call" | custom-call | flops 1000 | bytes 1 | tf_op jit(solution)/shard_map/pallas_call | solution.py:1137
  32.4 16.5 %shard_map.563 = (bf16[4,992,324]{2,1,0:T(8,128)(2,1)}, bf16[4,992,324]{2,1,0:T(8,128)(2,1)}, f32[992,324]{1,0:T(8,128)}, f32[992,1]{1,0:T(8,128)}, f32[992,384]...) custom-call(s32[1]{0:T(128)} %bitcast.rank_ref, s32[8]{0:T(128)} %len_ref.7, ...), custom_call_target="tpu_custom_call" | custom-call | flops 1000 | bytes 1 | tf_op jit(solution)/shard_map/pallas_call | solution.py:914
  50.9 2.2 collective-permute-done.8
  60.9 2.6 %collective-permute-start.12 = (f32[3,384]{1,0:T(4,128)S(1)}, f32[3,384]{1,0:T(4,128)S(1)}, u32[]{:S(2)}, u32[]{:S(2)}) collective-permute-start(f32[3,384]{1,0:T(4,128)S(1)} %pad_maximum_fusion.1), channel_id=1, source_target_pairs={{0,16},{4,20},{8,24},{12,28},{16,0},{20,4},{24,8},{28,12},{1,17},{... | collective-permute-start | bytes 13832 | tf_op jit(solution)/shard_map/ppermute | solution.py:927
  65.4 3.5 %collective-permute-done.13 = f32[3,384]{1,0:T(4,128)S(1)} collective-permute-done((f32[3,384]{1,0:T(4,128)S(1)}, f32[3,384]{1,0:T(4,128)S(1)}, u32[]{:S(2)}, u32[]{:S(2)}) %collective-permute-start.13) | collective-permute-done | bytes 4640 | tf_op jit(solution)/shard_map/ppermute | solution.py:927
  70.6 24.4 %shard_map.564 = (bf16[324,992]{1,0:T(8,128)(2,1)}, f32[992,324]{1,0:T(8,128)}, f32[992,384]{1,0:T(8,128)}, bf16[2,768,384]{2,1,0:T(8,128)(2,1)}, bf16[2,768,384...) custom-call(s32[1]{0:T(128)} %bitcast.rank_ref, s32[8]{0:T(128)} %len_ref.7, ...), custom_call_target="tpu_custom_call" | custom-call | flops 1000 | bytes 1 | tf_op jit(solution)/shard_map/pallas_call | solution.py:914
  104.6 3.6 %collective-permute-start.23 = (f32[2,384]{1,0:T(2,128)S(1)}, f32[2,384]{1,0:T(2,128)S(1)}, u32[]{:S(2)}, u32[]{:S(2)}) collective-permute-start(f32[2,384]{1,0:T(2,128)S(1)} %add.294), channel_id=1, source_target_pairs={{0,24},{4,28},{8,16},{12,20},{16,8},{20,12},{24,0},{28,4},{1,25},{... | collective-permute-start | bytes 9224 | tf_op jit(solution)/shard_map/ppermute | solution.py:927
  111.7 17.0 %shard_map.565 = (f32[992,324]{1,0:T(8,128)}, bf16[4,192,324]{2,1,0:T(8,128)(2,1)}, bf16[48,324]{1,0:T(8,128)(2,1)}) custom-call(s32[1]{0:T(128)} %bitcast.rank_ref, s32[8]{0:T(128)} %len_ref.7, f32[8,324]{1,0:T(8,128)} %norm_w.1, f32[34,8,384]{2,1,0:T(8,128)} %get-tuple-element.132.chan, f32[3,384]{1,0:T(4,128)} %pad_maximum_fusion.2.stat, ...), custom_call_target="tpu_custom_call" | custom-call | flops 14000000000 | bytes 14000000 | tf_op jit(solution)/shard_map/pallas_call | solution.py:914
  130.4 11.2 %shard_map.566 = (bf16[4,992,324]{2,1,0:T(8,128)(2,1)}, bf16[2,928,384]{2,1,0:T(8,128)(2,1)}, bf16[2,928,384]{2,1,0:T(8,128)(2,1)}) custom-call(f32[8,324]{1,0:T(8,128)} %norm_w.1, bf16[4,192,324]{2,1,0:T(8,128)(2,1)} %get-tuple-element.168.cin_grad, bf16[48,324]{1,0:T(8,128)(2,1)} %get-tuple-element.169.vectors, f32[992,324]{1,0:T(8,128)} %get-tuple-element.166.up_in, ...), custom_call_target="tpu_custom_call" | custom-call | flops 12000000000 | bytes 12000000 | tf_op jit(solution)/shard_map/pallas_call | solution.py:914
  141.9 8.5 %shard_map.567 = (f32[992,324]{1,0:T(8,128)}, f32[8,324]{1,0:T(8,128)}) custom-call(f32[8,324]{1,0:T(8,128)} %norm_w.1, f32[992,324]{1,0:T(8,128)} %get-tuple-element.166.up_in, f32[992,324]{1,0:T(8,128)} %get-tuple-element.140.n1_in, f32[992,1]{1,0:T(8,128)} %get-tuple-element.167.s1_in, bf16[864,384]{1,0:T(8,128)(2,1)} %get-tuple-element.135.w0, ...), custom_call_target="tpu_custom_call" | custom-call | flops 8000000000 | bytes 8000000 | tf_op jit(solution)/shard_map/pallas_call | solution.py:914
  152.1 2.1 collective-permute-start.28
  157.4 13.0 %shard_map.568 = (f32[324,992]{1,0:T(8,128)}, bf16[2,384,384]{2,1,0:T(8,128)(2,1)S(1)}, bf16[2,384,384]{2,1,0:T(8,128)(2,1)S(1)}) custom-call(s32[1]{0:T(128)} %bitcast.rank_ref, s32[8]{0:T(128)S(1)} %copy-done.30, bf16[992,324]{1,0:T(8,128)(2,1)S(1)} %copy-done.34, bf16[384,384]{1,0:T(8,128)(2,1)} %shard_map.560.w0, bf16[384,384]{1,0:T(8,128)(2,1)} %copy-done.48, ...), custom_call_target="tpu_custom_call" | custom-call | flops 16000000000 | bytes 16000000 | tf_op jit(solution)/shard_map/pallas_call | solution.py:1255
  173.1 4.6 %collective-permute-done.30 = bf16[192,384]{1,0:T(8,128)(2,1)S(1)} collective-permute-done((bf16[192,384]{1,0:T(8,128)(2,1)S(1)}, bf16[192,384]{1,0:T(8,128)(2,1)S(1)}, u32[]{:S(2)}, u32[]{:S(2)}) %collective-permute-start.30) | collective-permute-done | bytes 147488 | tf_op jit(solution)/shard_map/ppermute | solution.py:927
  180.2 4.0 %collective-permute-done.33 = bf16[192,384]{1,0:T(8,128)(2,1)S(1)} collective-permute-done((bf16[192,384]{1,0:T(8,128)(2,1)S(1)}, bf16[192,384]{1,0:T(8,128)(2,1)S(1)}, u32[]{:S(2)}, u32[]{:S(2)}) %collective-permute-start.33) | collective-permute-done | bytes 147488 | tf_op jit(solution)/shard_map/ppermute | solution.py:927
  197.3 5.5 %collective-permute-done.41 = bf16[192,384]{1,0:T(8,128)(2,1)S(1)} collective-permute-done((bf16[192,384]{1,0:T(8,128)(2,1)S(1)}, bf16[192,384]{1,0:T(8,128)(2,1)S(1)}, u32[]{:S(2)}, u32[]{:S(2)}) %collective-permute-start.41) | collective-permute-done | bytes 147488 | tf_op jit(solution)/shard_map/ppermute | solution.py:927
  203.3 4.1 %shard_map.569 = (f32[324,2,324]{2,1,0:T(2,128)}, f32[324,2,324]{2,1,0:T(2,128)}, f32[324,2,324]{2,1,0:T(2,128)S(1)}, f32[81,324]{1,0:T(8,128)}, f32[81,324]{1,0...) custom-call(s32[1]{0:T(128)} %bitcast.12.spot_ref, ...), custom_call_target="tpu_custom_call" | custom-call | flops 1000000 | bytes 2000000 | tf_op jit(solution)/shard_map/pallas_call | solution.py:898
  210.9 6.1 %collective-permute-done.43 = bf16[192,384]{1,0:T(8,128)(2,1)S(1)} collective-permute-done((bf16[192,384]{1,0:T(8,128)(2,1)S(1)}, bf16[192,384]{1,0:T(8,128)(2,1)S(1)}, u32[]{:S(2)}, u32[]{:S(2)}) %collective-permute-start.43) | collective-permute-done | bytes 147488 | tf_op jit(solution)/shard_map/ppermute | solution.py:927
  217.9 5.7 %shard_map.570 = (f32[324,2,324]{2,1,0:T(2,128)}, f32[324,2,324]{2,1,0:T(2,128)}, f32[324,2,324]{2,1,0:T(2,128)S(1)}, f32[81,2,324]{2,1,0:T(2,128)}, f32[81,2,32...) custom-call(s32[1]{0:T(128)} %bitcast.12.spot_ref, bf16[272,384]{1,0:T(8,128)(2,1)S(1)} %add_convert_fusion.11.mine, ...), custom_call_target="tpu_custom_call" | custom-call | flops 1000000 | bytes 2000000 | tf_op jit(solution)/shard_map/pallas_call | solution.py:898
  223.8 2.6 %shard_map.571 = (f32[81,4,324]{2,1,0:T(4,128)}, f32[3,81,324]{2,1,0:T(8,128)}, f32[81,324]{1,0:T(8,128)}, f32[81,4,324]{2,1,0:T(4,128)S(1)}, f32[31,324]{1,0:T(...) custom-call(s32[1]{0:T(128)} %bitcast.12.spot_ref, ...), custom_call_target="tpu_custom_call" | custom-call | flops 1000000 | bytes 2000000 | tf_op jit(solution)/shard_map/pallas_call | solution.py:898
  228.4 3.0 %collective-permute-done.46 = f32[32,128]{1,0:T(8,128)S(1)} collective-permute-done((f32[32,128]{1,0:T(8,128)S(1)}, f32[32,128]{1,0:T(8,128)S(1)}, u32[]{:S(2)}, u32[]{:S(2)}) %collective-permute-start.46) | collective-permute-done | bytes 16416 | tf_op jit(solution)/shard_map/ppermute | solution.py:927
  231.5 5.1 %shard_map.572 = (f32[324,2,324]{2,1,0:T(2,128)}, f32[324,2,324]{2,1,0:T(2,128)}, f32[81,4,324]{2,1,0:T(4,128)}, f32[81,2,324]{2,1,0:T(2,128)}, f32[81,324]{1,0:...) custom-call(f32[32,128]{1,0:T(8,128)S(1)} %add.343.sums, f32[324,2,324]{2,1,0:T(2,128)S(1)} %bitcast.71, ...), custom_call_target="tpu_custom_call" | custom-call | flops 1000000 | bytes 1000 | tf_op jit(solution)/shard_map/pallas_call | solution.py:914
  (221 shorter events, 64.3 us)
Async XLA Ops:
  2.9 10.2 %collective-permute-start = (bf16[384,384]{1,0:T(8,128)(2,1)}, bf16[384,384]{1,0:T(8,128)(2,1)S(1)}, u32[]{:S(2)}, u32[]{:S(2)}) collective-permute-start(bf16[384,384]{1,0:T(8,128)(2,1)} %shard_map.560.w0), channel_id=1, source_target_pairs={{0,2},{1,3},{2,0},{3,1},{4,6},{5,7},{6,4},{7,5},{8,10},{9,11},{10,... | collective-permute-start | bytes 884744 | tf_op jit(solution)/shard_map/ppermute | solution.py:927
  13.2 16.3 %collective-permute-start.1 = (bf16[864,384]{1,0:T(8,128)(2,1)}, bf16[864,384]{1,0:T(8,128)(2,1)S(1)}, u32[]{:S(2)}, u32[]{:S(2)}) collective-permute-start(bf16[864,384]{1,0:T(8,128)(2,1)} %get-tuple-element.135.w0), channel_id=1, source_target_pairs={{0,2},{1,3},{2,0},{3,1},{4,6},{5,7},{6,4},{7,5},{8,10},{9,11},{10,... | collective-permute-start | bytes 1990664 | tf_op jit(solution)/shard_map/ppermute | solution.py:927
  15.4 15.6 %collective-permute-start.5 = (bf16[864,384]{1,0:T(8,128)(2,1)}, bf16[864,384]{1,0:T(8,128)(2,1)S(1)}, u32[]{:S(2)}, u32[]{:S(2)}) collective-permute-start(bf16[864,384]{1,0:T(8,128)(2,1)} %get-tuple-element.135.w0), channel_id=1, source_target_pairs={{0,1},{1,0},{2,3},{3,2},{4,5},{5,4},{6,7},{7,6},{8,9},{9,8},{10,11... | collective-permute-start | bytes 1990664 | tf_op jit(solution)/shard_map/ppermute | solution.py:927
  29.7 19.2 %collective-permute-start.4 = (bf16[768,384]{1,0:T(8,128)(2,1)S(1)}, bf16[768,384]{1,0:T(8,128)(2,1)S(1)}, u32[]{:S(2)}, u32[]{:S(2)}) collective-permute-start(bf16[768,384]{1,0:T(8,128)(2,1)S(1)} %copy-done.43), channel_id=1, source_target_pairs={{0,2},{1,3},{2,0},{3,1},{4,6},{5,7},{6,4},{7,5},{8,10},{9,11},{10,... | collective-permute-start | bytes 1769480 | tf_op jit(solution)/shard_map/ppermute | solution.py:927
  57.1 12.5 %collective-permute-start.14 = (bf16[768,384]{1,0:T(8,128)(2,1)S(1)}, bf16[768,384]{1,0:T(8,128)(2,1)S(1)}, u32[]{:S(2)}, u32[]{:S(2)}) collective-permute-start(bf16[768,384]{1,0:T(8,128)(2,1)S(1)} %copy-done.43), channel_id=1, source_target_pairs={{0,1},{1,0},{2,3},{3,2},{4,5},{5,4},{6,7},{7,6},{8,9},{9,8},{10,11... | collective-permute-start | bytes 1769480 | tf_op jit(solution)/shard_map/ppermute | solution.py:927
  57.1 12.5 %collective-permute-start.15 = (bf16[768,384]{1,0:T(8,128)(2,1)S(1)}, bf16[768,384]{1,0:T(8,128)(2,1)S(1)}, u32[]{:S(2)}, u32[]{:S(2)}) collective-permute-start(bf16[768,384]{1,0:T(8,128)(2,1)S(1)} %collective-permute-done.4.w2), channel_id=1, source_target_pairs={{0,1},{1,0},{2,3},{3,2},{4,5},{5,4},{6,7},{7,6},{8,9},{9,8},{10,11... | collective-permute-start | bytes 1769480 | tf_op jit(solution)/shard_map/ppermute | solution.py:927
  103.8 7.3 %collective-permute-start.21 = (f32[2,384]{1,0:T(2,128)S(1)}, f32[2,384]{1,0:T(2,128)S(1)}, u32[]{:S(2)}, u32[]{:S(2)}) collective-permute-start(f32[2,384]{1,0:T(2,128)S(1)} %add.294), channel_id=1, source_target_pairs={{0,8},{4,12},{8,0},{12,4},{16,24},{20,28},{24,16},{28,20},{1,9},{5... | collective-permute-start | bytes 9224 | tf_op jit(solution)/shard_map/ppermute | solution.py:927
  103.8 7.3 %collective-permute-start.22 = (f32[2,384]{1,0:T(2,128)S(1)}, f32[2,384]{1,0:T(2,128)S(1)}, u32[]{:S(2)}, u32[]{:S(2)}) collective-permute-start(f32[2,384]{1,0:T(2,128)S(1)} %add.294), channel_id=1, source_target_pairs={{0,16},{4,20},{8,24},{12,28},{16,0},{20,4},{24,8},{28,12},{1,17},{... | collective-permute-start | bytes 9224 | tf_op jit(solution)/shard_map/ppermute | solution.py:927
  109.8 19.0 %collective-permute-start.24 = (bf16[768,384]{1,0:T(8,128)(2,1)S(1)}, bf16[768,384]{1,0:T(8,128)(2,1)S(1)}, u32[]{:S(2)}, u32[]{:S(2)}) collective-permute-start(bf16[768,384]{1,0:T(8,128)(2,1)S(1)} %get-tuple-element.237), channel_id=1, source_target_pairs={{0,2},{1,3},{2,0},{3,1},{4,6},{5,7},{6,4},{7,5},{8,10},{9,11},{10,... | collective-permute-start | bytes 1769480 | tf_op jit(solution)/shard_map/ppermute | solution.py:927
  128.8 12.8 %collective-permute-start.25 = (bf16[384,384]{1,0:T(8,128)(2,1)S(1)}, bf16[384,384]{1,0:T(8,128)(2,1)S(1)}, u32[]{:S(2)}, u32[]{:S(2)}) collective-permute-start(bf16[384,384]{1,0:T(8,128)(2,1)S(1)} %fusion.3), channel_id=1, source_target_pairs={{0,4},{4,0},{8,12},{12,8},{16,20},{20,16},{24,28},{28,24},{1,5},{5... | collective-permute-start | bytes 884744 | tf_op jit(solution)/shard_map/ppermute | solution.py:927
  141.6 12.6 %collective-permute-start.27 = (bf16[2,928,384]{2,1,0:T(8,128)(2,1)}, bf16[2,928,384]{2,1,0:T(8,128)(2,1)S(1)}, u32[]{:S(2)}, u32[]{:S(2)}) collective-permute-start(bf16[2,928,384]{2,1,0:T(8,128)(2,1)} %get-tuple-element.178), channel_id=1, source_target_pairs={{0,1},{1,0},{2,3},{3,2},{4,5},{5,4},{6,7},{7,6},{8,9},{9,8},{10,11... | collective-permute-start | bytes 4276232 | tf_op jit(solution)/shard_map/ppermute | solution.py:927
  141.8 9.5 %collective-permute-start.26 = (bf16[384,384]{1,0:T(8,128)(2,1)S(1)}, bf16[384,384]{1,0:T(8,128)(2,1)S(1)}, u32[]{:S(2)}, u32[]{:S(2)}) collective-permute-start(bf16[384,384]{1,0:T(8,128)(2,1)S(1)} %add_convert_fusion.10), channel_id=1, source_target_pairs={{0,8},{4,12},{8,0},{12,4},{16,24},{20,28},{24,16},{28,20},{1,9},{5... | collective-permute-start | bytes 884744 | tf_op jit(solution)/shard_map/ppermute | solution.py:927
  152.1 21.0 %collective-permute-start.28 = (bf16[384,384]{1,0:T(8,128)(2,1)}, bf16[384,384]{1,0:T(8,128)(2,1)}, u32[]{:S(2)}, u32[]{:S(2)}) collective-permute-start(bf16[384,384]{1,0:T(8,128)(2,1)} %add_convert_fusion.9), channel_id=1, source_target_pairs={{0,16},{4,20},{8,24},{12,28},{16,0},{20,4},{24,8},{28,12},{1,17},{... | collective-permute-start | bytes 884744 | tf_op jit(solution)/shard_map/ppermute | solution.py:927
  154.6 17.9 %collective-permute-start.29 = (bf16[928,384]{1,0:T(8,128)(2,1)S(1)}, bf16[928,384]{1,0:T(8,128)(2,1)S(1)}, u32[]{:S(2)}, u32[]{:S(2)}) collective-permute-start(bf16[928,384]{1,0:T(8,128)(2,1)S(1)} %get-tuple-element.235), channel_id=1, source_target_pairs={{0,2},{1,3},{2,0},{3,1},{4,6},{5,7},{6,4},{7,5},{8,10},{9,11},{10,... | collective-permute-start | bytes 2138120 | tf_op jit(solution)/shard_map/ppermute | solution.py:927
  173.1 15.4 %collective-permute-start.39 = (bf16[2,384,384]{2,1,0:T(8,128)(2,1)S(1)}, bf16[2,384,384]{2,1,0:T(8,128)(2,1)S(1)}, u32[]{:S(2)}, u32[]{:S(2)}) collective-permute-start(bf16[2,384,384]{2,1,0:T(8,128)(2,1)S(1)} %get-tuple-element.191), channel_id=1, source_target_pairs={{0,1},{1,0},{2,3},{3,2},{4,5},{5,4},{6,7},{7,6},{8,9},{9,8},{10,11... | collective-permute-start | bytes 1769480 | tf_op jit(solution)/shard_map/ppermute | solution.py:927
  184.2 7.8 %collective-permute-start.34 = (bf16[192,384]{1,0:T(8,128)(2,1)S(1)}, bf16[192,384]{1,0:T(8,128)(2,1)S(1)}, u32[]{:S(2)}, u32[]{:S(2)}) collective-permute-start(bf16[192,384]{1,0:T(8,128)(2,1)S(1)} %add_convert_fusion.19), channel_id=1, source_target_pairs={{0,16},{4,20},{8,24},{12,28},{16,0},{20,4},{24,8},{28,12},{1,17},{... | collective-permute-start | bytes 442376 | tf_op jit(solution)/shard_map/ppermute | solution.py:927
  186.1 7.4 %collective-permute-start.36 = (bf16[272,384]{1,0:T(8,128)(2,1)S(1)}, bf16[272,384]{1,0:T(8,128)(2,1)S(1)}, u32[]{:S(2)}, u32[]{:S(2)}) collective-permute-start(bf16[272,384]{1,0:T(8,128)(2,1)S(1)} %add_convert_fusion.13), channel_id=1, source_target_pairs={{0,8},{4,12},{8,0},{12,4},{16,24},{20,28},{24,16},{28,20},{1,9},{5... | collective-permute-start | bytes 626696 | tf_op jit(solution)/shard_map/ppermute | solution.py:927
  188.6 6.8 %collective-permute-start.40 = (bf16[384,384]{1,0:T(8,128)(2,1)S(1)}, bf16[384,384]{1,0:T(8,128)(2,1)S(1)}, u32[]{:S(2)}, u32[]{:S(2)}) collective-permute-start(bf16[384,384]{1,0:T(8,128)(2,1)S(1)} %get-tuple-element.239), channel_id=1, source_target_pairs={{0,2},{1,3},{2,0},{3,1},{4,6},{5,7},{6,4},{7,5},{8,10},{9,11},{10,... | collective-permute-start | bytes 884744 | tf_op jit(solution)/shard_map/ppermute | solution.py:927
  191.3 11.9 %collective-permute-start.32 = (bf16[384,384]{1,0:T(8,128)(2,1)S(1)}, bf16[384,384]{1,0:T(8,128)(2,1)S(1)}, u32[]{:S(2)}, u32[]{:S(2)}) collective-permute-start(bf16[384,384]{1,0:T(8,128)(2,1)S(1)} %add_convert_fusion.7.one_mine), channel_id=1, source_target_pairs={{0,4},{4,0},{8,12},{12,8},{16,20},{20,16},{24,28},{28,24},{1,5},{5... | collective-permute-start | bytes 884744 | tf_op jit(solution)/shard_map/ppermute | solution.py:927
  192.0 11.2 %collective-permute-start.35 = (bf16[192,384]{1,0:T(8,128)(2,1)S(1)}, bf16[192,384]{1,0:T(8,128)(2,1)S(1)}, u32[]{:S(2)}, u32[]{:S(2)}) collective-permute-start(bf16[192,384]{1,0:T(8,128)(2,1)S(1)} %add_convert_fusion.18.two_mine), channel_id=1, source_target_pairs={{0,4},{4,0},{8,12},{12,8},{16,20},{20,16},{24,28},{28,24},{1,5},{5... | collective-permute-start | bytes 442376 | tf_op jit(solution)/shard_map/ppermute | solution.py:927
  195.4 7.4 %collective-permute-start.41 = (bf16[192,384]{1,0:T(8,128)(2,1)S(1)}, bf16[192,384]{1,0:T(8,128)(2,1)S(1)}, u32[]{:S(2)}, u32[]{:S(2)}) collective-permute-start(bf16[192,384]{1,0:T(8,128)(2,1)S(1)} %fusion.7), channel_id=1, source_target_pairs={{0,4},{4,0},{8,12},{12,8},{16,20},{20,16},{24,28},{28,24},{1,5},{5... | collective-permute-start | bytes 442376 | tf_op jit(solution)/shard_map/ppermute | solution.py:927
  196.1 12.6 %collective-permute-start.37 = (bf16[272,384]{1,0:T(8,128)(2,1)S(1)}, bf16[272,384]{1,0:T(8,128)(2,1)S(1)}, u32[]{:S(2)}, u32[]{:S(2)}) collective-permute-start(bf16[272,384]{1,0:T(8,128)(2,1)S(1)} %add_convert_fusion.12), channel_id=1, source_target_pairs={{0,16},{4,20},{8,24},{12,28},{16,0},{20,4},{24,8},{28,12},{1,17},{... | collective-permute-start | bytes 626696 | tf_op jit(solution)/shard_map/ppermute | solution.py:927
  209.4 7.7 %collective-permute-start.43 = (bf16[192,384]{1,0:T(8,128)(2,1)S(1)}, bf16[192,384]{1,0:T(8,128)(2,1)S(1)}, u32[]{:S(2)}, u32[]{:S(2)}) collective-permute-start(bf16[192,384]{1,0:T(8,128)(2,1)S(1)} %add_convert_fusion.16), channel_id=1, source_target_pairs={{0,16},{4,20},{8,24},{12,28},{16,0},{20,4},{24,8},{28,12},{1,17},{... | collective-permute-start | bytes 442376 | tf_op jit(solution)/shard_map/ppermute | solution.py:927
  210.4 7.3 %collective-permute-start.38 = (bf16[272,384]{1,0:T(8,128)(2,1)S(1)}, bf16[272,384]{1,0:T(8,128)(2,1)S(1)}, u32[]{:S(2)}, u32[]{:S(2)}) collective-permute-start(bf16[272,384]{1,0:T(8,128)(2,1)S(1)} %add_convert_fusion.11.mine), channel_id=1, source_target_pairs={{0,4},{4,0},{8,12},{12,8},{16,20},{20,16},{24,28},{28,24},{1,5},{5... | collective-permute-start | bytes 626696 | tf_op jit(solution)/shard_map/ppermute | solution.py:927
  (73 other events, 474.0 us)
